TPU v7x, 32 devices: a whole 2x2x4 slice. The times are simulated.
32 devices in a mesh: shot: 4 (over y, x), tx: 4 (over z), ty: 2 (over core).
Axes of the slice: x: 2, y: 2, z: 4, core: 2. Of those that a mesh axis runs over, the one named last changes fastest.
Arguments:
- forward_prev: float32 [4, 128, 16, 256], P('shot', 'tx', 'ty'), may hold values from -6 to 6
- forward_now: float32 [4, 128, 16, 256], P('shot', 'tx', 'ty'), may hold values from -6 to 6
- adjoint_prev: float32 [4, 128, 16, 256], P('shot', 'tx', 'ty'), may hold values from -6 to 6
- adjoint_now: float32 [4, 128, 16, 256], P('shot', 'tx', 'ty'), may hold values from -6 to 6
- velocity_model: bfloat16 [8, 128, 8, 256], P(('tx', 'ty'), 'shot'), may hold values from 1.5 to 4.5
- aperture: int32 [4, 8, 32], P('shot', ('tx', 'ty')), may hold values from 0 to 127, as said below
- source_cell: int32 [4, 2], P('shot'), may hold values from 0 to 127, as said below
- source_strength: float32 [4], P('shot'), may hold values from -60 to 60
- receiver_cell: int32 [4, 128, 2], P('shot'), may hold values from 0 to 127, as said below
- receiver_trace: float32 [4, 128], P('shot'), may hold values from -60 to 60
Outputs:
- forward_next: float32 [4, 128, 16, 256], P('shot', 'tx', 'ty')
- adjoint_next: float32 [4, 128, 16, 256], P('shot', 'tx', 'ty')
- image_slab: float32 [8, 128, 8, 256], P(('tx', 'ty'), 'shot')
Inputs may be any that keep to these rules, and one draw needn't show every extreme that they name: `aperture`: each list of 32 block ids (one shot, one tile position) names every owner, id // 32, at most 8 times, and some owner exactly 8 times. `source_cell`: first entry below 128, second below 16. `receiver_cell`: first entry below 128, second below 16; receivers may share a cell.
All inputs are finite; a program needn't handle non-finite values.
Results may differ from a plain program's by a relative error of at most 0.0004.
Values may be sent and summed in bfloat16 or wider, within the bound.
No kernel may reach another device: no remote copies, remote signals or barrier semaphores. Data moves between devices by JAX's collectives and lax.ppermute only.
A program may use at most 64 MiB of HBM per device.

v0:
```python
import jax
import jax.numpy as jnp
from jax import lax
from jax.sharding import PartitionSpec as P

SURFACE_DEPTH = 8


STENCIL_WEIGHTS = (-205.0 / 72.0, 8.0 / 5.0, -1.0 / 5.0, 8.0 / 315.0, -1.0 / 560.0)
STEP_RATIO = 0.1


def padded_2(cells, sides, width):
    for axis, dim in sides:
        count = lax.axis_size(axis)
        ends = count - 1
        head = lax.slice_in_dim(cells, 0, width, axis=dim)
        tail = lax.slice_in_dim(cells, cells.shape[dim] - width, cells.shape[dim], axis=dim)
        cells = jnp.concatenate(
            [
                lax.ppermute(tail, axis, [(i, (i + 1) % count) for i in range(ends)]),
                cells,
                lax.ppermute(head, axis, [((i + 1) % count, i) for i in range(ends)]),
            ],
            axis=dim,
        )
    return cells


def laplacian(padded):
    extent_x = padded.shape[-3] - 8
    extent_y = padded.shape[-2] - 8
    extent_z = padded.shape[-1] - 8
    centre = padded[..., 4 : 4 + extent_x, 4 : 4 + extent_y, 4 : 4 + extent_z]
    summed = 3.0 * STENCIL_WEIGHTS[0] * centre
    for offset in range(1, 5):
        neighbours = (
            padded[..., 4 + offset : 4 + offset + extent_x, 4 : 4 + extent_y, 4 : 4 + extent_z]
            + padded[..., 4 - offset : 4 - offset + extent_x, 4 : 4 + extent_y, 4 : 4 + extent_z]
            + padded[..., 4 : 4 + extent_x, 4 + offset : 4 + offset + extent_y, 4 : 4 + extent_z]
            + padded[..., 4 : 4 + extent_x, 4 - offset : 4 - offset + extent_y, 4 : 4 + extent_z]
            + padded[..., 4 : 4 + extent_x, 4 : 4 + extent_y, 4 + offset : 4 + offset + extent_z]
            + padded[..., 4 : 4 + extent_x, 4 : 4 + extent_y, 4 - offset : 4 - offset + extent_z]
        )
        summed = summed + STENCIL_WEIGHTS[offset] * neighbours
    return summed


def injections(
    anchor_x, anchor_y, cells_x, cells_y, cells_z, source_xy, strength, receiver_xy, traces
):
    grid_x = lax.iota(jnp.int32, cells_x) + anchor_x
    grid_y = lax.iota(jnp.int32, cells_y) + anchor_y
    depth_mark = (lax.iota(jnp.int32, cells_z) == SURFACE_DEPTH).astype(jnp.float32)
    mark_x = (grid_x == source_xy[0]).astype(jnp.float32)
    mark_y = (grid_y == source_xy[1]).astype(jnp.float32)
    injected = strength * mark_x[:, None, None] * mark_y[None, :, None] * depth_mark[None, None, :]
    receiver_x = (receiver_xy[:, 0][:, None] == grid_x[None, :]).astype(jnp.float32) * traces[
        :, None
    ]
    receiver_y = (receiver_xy[:, 1][:, None] == grid_y[None, :]).astype(jnp.float32)
    surface = jnp.dot(receiver_x.T, receiver_y, precision=lax.Precision.HIGHEST)
    recorded = surface[:, :, None] * depth_mark[None, None, :]
    return (injected, recorded)


def on_device(
    forward_prev,
    forward_now,
    adjoint_prev,
    adjoint_now,
    velocity_model,
    aperture,
    source_cell,
    source_strength,
    receiver_cell,
    receiver_trace,
):
    shot_count = lax.axis_size("shot")
    cells_x = forward_now.shape[1]
    cells_y = forward_now.shape[2]
    cells_z = forward_now.shape[3]
    slab_rows = velocity_model.shape[1]
    capacity = max(2, cells_x // shot_count)
    slot_total = shot_count * capacity
    block_ids = aperture[0, 0]
    owners = block_ids // slab_rows
    local_ids = block_ids % slab_rows
    positions = lax.iota(jnp.int32, cells_x)
    earlier = (owners[:, None] == owners[None, :]) & (positions[None, :] < positions[:, None])
    ranking = jnp.sum(earlier.astype(jnp.int32), axis=1)
    slot_index = owners * capacity + ranking
    placed = slot_index[:, None] == lax.iota(jnp.int32, slot_total)[None, :]
    wanted = jnp.sum(jnp.where(placed, (local_ids + 1)[:, None], 0), axis=0) - 1
    incoming = lax.all_to_all(
        wanted.reshape(shot_count, capacity), "shot", split_axis=0, concat_axis=0, tiled=True
    )
    chosen = incoming.reshape(slot_total)[:, None] == lax.iota(jnp.int32, slab_rows)[None, :]
    blocks = jnp.dot(
        chosen.astype(jnp.bfloat16),
        velocity_model[0].reshape(slab_rows, cells_y * cells_z),
        preferred_element_type=jnp.float32,
    ).astype(jnp.bfloat16)
    arrived = lax.all_to_all(
        blocks.reshape(shot_count, capacity, cells_y * cells_z),
        "shot",
        split_axis=0,
        concat_axis=0,
        tiled=True,
    )
    velocity_tile = jnp.dot(
        placed.astype(jnp.bfloat16),
        arrived.reshape(slot_total, cells_y * cells_z),
        preferred_element_type=jnp.float32,
    )
    scaled = velocity_tile.reshape(cells_x, cells_y, cells_z) * STEP_RATIO
    courant = scaled * scaled
    stacked = jnp.concatenate([forward_now, adjoint_now], axis=0)
    padded = padded_2(stacked, (("tx", 1), ("ty", 2)), 4)
    padded = jnp.pad(padded, ((0, 0), (0, 0), (0, 0), (4, 4)))
    curvature = laplacian(padded)
    anchor_x = lax.axis_index("tx") * cells_x
    anchor_y = lax.axis_index("ty") * cells_y
    injected, recorded = injections(
        anchor_x,
        anchor_y,
        cells_x,
        cells_y,
        cells_z,
        source_cell[0],
        source_strength[0],
        receiver_cell[0],
        receiver_trace[0],
    )
    forward_next = 2.0 * forward_now[0] - forward_prev[0] + courant * (curvature[0] + injected)
    adjoint_next = 2.0 * adjoint_now[0] - adjoint_prev[0] + courant * (curvature[1] + recorded)
    correlation = (forward_next * adjoint_next).reshape(cells_x, cells_y * cells_z)
    row_ids = lax.iota(jnp.int32, slab_rows * lax.axis_size("shot"))
    matches = (row_ids[:, None] == block_ids[None, :]).astype(jnp.float32)
    image_part = lax.psum_scatter(
        jnp.dot(matches, correlation, precision=lax.Precision.HIGHEST),
        "shot",
        scatter_dimension=0,
        tiled=True,
    )
    image_slab = image_part.reshape(1, slab_rows, cells_y, cells_z)
    return (forward_next[None], adjoint_next[None], image_slab)


def solution(mesh):
    in_specs = (
        P("shot", "tx", "ty", None),
        P("shot", "tx", "ty", None),
        P("shot", "tx", "ty", None),
        P("shot", "tx", "ty", None),
        P(("tx", "ty"), "shot", None, None),
        P("shot", ("tx", "ty"), None),
        P("shot", None),
        P("shot"),
        P("shot", None, None),
        P("shot", None),
    )
    out_specs = (
        P("shot", "tx", "ty", None),
        P("shot", "tx", "ty", None),
        P(("tx", "ty"), "shot", None, None),
    )
    return jax.shard_map(
        on_device, mesh=mesh, in_specs=in_specs, out_specs=out_specs, check_vma=False
    )
```

profile of v0, /device:TPU:0, one launch (start us, length us, event | category | flops | bytes accessed | tf_op | source)
XLA Modules:
  0.0 80.2 jit_solution(11397924828815553948)
XLA Ops:
  7.2 1.0 %copy_dynamic-update-slice_fusion.1 = f32[2,32,8,256]{3,1,2,0:T(8,128)S(1)} fusion(f32[1,32,8,256]{3,2,1,0:T(8,128)} %param.11), kind=kLoop, calls=%fused_computation.74 | loop fusion | bytes 524288
  8.2 1.1 %copy_dynamic-update-slice_fusion = f32[2,32,8,256]{3,1,2,0:T(8,128)S(1)} fusion(f32[2,32,8,256]{3,1,2,0:T(8,128)S(1)} %copy_dynamic-update-slice_fusion.1, f32[1,32,8,256]{3,2,1,0:T(8,128)} %param.13), kind=kLoop, calls=%fused_computation.73 | loop fusion | bytes 524288 | tf_op jit(solution)/shard_map/concatenate | solution.py:118
  9.3 1.3 %collective-permute-start = (f32[2,4,8,256]{3,1,2,0:T(4,128)S(1)}, f32[2,4,8,256]{3,1,2,0:T(4,128)S(1)}, u32[]{:S(2)}, u32[]{:S(2)}) collective-permute-start(f32[2,4,8,256]{3,1,2,0:T(4,128)S(1)} %get-tuple-element.22), channel_id=1, source_target_pairs={{2,0},{4,2},{6,4},{3,1},{5,3},{7,5},{10,8},{12,10},{14,12},{11,9},... | collective-permute-start | bytes 196616 | tf_op jit(solution)/shard_map/ppermute | solution.py:23
  10.6 5.6 %collective-permute-start.1 = (f32[2,4,8,256]{3,1,2,0:T(4,128)S(1)}, f32[2,4,8,256]{3,1,2,0:T(4,128)S(1)}, u32[]{:S(2)}, u32[]{:S(2)}) collective-permute-start(f32[2,4,8,256]{3,1,2,0:T(4,128)S(1)} %get-tuple-element.23), channel_id=1, source_target_pairs={{0,2},{2,4},{4,6},{1,3},{3,5},{5,7},{8,10},{10,12},{12,14},{9,11},... | collective-permute-start | bytes 196616 | tf_op jit(solution)/shard_map/ppermute | solution.py:21
  16.2 0.7 and_select_fusion.1
  16.9 0.2 convert_reduce_fusion
  17.0 0.1 select_reduce_fusion
  17.1 0.7 sub.27
  17.8 4.2 %all-to-all-start = ((s32[4,1,8]{2,1,0:T(1,128)}), s32[4,1,8]{2,1,0:T(1,128)S(1)}, u32[]{:S(2)}, u32[]{:S(2)}) async-start(s32[4,1,8]{2,1,0:T(1,128)} %bitcast.3), calls=%async_computation | async-start | bytes 4096 | tf_op jit(solution)/shard_map/all_to_all | solution.py:95
  22.0 1.3 %fusion.64 = (s32[1,1]{1,0:T(1,128)}, s32[1,1]{1,0:T(1,128)}) fusion(s32[1,2]{1,0:T(1,128)} %param.16), kind=kLoop, calls=%fused_computation.118 | loop fusion | bytes 16 | tf_op jit(solution)/shard_map/slice | solution.py:55
  23.9 0.7 compare_convert_fusion.1
  24.6 0.8 slice_bitcast_fusion.3
  25.4 0.9 %fusion.41 = f32[32,8]{0,1:T(8,128)S(1)} fusion(s32[8]{0:T(128)S(1)} %iota_add_fusion, f32[128]{0:T(128)} %bitcast.81, s32[32]{0:T(128)S(1)} %iota_add_fusion.1, s32[128]{0:T(128)S(1)} %get-tuple-element.25, s32[128]{0:T(128)S(1)} %get-tuple-element.24), kind=kOutput, calls=%fused_computation.78 | convolution fusion | flops 402432 | bytes 2720 | tf_op jit(solution)/shard_map/dot_general | solution.py:62
  26.3 0.7 compare_select_fusion
  27.0 0.1 pad_maximum_fusion.1
  27.1 1.3 %collective-permute-start.2 = (f32[2,40,4,256]{3,1,2,0:T(8,128)S(1)}, f32[2,40,4,256]{3,1,2,0:T(8,128)S(1)}, u32[]{:S(2)}, u32[]{:S(2)}) collective-permute-start(f32[2,40,4,256]{3,1,2,0:T(8,128)S(1)} %get-tuple-element.21), channel_id=1, source_target_pairs={{1,0},{3,2},{5,4},{7,6},{9,8},{11,10},{13,12},{15,14},{17,16},{19,... | collective-permute-start | bytes 983048 | tf_op jit(solution)/shard_map/ppermute | solution.py:23
  28.4 3.1 %collective-permute-start.3 = (f32[2,40,4,256]{3,1,2,0:T(8,128)S(1)}, f32[2,40,4,256]{3,1,2,0:T(8,128)S(1)}, u32[]{:S(2)}, u32[]{:S(2)}) collective-permute-start(f32[2,40,4,256]{3,1,2,0:T(8,128)S(1)} %get-tuple-element.20), channel_id=1, source_target_pairs={{0,1},{2,3},{4,5},{6,7},{8,9},{10,11},{12,13},{14,15},{16,17},{18,... | collective-permute-start | bytes 983048 | tf_op jit(solution)/shard_map/ppermute | solution.py:21
  31.6 0.5 broadcast.241
  32.1 0.7 reduce.3
  32.8 0.1 eq.119
  32.9 0.9 %fusion = bf16[4,8,2048]{2,1,0:T(8,128)(2,1)} fusion(bf16[32,2048]{1,0:T(8,128)(2,1)S(1)} %bitcast.75, s32[32]{0:T(128)S(1)} %eq.119), kind=kOutput, calls=%fused_computation.3 | convolution fusion | flops 4260864 | bytes 262272 | tf_op jit(solution)/shard_map/dot_general | solution.py:99
  33.8 4.2 %all-to-all-start.1 = ((bf16[4,8,2048]{2,1,0:T(8,128)(2,1)}), bf16[4,8,2048]{2,1,0:T(8,128)(2,1)S(1)}, u32[]{:S(2)}, u32[]{:S(2)}) async-start(bf16[4,8,2048]{2,1,0:T(8,128)(2,1)} %fusion), calls=%async_computation.1 | async-start | bytes 262144 | tf_op jit(solution)/shard_map/all_to_all | solution.py:104
  38.0 0.2 pad_maximum_fusion
  38.2 0.7 select_maximum_fusion
  38.9 1.6 %fusion.11 = f32[2,32,8,256]{3,1,2,0:T(8,128)S(1)} fusion(f32[2,32,8,256]{3,1,2,0:T(8,128)S(1)} %copy_dynamic-update-slice_fusion, f32[2,4,8,256]{3,1,2,0:T(4,128)S(1)} %collective-permute-done.1, f32[2,4,8,256]{3,1,2,0:T(4,128)S(1)} %collective-permute-done, f32[2,40,16,264]{3,1,2,0:T(8,128)S(1)} %select_maximum_fusion, ...), kind=kLoop, calls=%fused_computation.34 | loop fusion | flops 4849664 | bytes 9568256 | tf_op jit(solution)/shard_map/add | solution.py:45
  40.5 2.5 %all-to-all-done.1 = bf16[4,8,2048]{2,1,0:T(8,128)(2,1)S(1)} async-done(((bf16[4,8,2048]{2,1,0:T(8,128)(2,1)}), bf16[4,8,2048]{2,1,0:T(8,128)(2,1)S(1)}, u32[]{:S(2)}, u32[]{:S(2)}) %all-to-all-start.1) | async-done | bytes 131104 | tf_op jit(solution)/shard_map/all_to_all | solution.py:104
  43.0 0.5 multiply_bitcast_fusion
  43.5 1.5 %fusion.43 = f32[128,2048]{1,0:T(8,128)} fusion(f32[32,2048]{1,0:T(8,128)S(1)} %bitcast.73, s32[32]{0:T(128)S(1)} %bitcast.80), kind=kOutput, calls=%fused_computation.80 | convolution fusion | flops 100667392 | bytes 1310848 | tf_op jit(solution)/shard_map/dot_general | solution.py:141
  45.1 0.9 %copy.51 = f32[1,32,8,256]{3,2,1,0:T(8,128)} copy(f32[1,32,8,256]{3,1,2,0:T(8,128)S(1)} %bitcast.72) | data formatting | bytes 524288
  46.0 0.9 %copy.52 = f32[1,32,8,256]{3,2,1,0:T(8,128)} copy(f32[1,32,8,256]{3,1,2,0:T(8,128)S(1)} %bitcast.71) | data formatting | bytes 524288
  46.8 24.8 %reduce-scatter.2.cloned.1.call-done = f32[32,2048]{1,0:T(8,128)} async-done(((f32[128,2048]{1,0:T(8,128)}), f32[32,2048]{1,0:T(8,128)}) %reduce-scatter.2.cloned.1.call-update) | async-done | bytes 262160 | tf_op jit(solution)/shard_map/reduce_scatter | solution.py:140
  71.7 1.7 %copy.56 = f32[4,8,8,256]{3,2,1,0:T(8,128)} copy(f32[4,8,8,256]{3,1,2,0:T(8,128)} %bitcast.76) | data formatting | bytes 524288
  (29 shorter events, 0.3 us)
Async XLA Ops:
  8.2 23.4 %copy-start.4 = (bf16[1,32,8,256]{3,2,1,0:T(8,128)(2,1)S(1)}, bf16[1,32,8,256]{3,2,1,0:T(8,128)(2,1)}, u32[]{:S(2)}) copy-start(bf16[1,32,8,256]{3,2,1,0:T(8,128)(2,1)} %param.14) | copy-start | bytes 393220
  9.3 17.7 %collective-permute-start = (f32[2,4,8,256]{3,1,2,0:T(4,128)S(1)}, f32[2,4,8,256]{3,1,2,0:T(4,128)S(1)}, u32[]{:S(2)}, u32[]{:S(2)}) collective-permute-start(f32[2,4,8,256]{3,1,2,0:T(4,128)S(1)} %get-tuple-element.22), channel_id=1, source_target_pairs={{2,0},{4,2},{6,4},{3,1},{5,3},{7,5},{10,8},{12,10},{14,12},{11,9},... | collective-permute-start | bytes 196616 | tf_op jit(solution)/shard_map/ppermute | solution.py:23
  10.6 16.4 %collective-permute-start.1 = (f32[2,4,8,256]{3,1,2,0:T(4,128)S(1)}, f32[2,4,8,256]{3,1,2,0:T(4,128)S(1)}, u32[]{:S(2)}, u32[]{:S(2)}) collective-permute-start(f32[2,4,8,256]{3,1,2,0:T(4,128)S(1)} %get-tuple-element.23), channel_id=1, source_target_pairs={{0,2},{2,4},{4,6},{1,3},{3,5},{5,7},{8,10},{10,12},{12,14},{9,11},... | collective-permute-start | bytes 196616 | tf_op jit(solution)/shard_map/ppermute | solution.py:21
  17.8 13.8 %all-to-all-start = ((s32[4,1,8]{2,1,0:T(1,128)}), s32[4,1,8]{2,1,0:T(1,128)S(1)}, u32[]{:S(2)}, u32[]{:S(2)}) async-start(s32[4,1,8]{2,1,0:T(1,128)} %bitcast.3), calls=%async_computation | async-start | bytes 4096 | tf_op jit(solution)/shard_map/all_to_all | solution.py:95
  27.1 10.8 %collective-permute-start.2 = (f32[2,40,4,256]{3,1,2,0:T(8,128)S(1)}, f32[2,40,4,256]{3,1,2,0:T(8,128)S(1)}, u32[]{:S(2)}, u32[]{:S(2)}) collective-permute-start(f32[2,40,4,256]{3,1,2,0:T(8,128)S(1)} %get-tuple-element.21), channel_id=1, source_target_pairs={{1,0},{3,2},{5,4},{7,6},{9,8},{11,10},{13,12},{15,14},{17,16},{19,... | collective-permute-start | bytes 983048 | tf_op jit(solution)/shard_map/ppermute | solution.py:23
  28.4 9.5 %collective-permute-start.3 = (f32[2,40,4,256]{3,1,2,0:T(8,128)S(1)}, f32[2,40,4,256]{3,1,2,0:T(8,128)S(1)}, u32[]{:S(2)}, u32[]{:S(2)}) collective-permute-start(f32[2,40,4,256]{3,1,2,0:T(8,128)S(1)} %get-tuple-element.20), channel_id=1, source_target_pairs={{0,1},{2,3},{4,5},{6,7},{8,9},{10,11},{12,13},{14,15},{16,17},{18,... | collective-permute-start | bytes 983048 | tf_op jit(solution)/shard_map/ppermute | solution.py:21
  33.8 9.2 %all-to-all-start.1 = ((bf16[4,8,2048]{2,1,0:T(8,128)(2,1)}), bf16[4,8,2048]{2,1,0:T(8,128)(2,1)S(1)}, u32[]{:S(2)}, u32[]{:S(2)}) async-start(bf16[4,8,2048]{2,1,0:T(8,128)(2,1)} %fusion), calls=%async_computation.1 | async-start | bytes 262144 | tf_op jit(solution)/shard_map/all_to_all | solution.py:104
  38.0 33.7 %reduce-scatter.2.cloned.1.call-start = ((), (), s32[]{:S(2)}) async-start(), calls=%async_computation.3 | async-start | bytes 1310720 | tf_op jit(solution)/shard_map/reduce_scatter | solution.py:140
  38.9 4.1 %copy-start = (f32[1,32,8,256]{3,2,1,0:T(8,128)S(1)}, f32[1,32,8,256]{3,2,1,0:T(8,128)}, u32[]{:S(2)}) copy-start(f32[1,32,8,256]{3,2,1,0:T(8,128)} %param.11) | copy-start | bytes 786436
  38.9 4.1 %copy-start.1 = (f32[1,32,8,256]{3,2,1,0:T(8,128)S(1)}, f32[1,32,8,256]{3,2,1,0:T(8,128)}, u32[]{:S(2)}) copy-start(f32[1,32,8,256]{3,2,1,0:T(8,128)} %param.13) | copy-start | bytes 786436
  38.9 4.1 %copy-start.2 = (f32[1,32,8,256]{3,2,1,0:T(8,128)S(1)}, f32[1,32,8,256]{3,2,1,0:T(8,128)}, u32[]{:S(2)}) copy-start(f32[1,32,8,256]{3,2,1,0:T(8,128)} %param.12) | copy-start | bytes 786436
  38.9 4.1 %copy-start.3 = (f32[1,32,8,256]{3,2,1,0:T(8,128)S(1)}, f32[1,32,8,256]{3,2,1,0:T(8,128)}, u32[]{:S(2)}) copy-start(f32[1,32,8,256]{3,2,1,0:T(8,128)} %param.10) | copy-start | bytes 786436
  40.5 3.0 %copy-start.5 = (s32[1,1,32]{2,1,0:T(1,128)S(1)}, s32[1,1,32]{2,1,0:T(1,128)}, u32[]{:S(2)}) copy-start(s32[1,1,32]{2,1,0:T(1,128)} %param.15) | copy-start | bytes 388
Sparse Core Ops, SparseCore 0:
  45.2 26.3 reduce-scatter.1
where the time goes:
time: 80.8 us; the launch traced here: 80.2 us
  waiting for transfers between devices  27.4 us (34%)
  starting transfers between devices  19.6 us (24%)
  between operations  14.9 us (18%)
  local copies, waits for them, and re-layouts  9.04 us (11%)
  other arithmetic  5.53 us (7%)
  matrix products  3.84 us (5%)
    reduce_scatter x1, waiting for transfers between devices, on_device(): lax.psum_scatter(jnp.dot(matches, correlation, precision=lax.Precision.HI...  24.8 us
    ppermute x2, starting transfers between devices, padded_2(): lax.ppermute(tail, axis, [(i, (i + 1) % count) for i in range(ends)])  8.63 us
    unnamed x17, local copies, waits for them, and re-layouts  4.55 us
    all_to_all x1, starting transfers between devices, on_device(): lax.all_to_all(blocks.reshape(shot_count, capacity, cells_y * cells_z), '...  4.19 us
    all_to_all x1, starting transfers between devices, on_device(): lax.all_to_all(wanted.reshape(shot_count, capacity), 'shot', split_axis=0...  4.15 us
    ppermute x2, starting transfers between devices, padded_2(): lax.ppermute(head, axis, [((i + 1) % count, i) for i in range(ends)])  2.58 us
    all_to_all x1, waiting for transfers between devices, on_device(): lax.all_to_all(blocks.reshape(shot_count, capacity, cells_y * cells_z), '...  2.48 us
  transfers between devices with their start and end apart: 7, of which 2 were waited for; matrix products, arithmetic and copies ran while one was open for 16% of the time, Pallas kernels for 0%

commit v1 on v0

v1 whole, which is shorter than its diff:
```python
import functools

import jax
import jax.numpy as jnp
from jax import lax
from jax.experimental import pallas as pl
from jax.experimental.pallas import tpu as pltpu
from jax.sharding import PartitionSpec as P

SURFACE_DEPTH = 8


STENCIL_WEIGHTS = (-205.0 / 72.0, 8.0 / 5.0, -1.0 / 5.0, 8.0 / 315.0, -1.0 / 560.0)
STEP_RATIO = 0.1
REACH = 4

VMEM = pl.BlockSpec(memory_space=pltpu.VMEM)
SMEM = pl.BlockSpec(memory_space=pltpu.SMEM)


def swaps(count):
    even = [(i, i + 1) for i in range(0, count - 1, 2)]
    odd = [(i, i + 1) for i in range(1, count - 1, 2)]
    return [[pair for a, b in pairs for pair in ((a, b), (b, a))] for pairs in (even, odd)]


def pack_kernel(where_ref, f_ref, a_ref, x_even_ref, x_odd_ref, y_even_ref, y_odd_ref=None):
    cells_x, cells_y, _ = f_ref.shape
    half = cells_x // 2
    x_at_even = where_ref[0] % 2 == 0
    y_at_even = where_ref[1] % 2 == 0
    tail, head = cells_x - REACH, 0
    start_even = jnp.where(x_at_even, tail, head)
    start_odd = jnp.where(x_at_even, head, tail)
    for field, ref in enumerate((f_ref, a_ref)):
        x_even_ref[field] = ref[pl.ds(start_even, REACH)]
        x_odd_ref[field] = ref[pl.ds(start_odd, REACH)]
        cells = ref[...]
        turned = jnp.roll(cells, REACH, axis=1)
        low = lax.broadcasted_iota(jnp.int32, (half,) + cells.shape[1:], 1) < REACH
        heads = jnp.where(low, cells[:half], turned[half:])
        tails = jnp.where(low, turned[:half], cells[half:])
        y_even_ref[field] = jnp.where(y_at_even, tails, heads)
        if y_odd_ref is not None:
            y_odd_ref[field] = jnp.where(y_at_even, heads, tails)


def stencil_kernel(count_y, where_ref, source_ref, strength_ref, cell_ref, trace_ref, f_ref, a_ref, *refs):
    if count_y > 2:
        x_even_ref, x_odd_ref, y_even_ref, y_odd_ref, out_ref, pad_ref, edge_ref = refs
    else:
        x_even_ref, x_odd_ref, y_even_ref, out_ref, pad_ref, edge_ref = refs
        y_odd_ref = None
    cells_x, cells_y, cells_z = f_ref.shape
    half = cells_x // 2
    x_at_even = where_ref[0] % 2 == 0
    y_at_even = where_ref[1] % 2 == 0
    row = lax.broadcasted_iota(jnp.int32, (cells_z, cells_z), 0)
    col = lax.broadcasted_iota(jnp.int32, (cells_z, cells_z), 1)
    gap = jnp.abs(row - col)
    band = jnp.zeros((cells_z, cells_z), jnp.float32)
    for offset in range(1, REACH + 1):
        band = jnp.where(gap == offset, STENCIL_WEIGHTS[offset], band)
    sub = lax.broadcasted_iota(jnp.int32, (cells_y, cells_z), 0)
    lane = lax.broadcasted_iota(jnp.int32, (cells_y, cells_z), 1)
    low = lax.broadcasted_iota(jnp.int32, (half, cells_y, cells_z), 1) < REACH

    cells = lax.broadcasted_iota(jnp.int32, (cells_x, cells_y, cell_ref.shape[1]), 0) * cells_y
    cells = cells + lax.broadcasted_iota(jnp.int32, cells.shape, 1)
    hit = jnp.where(cells == cell_ref[...][None], trace_ref[...][None], 0.0)
    surface = jnp.sum(hit, axis=2, keepdims=True)

    for field, ref in enumerate((f_ref, a_ref)):
        even, odd = x_even_ref[field], x_odd_ref[field]
        pad_ref[:REACH] = jnp.where(x_at_even, odd, even)
        pad_ref[REACH + cells_x :] = jnp.where(x_at_even, even, odd)
        cells = ref[...]
        pad_ref[REACH : REACH + cells_x] = cells
        even = y_even_ref[field]
        turned = jnp.roll(even, REACH, axis=1)
        if y_odd_ref is not None:
            odd = y_odd_ref[field]
            turned_odd = jnp.roll(odd, REACH, axis=1)
        else:
            odd = turned_odd = jnp.zeros_like(even)
        after_first = jnp.where(y_at_even, even, odd)
        after_second = jnp.where(y_at_even, turned, turned_odd)
        before_first = jnp.where(y_at_even, turned_odd, turned)
        before_second = jnp.where(y_at_even, odd, even)
        edge_ref[:half] = jnp.where(low, after_first, before_first)
        edge_ref[half:] = jnp.where(low, after_second, before_second)
        along_z = jnp.dot(
            cells.reshape(cells_x * cells_y, cells_z),
            band,
            precision=lax.Precision.HIGHEST,
            preferred_element_type=jnp.float32,
        )
        out_ref[field] = along_z.reshape(cells_x, cells_y, cells_z)

        def one_row(x, _, field=field):
            centre = pad_ref[x + REACH]
            edge = edge_ref[x]
            total = out_ref[field, x] + (3.0 * STENCIL_WEIGHTS[0]) * centre
            for offset in range(1, REACH + 1):
                after = jnp.roll(jnp.where(sub >= offset, centre, edge), -offset, axis=0)
                before = jnp.roll(jnp.where(sub < cells_y - offset, centre, edge), offset, axis=0)
                pairs = (pad_ref[x + REACH + offset] + pad_ref[x + REACH - offset]) + (after + before)
                total = total + STENCIL_WEIGHTS[offset] * pairs
            out_ref[field, x] = total
            return 0

        lax.fori_loop(0, cells_x, one_row, 0, unroll=4)
    depth = lax.broadcasted_iota(jnp.int32, (cells_x, cells_y, cells_z), 2) == SURFACE_DEPTH
    out_ref[1] = out_ref[1] + jnp.where(depth, surface, 0.0)
    source_x = source_ref[0] - where_ref[0] * cells_x
    source_y = source_ref[1] - where_ref[1] * cells_y

    @pl.when((source_x >= 0) & (source_x < cells_x))
    def _():
        mark = (sub == source_y) & (lane == SURFACE_DEPTH)
        out_ref[0, source_x] = out_ref[0, source_x] + jnp.where(mark, strength_ref[0], 0.0)


def rank_rows(ids_ref, rows_ref, taken_ref, owners, slab, capacity):
    for owner in range(owners):
        taken_ref[owner] = 0

    def one_row(r, _):
        owner = ids_ref[r] // slab
        slot = taken_ref[owner]
        rows_ref[owner * capacity + slot] = r
        taken_ref[owner] = slot + 1
        return 0

    lax.fori_loop(0, ids_ref.shape[0], one_row, 0, unroll=4)


def next_fields(r, block, v_ref, fields, curve_ref):
    f_prev_ref, f_now_ref, a_prev_ref, a_now_ref = fields
    scaled = v_ref[block] * STEP_RATIO
    courant = scaled * scaled
    f_next = 2.0 * f_now_ref[r] - f_prev_ref[r] + courant * curve_ref[0, r]
    a_next = 2.0 * a_now_ref[r] - a_prev_ref[r] + courant * curve_ref[1, r]
    return f_next, a_next


def send_kernel(owners, where_ref, ids_ref, *refs):
    fields, refs = refs[:4], refs[4:]
    curve_ref, refs = refs[0], refs[1:]
    slabs, refs = refs[: owners - 1], refs[owners - 1 :]
    outs, refs = refs[: owners - 1], refs[owners - 1 :]
    v_ref, rows_ref, taken_ref = refs
    slab = slabs[0].shape[0]
    capacity = outs[0].shape[0]
    rank_rows(ids_ref, rows_ref, taken_ref, owners, slab, capacity)
    me = where_ref[2]
    for k in range(1, owners):
        v_ref[...] = slabs[k - 1][...].astype(jnp.float32)
        for j in range(capacity):
            r = rows_ref[(me ^ k) * capacity + j]
            f_next, a_next = next_fields(r, ids_ref[r] % slab, v_ref, fields, curve_ref)
            outs[k - 1][j] = f_next * a_next


def output_kernel(owners, capacity, where_ref, *refs):
    lists, refs = refs[:owners], refs[owners:]
    fields, refs = refs[:4], refs[4:]
    curve_ref, refs = refs[0], refs[1:]
    slabs, refs = refs[:owners], refs[owners:]
    f_out_ref, a_out_ref, image_ref, places_ref, v_ref, rows_ref, taken_ref = refs
    ids_ref = lists[0]
    slab = slabs[0].shape[0]
    rank_rows(ids_ref, rows_ref, taken_ref, owners, slab, capacity)
    me = where_ref[2]
    image_ref[...] = jnp.zeros_like(image_ref)
    for k in range(owners):
        v_ref[...] = slabs[k][...].astype(jnp.float32)
        for j in range(capacity):
            r = rows_ref[(me ^ k) * capacity + j]
            block = ids_ref[r] % slab
            f_next, a_next = next_fields(r, block, v_ref, fields, curve_ref)
            f_out_ref[r] = f_next
            a_out_ref[r] = a_next
            if k == 0:
                image_ref[block] = image_ref[block] + f_next * a_next
    for k in range(1, owners):

        def one_row(r, slot, k=k):
            block = lists[k][r] - me * slab
            mine = (block >= 0) & (block < slab)

            @pl.when(mine)
            def _():
                places_ref[(k - 1) * capacity + slot] = block

            return slot + mine.astype(jnp.int32)

        lax.fori_loop(0, ids_ref.shape[0], one_row, 0)


def image_kernel(places_ref, own_ref, *refs):
    rows, out_ref = refs[:-1], refs[-1]
    capacity = rows[0].shape[0]
    out_ref[...] = own_ref[...]
    for k, ref in enumerate(rows):
        for j in range(capacity):
            block = places_ref[k * capacity + j]
            out_ref[block] = out_ref[block] + ref[j]


def on_device(
    forward_prev,
    forward_now,
    adjoint_prev,
    adjoint_now,
    velocity_model,
    aperture,
    source_cell,
    source_strength,
    receiver_cell,
    receiver_trace,
):
    owners = lax.axis_size("shot")
    count_x, count_y = lax.axis_size("tx"), lax.axis_size("ty")
    cells_x, cells_y, cells_z = forward_now.shape[1:]
    slab = velocity_model.shape[1]
    capacity = cells_x // owners
    fields = (forward_prev[0], forward_now[0], adjoint_prev[0], adjoint_now[0])
    at = [lax.axis_index("tx"), lax.axis_index("ty"), lax.axis_index("shot")]
    where = jnp.stack(at).astype(jnp.int32)
    ids = aperture[0, 0]

    def peer(value, k):
        return lax.ppermute(value, "shot", [(i, i ^ k) for i in range(owners)])

    slabs = [velocity_model[0]] + [peer(velocity_model[0], k) for k in range(1, owners)]
    lists = [ids] + [peer(ids, k) for k in range(1, owners)]

    f32 = jnp.float32
    x_face = jax.ShapeDtypeStruct((2, REACH, cells_y, cells_z), f32)
    y_face = jax.ShapeDtypeStruct((2, cells_x // 2, cells_y, cells_z), f32)
    faces = pl.pallas_call(
        pack_kernel,
        out_shape=(x_face, x_face, y_face) + ((y_face,) if count_y > 2 else ()),
        in_specs=[SMEM, VMEM, VMEM],
        out_specs=(VMEM,) * (4 if count_y > 2 else 3),
        name="pack_faces",
    )(where, fields[1], fields[3])
    x_even, x_odd = swaps(count_x)
    y_even, y_odd = swaps(count_y)
    halos = [lax.ppermute(faces[0], "tx", x_even), lax.ppermute(faces[1], "tx", x_odd)]
    halos.append(lax.ppermute(faces[2], "ty", y_even))
    if count_y > 2:
        halos.append(lax.ppermute(faces[3], "ty", y_odd))

    near_x = receiver_cell[0, :, 0] - at[0] * cells_x
    near_y = receiver_cell[0, :, 1] - at[1] * cells_y
    inside = (near_x >= 0) & (near_x < cells_x) & (near_y >= 0) & (near_y < cells_y)
    cell = jnp.where(inside, near_x * cells_y + near_y, -1)[None]

    curve = pl.pallas_call(
        functools.partial(stencil_kernel, count_y),
        out_shape=jax.ShapeDtypeStruct((2, cells_x, cells_y, cells_z), f32),
        in_specs=[SMEM, SMEM, SMEM, VMEM, VMEM, VMEM, VMEM] + [VMEM] * len(halos),
        out_specs=VMEM,
        scratch_shapes=[
            pltpu.VMEM((cells_x + 2 * REACH, cells_y, cells_z), f32),
            pltpu.VMEM((cells_x, cells_y, cells_z), f32),
        ],
        name="stencil",
    )(where, source_cell[0], source_strength, cell, receiver_trace, fields[1], fields[3], *halos)

    scratch = [
        pltpu.VMEM((slab, cells_y, cells_z), f32),
        pltpu.SMEM((cells_x,), jnp.int32),
        pltpu.SMEM((owners,), jnp.int32),
    ]
    row_block = jax.ShapeDtypeStruct((capacity, cells_y, cells_z), f32)
    to_send = pl.pallas_call(
        functools.partial(send_kernel, owners),
        out_shape=(row_block,) * (owners - 1),
        in_specs=[SMEM, SMEM] + [VMEM] * (5 + owners - 1),
        out_specs=(VMEM,) * (owners - 1),
        scratch_shapes=scratch,
        name="rows_to_send",
    )(where, ids, *fields, curve, *slabs[1:])
    arrived = [peer(rows, k) for k, rows in enumerate(to_send, 1)]

    field = jax.ShapeDtypeStruct((cells_x, cells_y, cells_z), f32)
    own = jax.ShapeDtypeStruct((slab, cells_y, cells_z), f32)
    table = jax.ShapeDtypeStruct(((owners - 1) * capacity,), jnp.int32)
    forward_next, adjoint_next, own_image, places = pl.pallas_call(
        functools.partial(output_kernel, owners, capacity),
        out_shape=(field, field, own, table),
        in_specs=[SMEM] * (1 + owners) + [VMEM] * (5 + owners),
        out_specs=(VMEM, VMEM, VMEM, SMEM),
        scratch_shapes=scratch,
        name="next_fields",
        cost_estimate=pl.CostEstimate(flops=2000000, bytes_accessed=3000000, transcendentals=0),
    )(where, *lists, *fields, curve, *slabs)

    image = pl.pallas_call(
        image_kernel,
        out_shape=own,
        in_specs=[SMEM] + [VMEM] * owners,
        out_specs=VMEM,
        name="image_rows",
    )(places, own_image, *arrived)
    return forward_next[None], adjoint_next[None], image[None]


def solution(mesh):
    in_specs = (
        P("shot", "tx", "ty", None),
        P("shot", "tx", "ty", None),
        P("shot", "tx", "ty", None),
        P("shot", "tx", "ty", None),
        P(("tx", "ty"), "shot", None, None),
        P("shot", ("tx", "ty"), None),
        P("shot", None),
        P("shot"),
        P("shot", None, None),
        P("shot", None),
    )
    out_specs = (
        P("shot", "tx", "ty", None),
        P("shot", "tx", "ty", None),
        P(("tx", "ty"), "shot", None, None),
    )
    return jax.shard_map(
        on_device, mesh=mesh, in_specs=in_specs, out_specs=out_specs, check_vma=False
    )
```

time: 80.8 us -> 41.5 us (0.51)
  the two profiles are of different devices: /device:TPU:0 before, /device:TPU:16 now
where the time goes in v1:
time: 41.5 us; the launch traced here: 41.2 us
  starting transfers between devices  15.7 us (38%)
  Pallas kernels  13.8 us (33%)
  waiting for transfers between devices  6.55 us (16%)
  local copies, waits for them, and re-layouts  2.65 us (6%)
  between operations  1.42 us (3%)
  other arithmetic  1.17 us (3%)
    ppermute x9, starting transfers between devices, peer(): return lax.ppermute(value, 'shot', [(i, i ^ k) for i in range(owners)])  12.1 us
    pallas_call x1, Pallas kernels, on_device(): pl.pallas_call(functools.partial(stencil_kernel, count_y), out_shape=jax....  3.96 us
    pallas_call x1, Pallas kernels, on_device(): pl.pallas_call(functools.partial(output_kernel, owners, capacity), out_sh...  3.67 us
    ppermute x9, waiting for transfers between devices, peer(): return lax.ppermute(value, 'shot', [(i, i ^ k) for i in range(owners)])  3.28 us
    ppermute x1, waiting for transfers between devices, on_device(): lax.ppermute(faces[1], 'tx', x_odd)  3.26 us
    unnamed x30, local copies, waits for them, and re-layouts  2.65 us
    pallas_call x1, Pallas kernels, on_device(): pl.pallas_call(functools.partial(send_kernel, owners), out_shape=(row_blo...  2.53 us
    ppermute x1, starting transfers between devices, on_device(): lax.ppermute(faces[1], 'tx', x_odd)  2.04 us
  transfers between devices with their start and end apart: 12, of which 3 were waited for; matrix products, arithmetic and copies ran while one was open for 1% of the time, Pallas kernels for 19%

profile of v1, /device:TPU:16, one launch (start us, length us, event | category | flops | bytes accessed | tf_op | source)
XLA Modules:
  0.0 41.2 jit_solution(11019516181412431319)
XLA Ops:
  0.6 0.7 %pad_add_fusion.where_ref = s32[3]{0:T(128)} fusion(s32[1]{0:T(128)} %bitcast.2, s32[1]{0:T(128)} %bitcast.1, s32[1]{0:T(128)} %bitcast), kind=kLoop, calls=%fused_computation.1 | loop fusion | flops 6 | bytes 24 | tf_op jit(solution)/shard_map/stack | solution.py:230
  1.3 1.8 %pack_faces.1 = (f32[2,4,8,256]{3,2,1,0:T(8,128)}, f32[2,4,8,256]{3,2,1,0:T(8,128)}, f32[2,16,8,256]{3,2,1,0:T(8,128)}) custom-call(s32[3]{0:T(128)} %pad_add_fusion.where_ref, f32[32,8,256]{2,1,0:T(8,128)} %bitcast.15, f32[32,8,256]{2,1,0:T(8,128)} %bitcast.19), custom_call_target="tpu_custom_call" | custom-call | tf_op jit(solution)/shard_map/pack_faces/pallas_call | solution.py:242
  3.1 1.6 %collective-permute-start.3 = (f32[2,4,8,256]{3,2,1,0:T(8,128)}, f32[2,4,8,256]{3,2,1,0:T(8,128)S(1)}, u32[]{:S(2)}, u32[]{:S(2)}) collective-permute-start(f32[2,4,8,256]{3,2,1,0:T(8,128)} %get-tuple-element.13), channel_id=1, source_target_pairs={{0,2},{2,0},{4,6},{6,4},{1,3},{3,1},{5,7},{7,5},{8,10},{10,8},{12,... | collective-permute-start | bytes 196616 | tf_op jit(solution)/shard_map/ppermute | solution.py:251
  4.7 1.5 %collective-permute-start.6 = (bf16[32,8,256]{2,1,0:T(8,128)(2,1)S(1)}, bf16[32,8,256]{2,1,0:T(8,128)(2,1)S(1)}, u32[]{:S(2)}, u32[]{:S(2)}) collective-permute-start(bf16[32,8,256]{2,1,0:T(8,128)(2,1)S(1)} %bitcast.29), channel_id=1, source_target_pairs={{0,8},{8,0},{16,24},{24,16},{1,9},{9,1},{17,25},{25,17},{2,10},{10... | collective-permute-start | bytes 393224 | tf_op jit(solution)/shard_map/ppermute | solution.py:234
  6.2 1.5 %collective-permute-start.7 = (bf16[32,8,256]{2,1,0:T(8,128)(2,1)S(1)}, bf16[32,8,256]{2,1,0:T(8,128)(2,1)S(1)}, u32[]{:S(2)}, u32[]{:S(2)}) collective-permute-start(bf16[32,8,256]{2,1,0:T(8,128)(2,1)S(1)} %bitcast.30), channel_id=1, source_target_pairs={{0,16},{8,24},{16,0},{24,8},{1,17},{9,25},{17,1},{25,9},{2,18},{10... | collective-permute-start | bytes 393224 | tf_op jit(solution)/shard_map/ppermute | solution.py:234
  7.7 0.5 %collective-permute-start.8 = (bf16[32,8,256]{2,1,0:T(8,128)(2,1)S(1)}, bf16[32,8,256]{2,1,0:T(8,128)(2,1)S(1)}, u32[]{:S(2)}, u32[]{:S(2)}) collective-permute-start(bf16[32,8,256]{2,1,0:T(8,128)(2,1)S(1)} %bitcast.31), channel_id=1, source_target_pairs={{0,24},{8,16},{16,8},{24,0},{1,25},{9,17},{17,9},{25,1},{2,26},{10... | collective-permute-start | bytes 393224 | tf_op jit(solution)/shard_map/ppermute | solution.py:234
  8.2 2.0 %collective-permute-start.4 = (f32[2,4,8,256]{3,2,1,0:T(8,128)}, f32[2,4,8,256]{3,2,1,0:T(8,128)S(1)}, u32[]{:S(2)}, u32[]{:S(2)}) collective-permute-start(f32[2,4,8,256]{3,2,1,0:T(8,128)} %get-tuple-element.14), channel_id=1, source_target_pairs={{2,4},{4,2},{3,5},{5,3},{10,12},{12,10},{11,13},{13,11},{18,20},{2... | collective-permute-start | bytes 196616 | tf_op jit(solution)/shard_map/ppermute | solution.py:251
  10.3 0.5 %fusion.cell_ref = s32[1,128]{1,0:T(1,128)} fusion(s32[1,128,2]{1,2,0:T(2,128)S(1)} %copy-done.11, s32[]{:T(128)S(6)} %mul.18, s32[]{:T(128)S(6)} %mul.17), kind=kLoop, calls=%fused_computation.2 | loop fusion | flops 1536 | bytes 1544 | tf_op jit(solution)/shard_map/jit(_where)/select_n | solution.py:259
  11.4 3.3 %collective-permute-done.4.refs_1_ = f32[2,4,8,256]{3,2,1,0:T(8,128)S(1)} collective-permute-done((f32[2,4,8,256]{3,2,1,0:T(8,128)}, f32[2,4,8,256]{3,2,1,0:T(8,128)S(1)}, u32[]{:S(2)}, u32[]{:S(2)}) %collective-permute-start.4) | collective-permute-done | bytes 65568 | tf_op jit(solution)/shard_map/ppermute | solution.py:251
  14.7 0.0 collective-permute-done.5.refs_2_
  14.7 0.6 %copy-done.9 = f32[2,4,8,256]{3,2,1,0:T(8,128)} copy-done((f32[2,4,8,256]{3,2,1,0:T(8,128)}, f32[2,4,8,256]{3,2,1,0:T(8,128)S(1)}, u32[]{:S(2)}) %copy-start.9) | copy-done | bytes 65560
  15.3 0.1 copy-done.3
  15.4 4.0 %stencil.1.refs_8_.refs_4_ = f32[2,32,8,256]{3,2,1,0:T(8,128)} custom-call(s32[3]{0:T(128)} %pad_add_fusion.where_ref, s32[2]{0:T(128)} %bitcast.37, f32[1]{0:T(128)S(6)} %copy.13.strength_ref, s32[1,128]{1,0:T(1,128)} %fusion.cell_ref, f32[1,128]{1,0:T(1,128)} %trace_ref.1, f32[32,8,256]{2,1,0:T(8,128)} %bitcast.16, f32[32,8,256]{2,1,0:T(8,128)} %bitcast.20, ...), custom_call_target="tpu_custom_call" | custom-call | tf_op jit(solution)/shard_map/stencil/pallas_call | solution.py:261
  19.4 0.0 collective-permute-done.6.refs_10_.refs_5_
  19.4 0.6 %copy-done = bf16[32,8,256]{2,1,0:T(8,128)(2,1)} copy-done((bf16[32,8,256]{2,1,0:T(8,128)(2,1)}, bf16[32,8,256]{2,1,0:T(8,128)(2,1)S(1)}, u32[]{:S(2)}) %copy-start) | copy-done | bytes 131096
  20.0 0.0 copy-done.1
  20.1 0.0 copy-done.2
  20.1 2.5 %rows_to_send.1 = (f32[8,8,256]{2,1,0:T(8,128)}, f32[8,8,256]{2,1,0:T(8,128)}, f32[8,8,256]{2,1,0:T(8,128)}) custom-call(s32[3]{0:T(128)} %pad_add_fusion.where_ref, s32[32]{0:T(128)} %bitcast.32, f32[32,8,256]{2,1,0:T(8,128)} %bitcast.23, f32[32,8,256]{2,1,0:T(8,128)} %bitcast.17, f32[32,8,256]{2,1,0:T(8,128)} %bitcast.25, f32[32,8,256]{2,1,0:T(8,128)} %bitcast.21, ...), custom_call_target="tpu_custom_call" | custom-call | tf_op jit(solution)/shard_map/rows_to_send/pallas_call | solution.py:279
  22.7 1.5 %collective-permute-start.9 = (f32[8,8,256]{2,1,0:T(8,128)}, f32[8,8,256]{2,1,0:T(8,128)S(1)}, u32[]{:S(2)}, u32[]{:S(2)}) collective-permute-start(f32[8,8,256]{2,1,0:T(8,128)} %get-tuple-element.20), channel_id=1, source_target_pairs={{0,8},{8,0},{16,24},{24,16},{1,9},{9,1},{17,25},{25,17},{2,10},{10... | collective-permute-start | bytes 196616 | tf_op jit(solution)/shard_map/ppermute | solution.py:234
  24.2 1.5 %collective-permute-start.10 = (f32[8,8,256]{2,1,0:T(8,128)}, f32[8,8,256]{2,1,0:T(8,128)S(1)}, u32[]{:S(2)}, u32[]{:S(2)}) collective-permute-start(f32[8,8,256]{2,1,0:T(8,128)} %get-tuple-element.21), channel_id=1, source_target_pairs={{0,16},{8,24},{16,0},{24,8},{1,17},{9,25},{17,1},{25,9},{2,18},{10... | collective-permute-start | bytes 196616 | tf_op jit(solution)/shard_map/ppermute | solution.py:234
  25.7 0.5 %collective-permute-start.11 = (f32[8,8,256]{2,1,0:T(8,128)}, f32[8,8,256]{2,1,0:T(8,128)S(1)}, u32[]{:S(2)}, u32[]{:S(2)}) collective-permute-start(f32[8,8,256]{2,1,0:T(8,128)} %get-tuple-element.22), channel_id=1, source_target_pairs={{0,24},{8,16},{16,8},{24,0},{1,25},{9,17},{17,9},{25,1},{2,26},{10... | collective-permute-start | bytes 196616 | tf_op jit(solution)/shard_map/ppermute | solution.py:234
  26.2 1.5 %collective-permute-start = (s32[32]{0:T(128)S(1)}, s32[32]{0:T(128)S(1)}, u32[]{:S(2)}, u32[]{:S(2)}) collective-permute-start(s32[32]{0:T(128)S(1)} %bitcast.34), channel_id=1, source_target_pairs={{0,8},{8,0},{16,24},{24,16},{1,9},{9,1},{17,25},{25,17},{2,10},{10... | collective-permute-start | bytes 392 | tf_op jit(solution)/shard_map/ppermute | solution.py:234
  27.6 1.5 %collective-permute-start.1 = (s32[32]{0:T(128)S(1)}, s32[32]{0:T(128)S(1)}, u32[]{:S(2)}, u32[]{:S(2)}) collective-permute-start(s32[32]{0:T(128)S(1)} %bitcast.35), channel_id=1, source_target_pairs={{0,16},{8,24},{16,0},{24,8},{1,17},{9,25},{17,1},{25,9},{2,18},{10... | collective-permute-start | bytes 392 | tf_op jit(solution)/shard_map/ppermute | solution.py:234
  29.2 0.9 %collective-permute-done.refs_1_ = s32[32]{0:T(128)S(1)} collective-permute-done((s32[32]{0:T(128)S(1)}, s32[32]{0:T(128)S(1)}, u32[]{:S(2)}, u32[]{:S(2)}) %collective-permute-start) | collective-permute-done | bytes 160 | tf_op jit(solution)/shard_map/ppermute | solution.py:234
  30.1 2.1 %collective-permute-start.2 = (s32[32]{0:T(128)S(1)}, s32[32]{0:T(128)S(1)}, u32[]{:S(2)}, u32[]{:S(2)}) collective-permute-start(s32[32]{0:T(128)S(1)} %bitcast.36), channel_id=1, source_target_pairs={{0,24},{8,16},{16,8},{24,0},{1,25},{9,17},{17,9},{25,1},{2,26},{10... | collective-permute-start | bytes 392 | tf_op jit(solution)/shard_map/ppermute | solution.py:234
  32.1 2.4 %collective-permute-done.2.refs_3_ = s32[32]{0:T(128)S(1)} collective-permute-done((s32[32]{0:T(128)S(1)}, s32[32]{0:T(128)S(1)}, u32[]{:S(2)}, u32[]{:S(2)}) %collective-permute-start.2) | collective-permute-done | bytes 160 | tf_op jit(solution)/shard_map/ppermute | solution.py:234
  34.5 0.6 %copy-done.14 = s32[32]{0:T(128)} copy-done((s32[32]{0:T(128)}, s32[32]{0:T(128)S(1)}, u32[]{:S(2)}) %copy-start.14) | copy-done | bytes 152
  35.1 3.7 %next_fields.1 = (f32[32,8,256]{2,1,0:T(8,128)}, f32[32,8,256]{2,1,0:T(8,128)}, f32[32,8,256]{2,1,0:T(8,128)}, s32[24]{0:T(128)}) custom-call(s32[3]{0:T(128)} %pad_add_fusion.where_ref, s32[32]{0:T(128)} %bitcast.33, s32[32]{0:T(128)} %copy-done.12, s32[32]{0:T(128)} %copy-done.13, s32[32]{0:T(128)} %copy-done.14, f32[32,8,256]{2,1,0:T(8,128)} %bitcast.24, ...), custom_call_target="tpu_custom_call" | custom-call | flops 2000000 | bytes 3000000 | tf_op jit(solution)/shard_map/next_fields/pallas_call | solution.py:292
  38.8 0.6 %copy-done.5 = f32[8,8,256]{2,1,0:T(8,128)} copy-done((f32[8,8,256]{2,1,0:T(8,128)}, f32[8,8,256]{2,1,0:T(8,128)S(1)}, u32[]{:S(2)}) %copy-start.5) | copy-done | bytes 65560
  39.4 0.0 copy-done.6
  39.4 0.0 copy-done.7
  39.5 1.8 %image_rows.1 = f32[32,8,256]{2,1,0:T(8,128)} custom-call(s32[24]{0:T(128)} %get-tuple-element.18.places_ref, f32[32,8,256]{2,1,0:T(8,128)} %get-tuple-element.19.own_ref, f32[8,8,256]{2,1,0:T(8,128)} %copy-done.5, f32[8,8,256]{2,1,0:T(8,128)} %copy-done.6, f32[8,8,256]{2,1,0:T(8,128)} %copy-done.7), custom_call_target="tpu_custom_call" | custom-call | tf_op jit(solution)/shard_map/image_rows/pallas_call | solution.py:302
  (29 shorter events, 0.1 us)
Async XLA Ops:
  1.3 3.4 %copy-start.4 = (bf16[1,32,8,256]{3,2,1,0:T(8,128)(2,1)S(1)}, bf16[1,32,8,256]{3,2,1,0:T(8,128)(2,1)}, u32[]{:S(2)}) copy-start(bf16[1,32,8,256]{3,2,1,0:T(8,128)(2,1)} %param.14) | copy-start | bytes 393220
  3.1 5.1 %collective-permute-start.3 = (f32[2,4,8,256]{3,2,1,0:T(8,128)}, f32[2,4,8,256]{3,2,1,0:T(8,128)S(1)}, u32[]{:S(2)}, u32[]{:S(2)}) collective-permute-start(f32[2,4,8,256]{3,2,1,0:T(8,128)} %get-tuple-element.13), channel_id=1, source_target_pairs={{0,2},{2,0},{4,6},{6,4},{1,3},{3,1},{5,7},{7,5},{8,10},{10,8},{12,... | collective-permute-start | bytes 196616 | tf_op jit(solution)/shard_map/ppermute | solution.py:251
  4.7 10.0 %collective-permute-start.5 = (f32[2,16,8,256]{3,2,1,0:T(8,128)}, f32[2,16,8,256]{3,2,1,0:T(8,128)S(1)}, u32[]{:S(2)}, u32[]{:S(2)}) collective-permute-start(f32[2,16,8,256]{3,2,1,0:T(8,128)} %get-tuple-element.15), channel_id=1, source_target_pairs={{0,1},{1,0},{2,3},{3,2},{4,5},{5,4},{6,7},{7,6},{8,9},{9,8},{10,11... | collective-permute-start | bytes 786440 | tf_op jit(solution)/shard_map/ppermute | solution.py:252
  4.7 14.7 %collective-permute-start.6 = (bf16[32,8,256]{2,1,0:T(8,128)(2,1)S(1)}, bf16[32,8,256]{2,1,0:T(8,128)(2,1)S(1)}, u32[]{:S(2)}, u32[]{:S(2)}) collective-permute-start(bf16[32,8,256]{2,1,0:T(8,128)(2,1)S(1)} %bitcast.29), channel_id=1, source_target_pairs={{0,8},{8,0},{16,24},{24,16},{1,9},{9,1},{17,25},{25,17},{2,10},{10... | collective-permute-start | bytes 393224 | tf_op jit(solution)/shard_map/ppermute | solution.py:234
  6.2 13.2 %collective-permute-start.7 = (bf16[32,8,256]{2,1,0:T(8,128)(2,1)S(1)}, bf16[32,8,256]{2,1,0:T(8,128)(2,1)S(1)}, u32[]{:S(2)}, u32[]{:S(2)}) collective-permute-start(bf16[32,8,256]{2,1,0:T(8,128)(2,1)S(1)} %bitcast.30), channel_id=1, source_target_pairs={{0,16},{8,24},{16,0},{24,8},{1,17},{9,25},{17,1},{25,9},{2,18},{10... | collective-permute-start | bytes 393224 | tf_op jit(solution)/shard_map/ppermute | solution.py:234
  7.7 11.7 %collective-permute-start.8 = (bf16[32,8,256]{2,1,0:T(8,128)(2,1)S(1)}, bf16[32,8,256]{2,1,0:T(8,128)(2,1)S(1)}, u32[]{:S(2)}, u32[]{:S(2)}) collective-permute-start(bf16[32,8,256]{2,1,0:T(8,128)(2,1)S(1)} %bitcast.31), channel_id=1, source_target_pairs={{0,24},{8,16},{16,8},{24,0},{1,25},{9,17},{17,9},{25,1},{2,26},{10... | collective-permute-start | bytes 393224 | tf_op jit(solution)/shard_map/ppermute | solution.py:234
  8.2 2.1 %copy-start.11 = (s32[1,128,2]{1,2,0:T(2,128)S(1)}, s32[1,128,2]{1,2,0:T(2,128)}, u32[]{:S(2)}) copy-start(s32[1,128,2]{1,2,0:T(2,128)} %param.18) | copy-start | bytes 3076
  8.2 6.5 %copy-start.8 = (f32[2,4,8,256]{3,2,1,0:T(8,128)}, f32[2,4,8,256]{3,2,1,0:T(8,128)S(1)}, u32[]{:S(2)}) copy-start(f32[2,4,8,256]{3,2,1,0:T(8,128)S(1)} %collective-permute-done.3.refs_0_) | copy-start | bytes 196612
  8.2 6.5 %collective-permute-start.4 = (f32[2,4,8,256]{3,2,1,0:T(8,128)}, f32[2,4,8,256]{3,2,1,0:T(8,128)S(1)}, u32[]{:S(2)}, u32[]{:S(2)}) collective-permute-start(f32[2,4,8,256]{3,2,1,0:T(8,128)} %get-tuple-element.14), channel_id=1, source_target_pairs={{2,4},{4,2},{3,5},{5,3},{10,12},{12,10},{11,13},{13,11},{18,20},{2... | collective-permute-start | bytes 196616 | tf_op jit(solution)/shard_map/ppermute | solution.py:251
  14.7 0.6 %copy-start.9 = (f32[2,4,8,256]{3,2,1,0:T(8,128)}, f32[2,4,8,256]{3,2,1,0:T(8,128)S(1)}, u32[]{:S(2)}) copy-start(f32[2,4,8,256]{3,2,1,0:T(8,128)S(1)} %collective-permute-done.4.refs_1_) | copy-start | bytes 196612
  14.7 0.7 %copy-start.3 = (f32[2,16,8,256]{3,2,1,0:T(8,128)}, f32[2,16,8,256]{3,2,1,0:T(8,128)S(1)}, u32[]{:S(2)}) copy-start(f32[2,16,8,256]{3,2,1,0:T(8,128)S(1)} %collective-permute-done.5.refs_2_) | copy-start | bytes 786436
  19.4 0.7 %copy-start = (bf16[32,8,256]{2,1,0:T(8,128)(2,1)}, bf16[32,8,256]{2,1,0:T(8,128)(2,1)S(1)}, u32[]{:S(2)}) copy-start(bf16[32,8,256]{2,1,0:T(8,128)(2,1)S(1)} %collective-permute-done.6.refs_10_.refs_5_) | copy-start | bytes 393220
  19.4 0.7 %copy-start.1 = (bf16[32,8,256]{2,1,0:T(8,128)(2,1)}, bf16[32,8,256]{2,1,0:T(8,128)(2,1)S(1)}, u32[]{:S(2)}) copy-start(bf16[32,8,256]{2,1,0:T(8,128)(2,1)S(1)} %collective-permute-done.7.refs_11_.refs_6_) | copy-start | bytes 393220
  19.4 0.7 %copy-start.2 = (bf16[32,8,256]{2,1,0:T(8,128)(2,1)}, bf16[32,8,256]{2,1,0:T(8,128)(2,1)S(1)}, u32[]{:S(2)}) copy-start(bf16[32,8,256]{2,1,0:T(8,128)(2,1)S(1)} %collective-permute-done.8.refs_12_.refs_7_) | copy-start | bytes 393220
  22.7 16.1 %collective-permute-start.9 = (f32[8,8,256]{2,1,0:T(8,128)}, f32[8,8,256]{2,1,0:T(8,128)S(1)}, u32[]{:S(2)}, u32[]{:S(2)}) collective-permute-start(f32[8,8,256]{2,1,0:T(8,128)} %get-tuple-element.20), channel_id=1, source_target_pairs={{0,8},{8,0},{16,24},{24,16},{1,9},{9,1},{17,25},{25,17},{2,10},{10... | collective-permute-start | bytes 196616 | tf_op jit(solution)/shard_map/ppermute | solution.py:234
  24.1 2.0 %copy-start.10 = (s32[1,1,32]{2,1,0:T(1,128)S(1)}, s32[1,1,32]{2,1,0:T(1,128)}, u32[]{:S(2)}) copy-start(s32[1,1,32]{2,1,0:T(1,128)} %param.15) | copy-start | bytes 388
  24.2 14.7 %collective-permute-start.10 = (f32[8,8,256]{2,1,0:T(8,128)}, f32[8,8,256]{2,1,0:T(8,128)S(1)}, u32[]{:S(2)}, u32[]{:S(2)}) collective-permute-start(f32[8,8,256]{2,1,0:T(8,128)} %get-tuple-element.21), channel_id=1, source_target_pairs={{0,16},{8,24},{16,0},{24,8},{1,17},{9,25},{17,1},{25,9},{2,18},{10... | collective-permute-start | bytes 196616 | tf_op jit(solution)/shard_map/ppermute | solution.py:234
  25.7 13.2 %collective-permute-start.11 = (f32[8,8,256]{2,1,0:T(8,128)}, f32[8,8,256]{2,1,0:T(8,128)S(1)}, u32[]{:S(2)}, u32[]{:S(2)}) collective-permute-start(f32[8,8,256]{2,1,0:T(8,128)} %get-tuple-element.22), channel_id=1, source_target_pairs={{0,24},{8,16},{16,8},{24,0},{1,25},{9,17},{17,9},{25,1},{2,26},{10... | collective-permute-start | bytes 196616 | tf_op jit(solution)/shard_map/ppermute | solution.py:234
  26.2 3.9 %collective-permute-start = (s32[32]{0:T(128)S(1)}, s32[32]{0:T(128)S(1)}, u32[]{:S(2)}, u32[]{:S(2)}) collective-permute-start(s32[32]{0:T(128)S(1)} %bitcast.34), channel_id=1, source_target_pairs={{0,8},{8,0},{16,24},{24,16},{1,9},{9,1},{17,25},{25,17},{2,10},{10... | collective-permute-start | bytes 392 | tf_op jit(solution)/shard_map/ppermute | solution.py:234
  27.6 4.5 %collective-permute-start.1 = (s32[32]{0:T(128)S(1)}, s32[32]{0:T(128)S(1)}, u32[]{:S(2)}, u32[]{:S(2)}) collective-permute-start(s32[32]{0:T(128)S(1)} %bitcast.35), channel_id=1, source_target_pairs={{0,16},{8,24},{16,0},{24,8},{1,17},{9,25},{17,1},{25,9},{2,18},{10... | collective-permute-start | bytes 392 | tf_op jit(solution)/shard_map/ppermute | solution.py:234
  30.1 4.4 %copy-start.12 = (s32[32]{0:T(128)}, s32[32]{0:T(128)S(1)}, u32[]{:S(2)}) copy-start(s32[32]{0:T(128)S(1)} %collective-permute-done.refs_1_) | copy-start | bytes 388
  30.1 4.4 %collective-permute-start.2 = (s32[32]{0:T(128)S(1)}, s32[32]{0:T(128)S(1)}, u32[]{:S(2)}, u32[]{:S(2)}) collective-permute-start(s32[32]{0:T(128)S(1)} %bitcast.36), channel_id=1, source_target_pairs={{0,24},{8,16},{16,8},{24,0},{1,25},{9,17},{17,9},{25,1},{2,26},{10... | collective-permute-start | bytes 392 | tf_op jit(solution)/shard_map/ppermute | solution.py:234
  32.1 2.4 %copy-start.13 = (s32[32]{0:T(128)}, s32[32]{0:T(128)S(1)}, u32[]{:S(2)}) copy-start(s32[32]{0:T(128)S(1)} %collective-permute-done.1.refs_2_) | copy-start | bytes 388
  34.5 0.6 %copy-start.14 = (s32[32]{0:T(128)}, s32[32]{0:T(128)S(1)}, u32[]{:S(2)}) copy-start(s32[32]{0:T(128)S(1)} %collective-permute-done.2.refs_3_) | copy-start | bytes 388
  38.8 0.6 %copy-start.5 = (f32[8,8,256]{2,1,0:T(8,128)}, f32[8,8,256]{2,1,0:T(8,128)S(1)}, u32[]{:S(2)}) copy-start(f32[8,8,256]{2,1,0:T(8,128)S(1)} %collective-permute-done.9.refs_0_) | copy-start | bytes 196612
  38.8 0.6 %copy-start.6 = (f32[8,8,256]{2,1,0:T(8,128)}, f32[8,8,256]{2,1,0:T(8,128)S(1)}, u32[]{:S(2)}) copy-start(f32[8,8,256]{2,1,0:T(8,128)S(1)} %collective-permute-done.10.refs_1_) | copy-start | bytes 196612
  38.8 0.6 %copy-start.7 = (f32[8,8,256]{2,1,0:T(8,128)}, f32[8,8,256]{2,1,0:T(8,128)S(1)}, u32[]{:S(2)}) copy-start(f32[8,8,256]{2,1,0:T(8,128)S(1)} %collective-permute-done.11.refs_2_) | copy-start | bytes 196612

commit v2 on v0

v2 whole, which is shorter than its diff:
```python
import functools

import jax
import jax.numpy as jnp
from jax import lax
from jax.experimental import pallas as pl
from jax.experimental.pallas import tpu as pltpu
from jax.sharding import PartitionSpec as P

SURFACE_DEPTH = 8


STENCIL_WEIGHTS = (-205.0 / 72.0, 8.0 / 5.0, -1.0 / 5.0, 8.0 / 315.0, -1.0 / 560.0)
STEP_RATIO = 0.1
REACH = 4

VMEM = pl.BlockSpec(memory_space=pltpu.VMEM)
SMEM = pl.BlockSpec(memory_space=pltpu.SMEM)
PARAMS = pltpu.CompilerParams(vmem_limit_bytes=16 * 1024 * 1024)
F32, BF16 = jnp.float32, jnp.bfloat16


def swaps(count):
    even = [(i, i + 1) for i in range(0, count - 1, 2)]
    odd = [(i, i + 1) for i in range(1, count - 1, 2)]
    return [[pair for a, b in pairs for pair in ((a, b), (b, a))] for pairs in (even, odd)]


def halves(value):
    high = value.astype(BF16)
    return high, (value - high.astype(F32)).astype(BF16)


def product(left, right):
    (a, b), (c, d) = left, right

    def dot(x, y):
        return jnp.dot(x, y, preferred_element_type=F32)

    return dot(a, c) + (dot(a, d) + dot(b, c))


def by_distance(gap, stride=1):
    weights = jnp.zeros(gap.shape, F32)
    for offset in range(1, REACH + 1):
        weights = jnp.where(gap == offset * stride, STENCIL_WEIGHTS[offset], weights)
    return weights


def pack_kernel(f_ref, a_ref, x_even_ref, x_odd_ref, y_even_ref, y_odd_ref=None):
    cells_x, cells_y, cells_z = f_ref.shape
    half = cells_x // 2
    x_at_even = lax.axis_index("tx") % 2 == 0
    y_at_even = lax.axis_index("ty") % 2 == 0
    tail, head = cells_x - REACH, 0
    start_even = jnp.where(x_at_even, tail, head)
    start_odd = jnp.where(x_at_even, head, tail)
    low = (lax.broadcasted_iota(jnp.int32, (half, cells_y, cells_z), 1) < REACH).astype(jnp.int32)

    def face(ref, tails):
        turn = jnp.where(tails, 0, half)
        turned = pltpu.roll(ref[pl.ds(turn, half)], REACH, 1)
        straight = ref[pl.ds(half - turn, half)]
        return jnp.where(low == tails.astype(jnp.int32), turned, straight)

    for field, ref in enumerate((f_ref, a_ref)):
        x_even_ref[field] = ref[pl.ds(start_even, REACH)]
        x_odd_ref[field] = ref[pl.ds(start_odd, REACH)]
        y_even_ref[field] = face(ref, y_at_even)
        if y_odd_ref is not None:
            y_odd_ref[field] = face(ref, jnp.logical_not(y_at_even))


def inner_kernel(
    owners, slab, source_ref, strength_ref, receiver_ref, trace_ref, ids_ref, fp_ref, fn_ref, ap_ref, an_ref,
    out_ref, rows_ref, taken_ref,
):
    cells_x, cells_y, cells_z = fn_ref.shape
    cells = cells_x * cells_y
    capacity = cells_x // owners
    row = lax.broadcasted_iota(jnp.int32, (cells_z, cells_z), 0)
    col = lax.broadcasted_iota(jnp.int32, (cells_z, cells_z), 1)
    along_z = halves(by_distance(jnp.abs(row - col)))
    row = lax.broadcasted_iota(jnp.int32, (cells, cells), 0)
    col = lax.broadcasted_iota(jnp.int32, (cells, cells), 1)
    gap = jnp.abs(row - col)
    along_y = jnp.where(row // cells_y == col // cells_y, by_distance(gap), 0.0)
    along_xy = halves(along_y + by_distance(gap, cells_y))
    for field, (prev_ref, now_ref) in enumerate(((fp_ref, fn_ref), (ap_ref, an_ref))):
        now = now_ref[...].reshape(cells, cells_z)
        parts = halves(now)
        total = product(parts, along_z) + product(along_xy, parts)
        total = total + (3.0 * STENCIL_WEIGHTS[0]) * now
        out_ref[2 + field] = total.reshape(cells_x, cells_y, cells_z)
        out_ref[field] = 2.0 * now_ref[...] - prev_ref[...]

    start_x = lax.axis_index("tx") * cells_x
    start_y = lax.axis_index("ty") * cells_y
    near_x = receiver_ref[0:1, :] - start_x
    near_y = receiver_ref[1:2, :] - start_y
    cell_x = lax.broadcasted_iota(jnp.int32, (cells_x, cells_y, near_x.shape[1]), 0)
    cell_y = lax.broadcasted_iota(jnp.int32, cell_x.shape, 1)
    hit = jnp.where((cell_x == near_x[None]) & (cell_y == near_y[None]), trace_ref[...][None], 0.0)
    surface = jnp.sum(hit, axis=2, keepdims=True)
    lanes = min(cells_z, 128)
    depth = lax.broadcasted_iota(jnp.int32, (cells_x, cells_y, lanes), 2) == SURFACE_DEPTH
    out_ref[3, :, :, :lanes] = out_ref[3, :, :, :lanes] + jnp.where(depth, surface, 0.0)
    source_x = source_ref[0, 0] - start_x
    source_y = source_ref[0, 1] - start_y

    @pl.when((source_x >= 0) & (source_x < cells_x))
    def _():
        sub = lax.broadcasted_iota(jnp.int32, (cells_y, cells_z), 0)
        lane = lax.broadcasted_iota(jnp.int32, (cells_y, cells_z), 1)
        mark = (sub == source_y) & (lane == SURFACE_DEPTH)
        out_ref[2, source_x] = out_ref[2, source_x] + jnp.where(mark, strength_ref[0], 0.0)

    for owner in range(owners):
        taken_ref[owner] = 0

    def one_row(r, _):
        owner = ids_ref[0, 0, r] // slab
        slot = taken_ref[owner]
        rows_ref[owner * capacity + slot] = r
        taken_ref[owner] = slot + 1
        return 0

    lax.fori_loop(0, cells_x, one_row, 0, unroll=4)


def edge_kernel(x_even_ref, x_odd_ref, *refs):
    y_refs, (in_ref, out_ref) = refs[:-2], refs[-2:]
    _, cells_x, cells_y, cells_z = in_ref.shape
    half = cells_x // 2
    cells = cells_x * cells_y
    x_at_even = lax.axis_index("tx") % 2 == 0
    y_at_even = lax.axis_index("ty") % 2 == 0
    row = lax.broadcasted_iota(jnp.int32, (cells, half * cells_y), 0)
    col = lax.broadcasted_iota(jnp.int32, (cells, half * cells_y), 1)
    sub = col % cells_y
    same = row // cells_y == col // cells_y + half * (sub // REACH)
    layer, y = sub % REACH, row % cells_y
    after = by_distance(jnp.where(same, cells_y + layer - y, 0))
    before = by_distance(jnp.where(same, y + REACH - layer, 0))
    from_even = halves(jnp.where(y_at_even, after, before))
    from_odd = halves(jnp.where(y_at_even, before, after))
    for field in range(2):
        curve = in_ref[2 + field].reshape(cells, cells_z)
        for ref, weights in zip(y_refs, (from_even, from_odd)):
            curve = curve + product(weights, halves(ref[field].reshape(half * cells_y, cells_z)))
        out_ref[2 + field] = curve.reshape(cells_x, cells_y, cells_z)
        out_ref[field] = in_ref[field]
        before_x = jnp.where(x_at_even, x_odd_ref[field], x_even_ref[field])
        after_x = jnp.where(x_at_even, x_even_ref[field], x_odd_ref[field])
        for place in range(REACH):
            low = out_ref[2 + field, place]
            high = out_ref[2 + field, cells_x - REACH + place]
            for layer in range(REACH):
                if place + REACH - layer <= REACH:
                    low = low + STENCIL_WEIGHTS[place + REACH - layer] * before_x[layer]
                if layer + REACH - place <= REACH:
                    high = high + STENCIL_WEIGHTS[layer + REACH - place] * after_x[layer]
            out_ref[2 + field, place] = low
            out_ref[2 + field, cells_x - REACH + place] = high


def next_kernel(owners, rows_ref, ids_ref, *refs):
    state_ref, slabs, refs = refs[0], refs[1 : 1 + owners], refs[1 + owners :]
    messages, (f_out_ref, a_out_ref) = refs[:owners], refs[owners:]
    slab, cells_y, cells_z = slabs[0].shape
    capacity = f_out_ref.shape[0] // owners
    lanes = messages[0].shape[1]
    count = capacity * cells_y
    me = lax.axis_index("shot")
    lane = lax.broadcasted_iota(jnp.int32, (cells_y, lanes), 1) // cells_y
    for k in range(owners):
        place = jnp.zeros((cells_y, lanes), F32)
        for j in range(capacity):
            r = rows_ref[(me ^ k) * capacity + j]
            block = ids_ref[0, 0, r] % slab
            scaled = slabs[k][block].astype(F32) * STEP_RATIO
            courant = scaled * scaled
            f_next = state_ref[0, r] + courant * state_ref[2, r]
            a_next = state_ref[1, r] + courant * state_ref[3, r]
            f_out_ref[r] = f_next
            a_out_ref[r] = a_next
            image = f_next * a_next
            for part in range(cells_z // lanes):
                start = part * count + j * cells_y
                messages[k][start : start + cells_y, :] = image[:, part * lanes : (part + 1) * lanes]
            place = jnp.where(lane == j, block.astype(F32), place)
        messages[k][(cells_z // lanes) * count :, :] = place


def image_kernel(*refs):
    messages, out_ref = refs[:-1], refs[-1]
    slab, cells_y, cells_z = out_ref.shape
    lanes = messages[0].shape[1]
    parts = cells_z // lanes
    count = (messages[0].shape[0] - cells_y) // parts
    places = jnp.concatenate([ref[parts * count : parts * count + 1, :count] for ref in messages], axis=1)
    row = lax.broadcasted_iota(jnp.int32, (slab * cells_y, places.shape[1]), 0)
    col = lax.broadcasted_iota(jnp.int32, row.shape, 1)
    chosen = (row // cells_y == places.astype(jnp.int32)) & (row % cells_y == col % cells_y)
    chosen = jnp.where(chosen, 1.0, 0.0).astype(BF16)
    for part in range(parts):
        rows = jnp.concatenate([ref[part * count : (part + 1) * count, :] for ref in messages], axis=0)
        high, low = halves(rows)
        total = jnp.dot(chosen, high, preferred_element_type=F32) + jnp.dot(chosen, low, preferred_element_type=F32)
        out_ref[:, :, part * lanes : (part + 1) * lanes] = total.reshape(slab, cells_y, lanes)


def in_vmem(value):
    return pltpu.with_memory_space_constraint(value, pltpu.VMEM)


def in_smem(value):
    return pltpu.with_memory_space_constraint(value, pltpu.SMEM)


def on_device(
    forward_prev,
    forward_now,
    adjoint_prev,
    adjoint_now,
    velocity_model,
    aperture,
    source_cell,
    source_strength,
    receiver_cell,
    receiver_trace,
):
    owners = lax.axis_size("shot")
    count_x, count_y = lax.axis_size("tx"), lax.axis_size("ty")
    cells_x, cells_y, cells_z = forward_now.shape[1:]
    slab = velocity_model.shape[1]
    capacity = cells_x // owners
    forward_now, adjoint_now = in_vmem(forward_now[0]), in_vmem(adjoint_now[0])

    def peer(value, k):
        return lax.ppermute(value, "shot", [(i, i ^ k) for i in range(owners)])

    own_slab = velocity_model[0]
    slabs = [own_slab] + [peer(own_slab, k) for k in range(1, owners)]

    sides = 2 if count_y > 2 else 1
    x_face = pltpu.VMEM((2, REACH, cells_y, cells_z), F32)
    y_face = pltpu.VMEM((2, cells_x // 2, cells_y, cells_z), F32)
    faces = pl.pallas_call(
        pack_kernel,
        out_shape=(x_face, x_face) + (y_face,) * sides,
        in_specs=[VMEM, VMEM],
        out_specs=(VMEM,) * (2 + sides),
        compiler_params=PARAMS,
        name="pack_faces",
    )(forward_now, adjoint_now)
    halos = [lax.ppermute(face, "tx", pairs) for face, pairs in zip(faces[:2], swaps(count_x))]
    halos += [lax.ppermute(face, "ty", pairs) for face, pairs in zip(faces[2:], swaps(count_y))]

    state_shape = pltpu.VMEM((4, cells_x, cells_y, cells_z), F32)
    state, rows = pl.pallas_call(
        functools.partial(inner_kernel, owners, slab),
        out_shape=(state_shape, pltpu.SMEM((cells_x,), jnp.int32)),
        in_specs=[SMEM, SMEM, VMEM, VMEM, SMEM] + [VMEM] * 4,
        out_specs=(VMEM, SMEM),
        scratch_shapes=[pltpu.SMEM((owners,), jnp.int32)],
        compiler_params=PARAMS,
        name="inner_cells",
    )(
        source_cell,
        source_strength,
        receiver_cell[0].T,
        receiver_trace,
        aperture,
        in_vmem(forward_prev[0]),
        forward_now,
        in_vmem(adjoint_prev[0]),
        adjoint_now,
    )
    state = pl.pallas_call(
        edge_kernel,
        out_shape=state_shape,
        in_specs=[VMEM] * (len(halos) + 1),
        out_specs=VMEM,
        input_output_aliases={len(halos): 0},
        compiler_params=PARAMS,
        name="edge_cells",
    )(*[in_vmem(halo) for halo in halos], in_vmem(state))

    lanes = min(cells_z, 128)
    message = pltpu.VMEM(((cells_z // lanes) * capacity * cells_y + cells_y, lanes), F32)
    field = pltpu.VMEM((cells_x, cells_y, cells_z), F32)
    results = pl.pallas_call(
        functools.partial(next_kernel, owners),
        out_shape=(message,) * owners + (field, field),
        in_specs=[SMEM, SMEM] + [VMEM] * (1 + owners),
        out_specs=(VMEM,) * (owners + 2),
        compiler_params=PARAMS,
        name="next_cells",
    )(in_smem(rows), aperture, in_vmem(state), *[in_vmem(block) for block in slabs])
    messages, (forward_next, adjoint_next) = results[:owners], results[owners:]
    arrived = [messages[0]] + [peer(rows, k) for k, rows in enumerate(messages[1:], 1)]

    image = pl.pallas_call(
        image_kernel,
        out_shape=jax.ShapeDtypeStruct((slab, cells_y, cells_z), F32),
        in_specs=[VMEM] * owners,
        out_specs=VMEM,
        compiler_params=PARAMS,
        name="image_rows",
    )(*[in_vmem(rows) for rows in arrived])
    return forward_next[None], adjoint_next[None], image[None]


def solution(mesh):
    in_specs = (
        P("shot", "tx", "ty", None),
        P("shot", "tx", "ty", None),
        P("shot", "tx", "ty", None),
        P("shot", "tx", "ty", None),
        P(("tx", "ty"), "shot", None, None),
        P("shot", ("tx", "ty"), None),
        P("shot", None),
        P("shot"),
        P("shot", None, None),
        P("shot", None),
    )
    out_specs = (
        P("shot", "tx", "ty", None),
        P("shot", "tx", "ty", None),
        P(("tx", "ty"), "shot", None, None),
    )
    return jax.shard_map(
        on_device, mesh=mesh, in_specs=in_specs, out_specs=out_specs, check_vma=False
    )
```

time: 80.8 us -> 27.4 us (0.34)
  the two profiles are of different devices: /device:TPU:0 before, /device:TPU:8 now
where the time goes in v2:
time: 27.4 us; the launch traced here: 27.1 us
  starting transfers between devices  11.3 us (41%)
  local copies, waits for them, and re-layouts  6.22 us (23%)
  waiting for transfers between devices  4.21 us (15%)
  Pallas kernels  3.83 us (14%)
  between operations  1.47 us (5%)
    ppermute x6, starting transfers between devices, peer(): return lax.ppermute(value, 'shot', [(i, i ^ k) for i in range(owners)])  7.11 us
    unnamed x24, local copies, waits for them, and re-layouts  6.22 us
    ppermute x2, starting transfers between devices, on_device(): lax.ppermute(face, 'tx', pairs)  4.17 us
    ppermute x6, waiting for transfers between devices, peer(): return lax.ppermute(value, 'shot', [(i, i ^ k) for i in range(owners)])  3.33 us
    pallas_call x1, Pallas kernels, on_device(): pl.pallas_call(functools.partial(inner_kernel, owners, slab), out_shape=(...  1.46 us
    pallas_call x1, Pallas kernels, on_device(): pl.pallas_call(image_kernel, out_shape=jax.ShapeDtypeStruct((slab, cells_...  1.05 us
    ppermute x2, waiting for transfers between devices, on_device(): lax.ppermute(face, 'tx', pairs)  0.88 us
    pallas_call x1, Pallas kernels, on_device(): pl.pallas_call(functools.partial(next_kernel, owners), out_shape=(message...  0.78 us
  transfers between devices with their start and end apart: 9, of which 3 were waited for; matrix products, arithmetic and copies ran while one was open for 5% of the time, Pallas kernels for 7%

profile of v2, /device:TPU:8, one launch (start us, length us, event | category | flops | bytes accessed | tf_op | source)
XLA Modules:
  0.0 27.1 jit_solution(4765100535535709519)
XLA Ops:
  0.6 0.9 %copy-done = f32[1,32,8,256]{3,2,1,0:T(8,128)S(1)} copy-done((f32[1,32,8,256]{3,2,1,0:T(8,128)S(1)}, f32[1,32,8,256]{3,2,1,0:T(8,128)}, u32[]{:S(2)}) %copy-start) | copy-done | bytes 262168
  1.6 0.9 %copy-done.2 = f32[1,32,8,256]{3,2,1,0:T(8,128)S(1)} copy-done((f32[1,32,8,256]{3,2,1,0:T(8,128)S(1)}, f32[1,32,8,256]{3,2,1,0:T(8,128)}, u32[]{:S(2)}) %copy-start.2) | copy-done | bytes 262168
  2.6 0.1 collective-permute-start.2
  2.7 0.1 collective-permute-start
  2.7 1.9 %collective-permute-start.3 = (bf16[32,8,256]{2,1,0:T(8,128)(2,1)}, bf16[32,8,256]{2,1,0:T(8,128)(2,1)S(1)}, u32[]{:S(2)}, u32[]{:S(2)}) collective-permute-start(bf16[32,8,256]{2,1,0:T(8,128)(2,1)} %bitcast.19), channel_id=1, source_target_pairs={{0,8},{8,0},{16,24},{24,16},{1,9},{9,1},{17,25},{25,17},{2,10},{10... | collective-permute-start | bytes 393224 | tf_op jit(solution)/shard_map/ppermute | solution.py:241
  4.7 1.5 %collective-permute-start.4 = (bf16[32,8,256]{2,1,0:T(8,128)(2,1)}, bf16[32,8,256]{2,1,0:T(8,128)(2,1)S(1)}, u32[]{:S(2)}, u32[]{:S(2)}) collective-permute-start(bf16[32,8,256]{2,1,0:T(8,128)(2,1)} %bitcast.20), channel_id=1, source_target_pairs={{0,16},{8,24},{16,0},{24,8},{1,17},{9,25},{17,1},{25,9},{2,18},{10... | collective-permute-start | bytes 393224 | tf_op jit(solution)/shard_map/ppermute | solution.py:241
  6.2 0.1 collective-permute-start.5
  6.3 0.9 %collective-permute-done.x_even_ref = f32[2,4,8,256]{3,2,1,0:T(8,128)S(1)} collective-permute-done((f32[2,4,8,256]{3,2,1,0:T(8,128)S(1)}, f32[2,4,8,256]{3,2,1,0:T(8,128)S(1)}, u32[]{:S(2)}, u32[]{:S(2)}) %collective-permute-start) | collective-permute-done | bytes 65568 | tf_op jit(solution)/shard_map/ppermute | solution.py:257
  7.2 4.1 %collective-permute-start.1 = (f32[2,4,8,256]{3,2,1,0:T(8,128)S(1)}, f32[2,4,8,256]{3,2,1,0:T(8,128)S(1)}, u32[]{:S(2)}, u32[]{:S(2)}) collective-permute-start(f32[2,4,8,256]{3,2,1,0:T(8,128)S(1)} %get-tuple-element.16), channel_id=1, source_target_pairs={{2,4},{4,2},{3,5},{5,3},{10,12},{12,10},{11,13},{13,11},{18,20},{2... | collective-permute-start | bytes 196616 | tf_op jit(solution)/shard_map/ppermute | solution.py:257
  11.3 0.0 copy-start.9
  11.3 0.0 copy-start.10
  12.0 0.0 copy-start.7
  12.0 0.0 copy-start.8
  12.0 0.6 %copy-done.7 = s32[1,1,32]{2,1,0:T(1,128)S(1)} copy-done((s32[1,1,32]{2,1,0:T(1,128)S(1)}, s32[1,1,32]{2,1,0:T(1,128)}, u32[]{:S(2)}) %copy-start.7) | copy-done | bytes 152
  12.6 0.0 copy-done.8
  12.7 0.9 %copy-done.4 = f32[1,32,8,256]{3,2,1,0:T(8,128)S(1)} copy-done((f32[1,32,8,256]{3,2,1,0:T(8,128)S(1)}, f32[1,32,8,256]{3,2,1,0:T(8,128)}, u32[]{:S(2)}) %copy-start.4) | copy-done | bytes 262168
  13.6 0.9 %copy-done.5 = f32[1,32,8,256]{3,2,1,0:T(8,128)S(1)} copy-done((f32[1,32,8,256]{3,2,1,0:T(8,128)S(1)}, f32[1,32,8,256]{3,2,1,0:T(8,128)}, u32[]{:S(2)}) %copy-start.5) | copy-done | bytes 262168
  14.6 1.5 %inner_cells.1 = (f32[4,32,8,256]{3,2,1,0:T(8,128)S(1)}, s32[32]{0:T(128)S(4)}) custom-call(s32[1,2]{1,0:T(1,128)S(1)} %copy-done.9, f32[1]{0:T(128)S(6)} %copy.17.strength_ref, s32[2,128]{1,0:T(2,128)S(1)} %bitcast.23, f32[1,128]{1,0:T(1,128)S(1)} %copy-done.10, s32[1,1,32]{2,1,0:T(1,128)S(1)} %copy-done.7, f32[32,8,256]{2,1,0:T(8,128)S(1)} %bitcast.17, ...), custom_call_target="tpu_custom_call" | custom-call | tf_op jit(solution)/shard_map/inner_cells/pallas_call | solution.py:261
  16.0 0.0 collective-permute-done.1.x_odd_ref
  16.0 0.0 collective-permute-done.2.refs_0_
  16.0 0.0 copy-start.6
  16.1 0.5 %edge_cells.1.refs_0_ = f32[4,32,8,256]{3,2,1,0:T(8,128)S(1)} custom-call(f32[2,4,8,256]{3,2,1,0:T(8,128)S(1)} %collective-permute-done.x_even_ref, f32[2,4,8,256]{3,2,1,0:T(8,128)S(1)} %collective-permute-done.1.x_odd_ref, f32[2,16,8,256]{3,2,1,0:T(8,128)S(1)} %collective-permute-done.2.refs_0_, ...), custom_call_target="tpu_custom_call", output_to_operand_aliasing={{}: (3, {})} | custom-call | tf_op jit(solution)/shard_map/edge_cells/pallas_call | solution.py:280
  16.6 0.4 %copy-done.6 = bf16[1,32,8,256]{3,2,1,0:T(8,128)(2,1)S(1)} copy-done((bf16[1,32,8,256]{3,2,1,0:T(8,128)(2,1)S(1)}, bf16[1,32,8,256]{3,2,1,0:T(8,128)(2,1)}, u32[]{:S(2)}) %copy-start.6) | copy-done | bytes 131096
  17.0 0.8 %next_cells.1 = (f32[136,128]{1,0:T(8,128)S(1)}, f32[136,128]{1,0:T(8,128)S(1)}, f32[136,128]{1,0:T(8,128)S(1)}, f32[136,128]{1,0:T(8,128)S(1)}, f32[32,8,256]{2,1,0:T(8,128)S(1)}, /*index=5*/f32[32,8,256]{2,1,0:T(8,128)S(1)}) custom-call(s32[32]{0:T(128)S(4)} %get-tuple-element.14.rows_ref, s32[1,1,32]{2,1,0:T(1,128)S(1)} %copy-done.7, ...), custom_call_target="tpu_custom_call" | custom-call | tf_op jit(solution)/shard_map/next_cells/pallas_call | solution.py:293
  17.7 1.6 %collective-permute-start.6 = (f32[136,128]{1,0:T(8,128)S(1)}, f32[136,128]{1,0:T(8,128)S(1)}, u32[]{:S(2)}, u32[]{:S(2)}) collective-permute-start(f32[136,128]{1,0:T(8,128)S(1)} %get-tuple-element.22), channel_id=1, source_target_pairs={{0,8},{8,0},{16,24},{24,16},{1,9},{9,1},{17,25},{25,17},{2,10},{10... | collective-permute-start | bytes 208904 | tf_op jit(solution)/shard_map/ppermute | solution.py:241
  19.3 1.5 %collective-permute-start.7 = (f32[136,128]{1,0:T(8,128)S(1)}, f32[136,128]{1,0:T(8,128)S(1)}, u32[]{:S(2)}, u32[]{:S(2)}) collective-permute-start(f32[136,128]{1,0:T(8,128)S(1)} %get-tuple-element.23), channel_id=1, source_target_pairs={{0,16},{8,24},{16,0},{24,8},{1,17},{9,25},{17,1},{25,9},{2,18},{10... | collective-permute-start | bytes 208904 | tf_op jit(solution)/shard_map/ppermute | solution.py:241
  20.8 0.5 %collective-permute-start.8 = (f32[136,128]{1,0:T(8,128)S(1)}, f32[136,128]{1,0:T(8,128)S(1)}, u32[]{:S(2)}, u32[]{:S(2)}) collective-permute-start(f32[136,128]{1,0:T(8,128)S(1)} %get-tuple-element.24), channel_id=1, source_target_pairs={{0,24},{8,16},{16,8},{24,0},{1,25},{9,17},{17,9},{25,1},{2,26},{10... | collective-permute-start | bytes 208904 | tf_op jit(solution)/shard_map/ppermute | solution.py:241
  21.3 0.7 %copy.15 = f32[1,32,8,256]{3,2,1,0:T(8,128)} copy(f32[1,32,8,256]{3,2,1,0:T(8,128)S(1)} %bitcast.12) | data formatting | bytes 524288
  22.0 0.7 %copy.16 = f32[1,32,8,256]{3,2,1,0:T(8,128)} copy(f32[1,32,8,256]{3,2,1,0:T(8,128)S(1)} %bitcast.11) | data formatting | bytes 524288
  22.7 1.6 %collective-permute-done.7.refs_2_ = f32[136,128]{1,0:T(8,128)S(1)} collective-permute-done((f32[136,128]{1,0:T(8,128)S(1)}, f32[136,128]{1,0:T(8,128)S(1)}, u32[]{:S(2)}, u32[]{:S(2)}) %collective-permute-start.7) | collective-permute-done | bytes 69664 | tf_op jit(solution)/shard_map/ppermute | solution.py:241
  24.3 1.7 %collective-permute-done.8.refs_3_ = f32[136,128]{1,0:T(8,128)S(1)} collective-permute-done((f32[136,128]{1,0:T(8,128)S(1)}, f32[136,128]{1,0:T(8,128)S(1)}, u32[]{:S(2)}, u32[]{:S(2)}) %collective-permute-start.8) | collective-permute-done | bytes 69664 | tf_op jit(solution)/shard_map/ppermute | solution.py:241
  26.0 1.0 %image_rows.1 = f32[32,8,256]{2,1,0:T(8,128)} custom-call(f32[136,128]{1,0:T(8,128)S(1)} %get-tuple-element.21.refs_0_, f32[136,128]{1,0:T(8,128)S(1)} %collective-permute-done.6.refs_1_, f32[136,128]{1,0:T(8,128)S(1)} %collective-permute-done.7.refs_2_, f32[136,128]{1,0:T(8,128)S(1)} %collective-permute-done.8.refs_3_), custom_call_target="tpu_custom_call" | custom-call | tf_op jit(solution)/shard_map/image_rows/pallas_call | solution.py:304
  (15 shorter events, 0.1 us)
Async XLA Ops:
  0.6 1.0 %copy-start = (f32[1,32,8,256]{3,2,1,0:T(8,128)S(1)}, f32[1,32,8,256]{3,2,1,0:T(8,128)}, u32[]{:S(2)}) copy-start(f32[1,32,8,256]{3,2,1,0:T(8,128)} %param.11) | copy-start | bytes 786436
  1.6 0.9 %copy-start.2 = (f32[1,32,8,256]{3,2,1,0:T(8,128)S(1)}, f32[1,32,8,256]{3,2,1,0:T(8,128)}, u32[]{:S(2)}) copy-start(f32[1,32,8,256]{3,2,1,0:T(8,128)} %param.13) | copy-start | bytes 786436
  2.5 9.5 %copy-start.1 = (f32[1,32,8,256]{3,2,1,0:T(8,128)S(1)}, f32[1,32,8,256]{3,2,1,0:T(8,128)}, u32[]{:S(2)}) copy-start(f32[1,32,8,256]{3,2,1,0:T(8,128)} %param.11) | copy-start | bytes 786436
  2.5 9.5 %copy-start.3 = (f32[1,32,8,256]{3,2,1,0:T(8,128)S(1)}, f32[1,32,8,256]{3,2,1,0:T(8,128)}, u32[]{:S(2)}) copy-start(f32[1,32,8,256]{3,2,1,0:T(8,128)} %param.13) | copy-start | bytes 786436
  2.6 13.5 %collective-permute-start.2 = (f32[2,16,8,256]{3,2,1,0:T(8,128)S(1)}, f32[2,16,8,256]{3,2,1,0:T(8,128)S(1)}, u32[]{:S(2)}, u32[]{:S(2)}) collective-permute-start(f32[2,16,8,256]{3,2,1,0:T(8,128)S(1)} %get-tuple-element.17), channel_id=1, source_target_pairs={{0,1},{1,0},{2,3},{3,2},{4,5},{5,4},{6,7},{7,6},{8,9},{9,8},{10,11... | collective-permute-start | bytes 786440 | tf_op jit(solution)/shard_map/ppermute | solution.py:258
  2.7 4.5 %collective-permute-start = (f32[2,4,8,256]{3,2,1,0:T(8,128)S(1)}, f32[2,4,8,256]{3,2,1,0:T(8,128)S(1)}, u32[]{:S(2)}, u32[]{:S(2)}) collective-permute-start(f32[2,4,8,256]{3,2,1,0:T(8,128)S(1)} %get-tuple-element.15), channel_id=1, source_target_pairs={{0,2},{2,0},{4,6},{6,4},{1,3},{3,1},{5,7},{7,5},{8,10},{10,8},{12,... | collective-permute-start | bytes 196616 | tf_op jit(solution)/shard_map/ppermute | solution.py:257
  2.7 13.8 %collective-permute-start.3 = (bf16[32,8,256]{2,1,0:T(8,128)(2,1)}, bf16[32,8,256]{2,1,0:T(8,128)(2,1)S(1)}, u32[]{:S(2)}, u32[]{:S(2)}) collective-permute-start(bf16[32,8,256]{2,1,0:T(8,128)(2,1)} %bitcast.19), channel_id=1, source_target_pairs={{0,8},{8,0},{16,24},{24,16},{1,9},{9,1},{17,25},{25,17},{2,10},{10... | collective-permute-start | bytes 393224 | tf_op jit(solution)/shard_map/ppermute | solution.py:241
  4.7 11.9 %collective-permute-start.4 = (bf16[32,8,256]{2,1,0:T(8,128)(2,1)}, bf16[32,8,256]{2,1,0:T(8,128)(2,1)S(1)}, u32[]{:S(2)}, u32[]{:S(2)}) collective-permute-start(bf16[32,8,256]{2,1,0:T(8,128)(2,1)} %bitcast.20), channel_id=1, source_target_pairs={{0,16},{8,24},{16,0},{24,8},{1,17},{9,25},{17,1},{25,9},{2,18},{10... | collective-permute-start | bytes 393224 | tf_op jit(solution)/shard_map/ppermute | solution.py:241
  6.2 10.4 %collective-permute-start.5 = (bf16[32,8,256]{2,1,0:T(8,128)(2,1)}, bf16[32,8,256]{2,1,0:T(8,128)(2,1)S(1)}, u32[]{:S(2)}, u32[]{:S(2)}) collective-permute-start(bf16[32,8,256]{2,1,0:T(8,128)(2,1)} %bitcast.21), channel_id=1, source_target_pairs={{0,24},{8,16},{16,8},{24,0},{1,25},{9,17},{17,9},{25,1},{2,26},{10... | collective-permute-start | bytes 393224 | tf_op jit(solution)/shard_map/ppermute | solution.py:241
  7.2 8.9 %collective-permute-start.1 = (f32[2,4,8,256]{3,2,1,0:T(8,128)S(1)}, f32[2,4,8,256]{3,2,1,0:T(8,128)S(1)}, u32[]{:S(2)}, u32[]{:S(2)}) collective-permute-start(f32[2,4,8,256]{3,2,1,0:T(8,128)S(1)} %get-tuple-element.16), channel_id=1, source_target_pairs={{2,4},{4,2},{3,5},{5,3},{10,12},{12,10},{11,13},{13,11},{18,20},{2... | collective-permute-start | bytes 196616 | tf_op jit(solution)/shard_map/ppermute | solution.py:257
  11.3 0.7 %copy-start.9 = (s32[1,2]{1,0:T(1,128)S(1)}, s32[1,2]{1,0:T(1,128)}, u32[]{:S(2)}) copy-start(s32[1,2]{1,0:T(1,128)} %source_ref.1) | copy-start | bytes 28
  11.3 0.7 %copy-start.10 = (f32[1,128]{1,0:T(1,128)S(1)}, f32[1,128]{1,0:T(1,128)}, u32[]{:S(2)}) copy-start(f32[1,128]{1,0:T(1,128)} %trace_ref.1) | copy-start | bytes 1540
  12.0 0.7 %copy-start.7 = (s32[1,1,32]{2,1,0:T(1,128)S(1)}, s32[1,1,32]{2,1,0:T(1,128)}, u32[]{:S(2)}) copy-start(s32[1,1,32]{2,1,0:T(1,128)} %ids_ref.3) | copy-start | bytes 388
  12.0 0.7 %copy-start.8 = (s32[1,128,2]{1,2,0:T(2,128)S(1)}, s32[1,128,2]{1,2,0:T(2,128)}, u32[]{:S(2)}) copy-start(s32[1,128,2]{1,2,0:T(2,128)} %param.18) | copy-start | bytes 3076
  12.7 0.9 %copy-start.4 = (f32[1,32,8,256]{3,2,1,0:T(8,128)S(1)}, f32[1,32,8,256]{3,2,1,0:T(8,128)}, u32[]{:S(2)}) copy-start(f32[1,32,8,256]{3,2,1,0:T(8,128)} %param.10) | copy-start | bytes 786436
  13.6 0.9 %copy-start.5 = (f32[1,32,8,256]{3,2,1,0:T(8,128)S(1)}, f32[1,32,8,256]{3,2,1,0:T(8,128)}, u32[]{:S(2)}) copy-start(f32[1,32,8,256]{3,2,1,0:T(8,128)} %param.12) | copy-start | bytes 786436
  16.0 0.9 %copy-start.6 = (bf16[1,32,8,256]{3,2,1,0:T(8,128)(2,1)S(1)}, bf16[1,32,8,256]{3,2,1,0:T(8,128)(2,1)}, u32[]{:S(2)}) copy-start(bf16[1,32,8,256]{3,2,1,0:T(8,128)(2,1)} %param.14) | copy-start | bytes 393220
  17.7 5.0 %collective-permute-start.6 = (f32[136,128]{1,0:T(8,128)S(1)}, f32[136,128]{1,0:T(8,128)S(1)}, u32[]{:S(2)}, u32[]{:S(2)}) collective-permute-start(f32[136,128]{1,0:T(8,128)S(1)} %get-tuple-element.22), channel_id=1, source_target_pairs={{0,8},{8,0},{16,24},{24,16},{1,9},{9,1},{17,25},{25,17},{2,10},{10... | collective-permute-start | bytes 208904 | tf_op jit(solution)/shard_map/ppermute | solution.py:241
  19.3 5.0 %collective-permute-start.7 = (f32[136,128]{1,0:T(8,128)S(1)}, f32[136,128]{1,0:T(8,128)S(1)}, u32[]{:S(2)}, u32[]{:S(2)}) collective-permute-start(f32[136,128]{1,0:T(8,128)S(1)} %get-tuple-element.23), channel_id=1, source_target_pairs={{0,16},{8,24},{16,0},{24,8},{1,17},{9,25},{17,1},{25,9},{2,18},{10... | collective-permute-start | bytes 208904 | tf_op jit(solution)/shard_map/ppermute | solution.py:241
  20.8 5.2 %collective-permute-start.8 = (f32[136,128]{1,0:T(8,128)S(1)}, f32[136,128]{1,0:T(8,128)S(1)}, u32[]{:S(2)}, u32[]{:S(2)}) collective-permute-start(f32[136,128]{1,0:T(8,128)S(1)} %get-tuple-element.24), channel_id=1, source_target_pairs={{0,24},{8,16},{16,8},{24,0},{1,25},{9,17},{17,9},{25,1},{2,26},{10... | collective-permute-start | bytes 208904 | tf_op jit(solution)/shard_map/ppermute | solution.py:241

commit v3 on v2

v3 whole, which is shorter than its diff:
```python
import functools

import jax
import jax.numpy as jnp
from jax import lax
from jax.experimental import pallas as pl
from jax.experimental.pallas import tpu as pltpu
from jax.sharding import PartitionSpec as P

SURFACE_DEPTH = 8


STENCIL_WEIGHTS = (-205.0 / 72.0, 8.0 / 5.0, -1.0 / 5.0, 8.0 / 315.0, -1.0 / 560.0)
STEP_RATIO = 0.1
REACH = 4

VMEM = pl.BlockSpec(memory_space=pltpu.VMEM)
SMEM = pl.BlockSpec(memory_space=pltpu.SMEM)
HBM = pl.BlockSpec(memory_space=pltpu.HBM)
CHEAP = pl.CostEstimate(flops=0, bytes_accessed=0, transcendentals=0)
PARAMS = pltpu.CompilerParams(vmem_limit_bytes=16 * 1024 * 1024)
F32, BF16 = jnp.float32, jnp.bfloat16


def swaps(axis, other):
    count, others = lax.axis_size(axis), lax.axis_size(other)
    even = [(i, i + 1) for i in range(0, count - 1, 2)]
    odd = [(i, i + 1) for i in range(1, count - 1, 2)]

    def rank(a, o):
        return a * others + o if axis == "tx" else o * count + a

    def ranks(pairs):
        return [(rank(a, o), rank(b, o)) for a, b in pairs for o in range(others)]

    idle = [i for i in range(count) if i not in {end for pair in odd for end in pair}]
    idle = [(rank(i, o), rank(i, o + 1)) for i in idle for o in range(0, others - 1, 2)]
    return [[way for a, b in pairs for way in ((a, b), (b, a))] for pairs in (ranks(even), ranks(odd) + idle)]


def has_odd(axis):
    at = lax.axis_index(axis)
    return jnp.where(at % 2 == 0, at > 0, at < lax.axis_size(axis) - 1)


def halves(value):
    high = value.astype(BF16)
    return high, (value - high.astype(F32)).astype(BF16)


def product(left, right):
    (a, b), (c, d) = left, right

    def dot(x, y):
        return jnp.dot(x, y, preferred_element_type=F32)

    return dot(a, c) + (dot(a, d) + dot(b, c))


def by_distance(gap, stride=1):
    weights = jnp.zeros(gap.shape, F32)
    for offset in range(1, REACH + 1):
        weights = jnp.where(gap == offset * stride, STENCIL_WEIGHTS[offset], weights)
    return weights


def load_kernel(f_hbm, a_hbm, v_hbm, f_ref, a_ref, v_ref, *refs):
    faces, sems = refs[:-1], refs[-1]
    sources, fields = (f_hbm, a_hbm, v_hbm), (f_ref, a_ref, v_ref)
    copies = [pltpu.make_async_copy(src, dst, sems.at[n]) for n, (src, dst) in enumerate(zip(sources, fields))]
    for copy in copies:
        copy.start()
    cells_x, cells_y, cells_z = f_ref.shape
    half = cells_x // 2
    at_even = lax.axis_index("ty") % 2 == 0
    low = (lax.broadcasted_iota(jnp.int32, (half, cells_y, cells_z), 1) < REACH).astype(jnp.int32)
    for field in range(2):
        ref = fields[field]
        copies[field].wait()
        for face, tails in zip(faces, (at_even, jnp.logical_not(at_even))):
            turn = jnp.where(tails, 0, half)
            turned = pltpu.roll(ref[pl.ds(turn, half)], REACH, 1)
            straight = ref[pl.ds(half - turn, half)]
            face[field] = jnp.where(low == tails.astype(jnp.int32), turned, straight)
    copies[2].wait()


def face_kernel(f_ref, a_ref, _, even_ref, odd_ref):
    at_even = lax.axis_index("tx") % 2 == 0
    tail, head = f_ref.shape[0] - REACH, 0
    for field, ref in enumerate((f_ref, a_ref)):
        even_ref[field] = ref[pl.ds(jnp.where(at_even, tail, head), REACH)]
        odd_ref[field] = ref[pl.ds(jnp.where(at_even, head, tail), REACH)]


def inner_kernel(
    owners, slab, strength_ref, source_hbm, receiver_hbm, trace_hbm, ids_hbm, fp_hbm, ap_hbm, fn_ref, an_ref,
    out_ref, rows_ref, blocks_ref, taken_ref, *scratch,
):
    cells_x, cells_y, cells_z = fn_ref.shape
    cells = cells_x * cells_y
    capacity = cells_x // owners
    scratch, sems = scratch[:-1], scratch[-1]
    source_ref, receiver_ref, trace_ref, ids_ref, fp_ref, ap_ref = scratch
    sources = (source_hbm, receiver_hbm, trace_hbm, ids_hbm, fp_hbm, ap_hbm)
    copies = [pltpu.make_async_copy(src, dst, sems.at[n]) for n, (src, dst) in enumerate(zip(sources, scratch))]
    for copy in copies:
        copy.start()
    row = lax.broadcasted_iota(jnp.int32, (cells_z, cells_z), 0)
    col = lax.broadcasted_iota(jnp.int32, (cells_z, cells_z), 1)
    along_z = halves(by_distance(jnp.abs(row - col)))
    row = lax.broadcasted_iota(jnp.int32, (cells, cells), 0)
    col = lax.broadcasted_iota(jnp.int32, (cells, cells), 1)
    gap = jnp.abs(row - col)
    along_y = jnp.where(row // cells_y == col // cells_y, by_distance(gap), 0.0)
    along_xy = halves(along_y + by_distance(gap, cells_y))
    for field, now_ref in enumerate((fn_ref, an_ref)):
        now = now_ref[...].reshape(cells, cells_z)
        parts = halves(now)
        total = product(parts, along_z) + product(along_xy, parts)
        total = total + (3.0 * STENCIL_WEIGHTS[0]) * now
        out_ref[2 + field] = total.reshape(cells_x, cells_y, cells_z)

    for copy in copies[:4]:
        copy.wait()
    start_x = lax.axis_index("tx") * cells_x
    start_y = lax.axis_index("ty") * cells_y
    near_x = receiver_ref[0:1, :] - start_x
    near_y = receiver_ref[1:2, :] - start_y
    cell_x = lax.broadcasted_iota(jnp.int32, (cells_x, cells_y, near_x.shape[1]), 0)
    cell_y = lax.broadcasted_iota(jnp.int32, cell_x.shape, 1)
    hit = jnp.where((cell_x == near_x[None]) & (cell_y == near_y[None]), trace_ref[...][None], 0.0)
    surface = jnp.sum(hit, axis=2, keepdims=True)
    lanes = min(cells_z, 128)
    depth = lax.broadcasted_iota(jnp.int32, (cells_x, cells_y, lanes), 2) == SURFACE_DEPTH
    out_ref[3, :, :, :lanes] = out_ref[3, :, :, :lanes] + jnp.where(depth, surface, 0.0)
    source_x = source_ref[0, 0] - start_x
    source_y = source_ref[0, 1] - start_y

    @pl.when((source_x >= 0) & (source_x < cells_x))
    def _():
        sub = lax.broadcasted_iota(jnp.int32, (cells_y, cells_z), 0)
        lane = lax.broadcasted_iota(jnp.int32, (cells_y, cells_z), 1)
        mark = (sub == source_y) & (lane == SURFACE_DEPTH)
        out_ref[2, source_x] = out_ref[2, source_x] + jnp.where(mark, strength_ref[0], 0.0)

    for owner in range(owners):
        taken_ref[owner] = 0

    def one_row(r, _):
        owner = ids_ref[0, 0, r] // slab
        slot = taken_ref[owner]
        rows_ref[owner * capacity + slot] = r
        blocks_ref[owner * capacity + slot] = ids_ref[0, 0, r] - owner * slab
        taken_ref[owner] = slot + 1
        return 0

    lax.fori_loop(0, cells_x, one_row, 0, unroll=4)
    for field, (copy, prev_ref, now_ref) in enumerate(zip(copies[4:], (fp_ref, ap_ref), (fn_ref, an_ref))):
        copy.wait()
        out_ref[field] = 2.0 * now_ref[...] - prev_ref[...]


def add_edges(state_ref, x_even_ref, x_odd_ref, y_refs, curve_ref):
    _, cells_x, cells_y, cells_z = curve_ref.shape
    half = cells_x // 2
    cells = cells_x * cells_y
    x_at_even = lax.axis_index("tx") % 2 == 0
    y_at_even = lax.axis_index("ty") % 2 == 0
    row = lax.broadcasted_iota(jnp.int32, (cells, half * cells_y), 0)
    col = lax.broadcasted_iota(jnp.int32, (cells, half * cells_y), 1)
    sub = col % cells_y
    same = row // cells_y == col // cells_y + half * (sub // REACH)
    layer, y = sub % REACH, row % cells_y
    after = by_distance(jnp.where(same, cells_y + layer - y, 0))
    before = by_distance(jnp.where(same, y + REACH - layer, 0))
    from_even = halves(jnp.where(y_at_even, after, before))
    from_odd = halves(jnp.where(has_odd("ty"), jnp.where(y_at_even, before, after), 0.0))
    x_has_odd = has_odd("tx")
    for field in range(2):
        curve = state_ref[2 + field].reshape(cells, cells_z)
        for ref, weights in zip(y_refs, (from_even, from_odd)):
            curve = curve + product(weights, halves(ref[field].reshape(half * cells_y, cells_z)))
        curve_ref[field] = curve.reshape(cells_x, cells_y, cells_z)
        x_odd = jnp.where(x_has_odd, x_odd_ref[field], 0.0)
        before_x = jnp.where(x_at_even, x_odd, x_even_ref[field])
        after_x = jnp.where(x_at_even, x_even_ref[field], x_odd)
        for place in range(REACH):
            low = curve_ref[field, place]
            high = curve_ref[field, cells_x - REACH + place]
            for layer in range(REACH):
                if place + REACH - layer <= REACH:
                    low = low + STENCIL_WEIGHTS[place + REACH - layer] * before_x[layer]
                if layer + REACH - place <= REACH:
                    high = high + STENCIL_WEIGHTS[layer + REACH - place] * after_x[layer]
            curve_ref[field, place] = low
            curve_ref[field, cells_x - REACH + place] = high


def courant_kernel(rows_ref, blocks_ref, *refs):
    slabs, out_ref = refs[:-1], refs[-1]
    capacity = out_ref.shape[0] // len(slabs)
    me = lax.axis_index("shot")
    for k, ref in enumerate(slabs):
        for j in range(capacity):
            slot = (me ^ k) * capacity + j
            scaled = ref[blocks_ref[slot]].astype(F32) * STEP_RATIO
            out_ref[rows_ref[slot]] = scaled * scaled


def scale_code(largest):
    least = jnp.maximum(largest, 2.0**-78) * (1.0 / 32752.0)
    exponent = jnp.floor(jnp.log2(least) + 1e-4)
    mantissa = jnp.ceil(least * jnp.exp2(7.0 - exponent))
    code = (exponent.astype(jnp.int32) + 30) * 512 + mantissa.astype(jnp.int32)
    return mantissa * jnp.exp2(exponent - 7.0), code


def scale_of(code):
    exponent = (code >> 9) - 37
    return (code & 511).astype(F32) * jnp.exp2(exponent.astype(F32))


def next_kernel(owners, rows_ref, blocks_ref, courant_ref, state_ref, x_even_ref, x_odd_ref, *refs):
    y_refs, refs = refs[: -owners - 3], refs[-owners - 3 :]
    messages, (f_out_ref, a_out_ref, curve_ref) = refs[:owners], refs[owners:]
    add_edges(state_ref, x_even_ref, x_odd_ref, y_refs, curve_ref)
    cells_x, cells_y, cells_z = f_out_ref.shape
    capacity = cells_x // owners
    lanes = messages[0].shape[1]
    parts = cells_z // lanes
    count = capacity * cells_y
    me = lax.axis_index("shot")
    lane = lax.broadcasted_iota(jnp.int32, (cells_y, lanes), 1) // cells_y
    for k in list(range(1, owners)) + [0]:
        place = jnp.zeros((cells_y, lanes), jnp.int32)
        images = []
        for j in range(capacity):
            slot = (me ^ k) * capacity + j
            r, block = rows_ref[slot], blocks_ref[slot]
            courant = courant_ref[r]
            f_next = state_ref[0, r] + courant * curve_ref[0, r]
            a_next = state_ref[1, r] + courant * curve_ref[1, r]
            f_out_ref[r] = f_next
            a_out_ref[r] = a_next
            images.append(f_next * a_next)
            place = jnp.where(lane == j, block, place)
        image = jnp.concatenate(images, axis=0)
        if k == 0:
            scales = jnp.ones((cells_y, lanes), jnp.int32)
        else:
            scale, code = scale_code(jnp.max(jnp.abs(image), axis=1, keepdims=True))
            image = jnp.round(image * (1.0 / scale)).astype(jnp.int32)
            scales = jnp.zeros((cells_y, lanes), jnp.int32)
            for j in range(capacity):
                scales = jnp.where(lane == j, code[j * cells_y : (j + 1) * cells_y], scales)
        kind = messages[k].dtype
        for part in range(parts):
            messages[k][part * count : (part + 1) * count, :] = image[:, part * lanes : (part + 1) * lanes].astype(kind)
        messages[k][parts * count :, :] = jnp.concatenate([scales, place], axis=0).astype(kind)


def image_kernel(*refs):
    messages, out_ref = refs[:-1], refs[-1]
    slab, cells_y, cells_z = out_ref.shape
    lanes = messages[0].shape[1]
    parts = cells_z // lanes
    count = (messages[0].shape[0] - 2 * cells_y) // parts
    scales, places = [], []
    for k, ref in enumerate(messages):
        tail = ref[parts * count :, :count].astype(jnp.int32)
        scale = scale_of(tail[:cells_y]) if k else jnp.ones((cells_y, count), F32)
        scales.append(scale)
        places.append(tail[cells_y:])
    scales, places = jnp.concatenate(scales, axis=1), jnp.concatenate(places, axis=1)
    shape = (slab,) + places.shape
    block = lax.broadcasted_iota(jnp.int32, shape, 0)
    y = lax.broadcasted_iota(jnp.int32, shape, 1)
    y_of_row = lax.broadcasted_iota(jnp.int32, shape, 2) % cells_y
    chosen = jnp.where((block == places[None]) & (y == y_of_row), scales[None], 0.0)
    chosen = chosen.reshape(slab * cells_y, places.shape[1]).astype(BF16)
    for part in range(parts):
        rows = [ref[part * count : (part + 1) * count, :].astype(F32) for ref in messages]
        high, low = halves(jnp.concatenate(rows, axis=0))
        total = jnp.dot(chosen, high, preferred_element_type=F32) + jnp.dot(chosen, low, preferred_element_type=F32)
        out_ref[:, :, part * lanes : (part + 1) * lanes] = total.reshape(slab, cells_y, lanes)


def in_vmem(value):
    return pltpu.with_memory_space_constraint(value, pltpu.VMEM)


def in_hbm(value):
    return pltpu.with_memory_space_constraint(value, pltpu.HBM)


def in_smem(value):
    return pltpu.with_memory_space_constraint(value, pltpu.SMEM)


def on_device(
    forward_prev,
    forward_now,
    adjoint_prev,
    adjoint_now,
    velocity_model,
    aperture,
    source_cell,
    source_strength,
    receiver_cell,
    receiver_trace,
):
    owners = lax.axis_size("shot")
    count_y = lax.axis_size("ty")
    cells_x, cells_y, cells_z = forward_now.shape[1:]
    slab = velocity_model.shape[1]
    capacity = cells_x // owners

    def peer(value, k):
        return lax.ppermute(value, "shot", [(i, i ^ k) for i in range(owners)])

    slabs = [peer(velocity_model[0], k) for k in range(1, owners)]

    sides = 2 if count_y > 2 else 1
    field = pltpu.VMEM((cells_x, cells_y, cells_z), F32)
    x_face = pltpu.VMEM((2, REACH, cells_y, cells_z), F32)
    y_face = pltpu.VMEM((2, cells_x // 2, cells_y, cells_z), F32)
    forward_now, adjoint_now, own_slab, *faces = pl.pallas_call(
        load_kernel,
        out_shape=(field, field, pltpu.VMEM(velocity_model.shape[1:], BF16)) + (y_face,) * sides,
        in_specs=[HBM] * 3,
        out_specs=(VMEM,) * (3 + sides),
        scratch_shapes=[pltpu.SemaphoreType.DMA((3,))],
        compiler_params=PARAMS,
        cost_estimate=CHEAP,
        name="load_fields",
    )(in_hbm(forward_now[0]), in_hbm(adjoint_now[0]), in_hbm(velocity_model[0]))
    forward_now, adjoint_now = in_vmem(forward_now), in_vmem(adjoint_now)
    slabs = [own_slab] + slabs
    halos = [in_vmem(lax.ppermute(face, ("tx", "ty"), pairs)) for face, pairs in zip(faces, swaps("ty", "tx"))]
    faces = pl.pallas_call(
        face_kernel,
        out_shape=(x_face, x_face),
        in_specs=[VMEM] * 3,
        out_specs=(VMEM, VMEM),
        compiler_params=PARAMS,
        cost_estimate=CHEAP,
        name="faces_along_x",
    )(forward_now, adjoint_now, halos[0])
    x_halos = [lax.ppermute(face, ("tx", "ty"), pairs) for face, pairs in zip(faces, swaps("tx", "ty"))]
    halos = [in_vmem(halo) for halo in x_halos] + halos

    table = pltpu.SMEM((cells_x,), jnp.int32)
    small = [source_cell, receiver_cell[0].T, receiver_trace, aperture]
    state, rows, blocks = pl.pallas_call(
        functools.partial(inner_kernel, owners, slab),
        out_shape=(pltpu.VMEM((4, cells_x, cells_y, cells_z), F32), table, table),
        in_specs=[SMEM] + [HBM] * 6 + [VMEM] * 2,
        out_specs=(VMEM, SMEM, SMEM),
        scratch_shapes=[
            pltpu.SMEM((owners,), jnp.int32),
            pltpu.SMEM(source_cell.shape, jnp.int32),
            pltpu.VMEM(small[1].shape, jnp.int32),
            pltpu.VMEM(receiver_trace.shape, F32),
            pltpu.SMEM(aperture.shape, jnp.int32),
            field,
            field,
            pltpu.SemaphoreType.DMA((6,)),
        ],
        compiler_params=PARAMS,
        cost_estimate=CHEAP,
        name="inner_cells",
    )(source_strength, *[in_hbm(value) for value in small + [forward_prev[0], adjoint_prev[0]]], forward_now, adjoint_now)
    rows, blocks = in_smem(rows), in_smem(blocks)
    courant = pl.pallas_call(
        courant_kernel,
        out_shape=field,
        in_specs=[SMEM] * 2 + [VMEM] * owners,
        out_specs=VMEM,
        compiler_params=PARAMS,
        cost_estimate=CHEAP,
        name="courant_rows",
    )(rows, blocks, *[in_vmem(block) for block in slabs])

    lanes = min(cells_z, 128)
    message = ((cells_z // lanes) * capacity * cells_y + 2 * cells_y, lanes)
    results = pl.pallas_call(
        functools.partial(next_kernel, owners),
        out_shape=(pltpu.VMEM(message, F32),) + (pltpu.VMEM(message, jnp.int16),) * (owners - 1) + (field, field),
        in_specs=[SMEM] * 2 + [VMEM] * (2 + len(halos)),
        out_specs=(VMEM,) * (owners + 2),
        scratch_shapes=[pltpu.VMEM((2, cells_x, cells_y, cells_z), F32)],
        compiler_params=PARAMS,
        name="next_cells",
    )(rows, blocks, in_vmem(courant), in_vmem(state), *halos)
    messages, (forward_next, adjoint_next) = results[:owners], results[owners:]
    arrived = [messages[0]] + [peer(rows, k) for k, rows in enumerate(messages[1:], 1)]

    image = pl.pallas_call(
        image_kernel,
        out_shape=jax.ShapeDtypeStruct((slab, cells_y, cells_z), F32),
        in_specs=[VMEM] * owners,
        out_specs=VMEM,
        compiler_params=PARAMS,
        name="image_rows",
    )(*[in_vmem(rows) for rows in arrived])
    return forward_next[None], adjoint_next[None], image[None]


def solution(mesh):
    in_specs = (
        P("shot", "tx", "ty", None),
        P("shot", "tx", "ty", None),
        P("shot", "tx", "ty", None),
        P("shot", "tx", "ty", None),
        P(("tx", "ty"), "shot", None, None),
        P("shot", ("tx", "ty"), None),
        P("shot", None),
        P("shot"),
        P("shot", None, None),
        P("shot", None),
    )
    out_specs = (
        P("shot", "tx", "ty", None),
        P("shot", "tx", "ty", None),
        P(("tx", "ty"), "shot", None, None),
    )
    return jax.shard_map(
        on_device, mesh=mesh, in_specs=in_specs, out_specs=out_specs, check_vma=False
    )
```

time: 27.4 us -> 21.9 us (0.80)
  the two profiles are of different devices: /device:TPU:8 before, /device:TPU:0 now
where the time goes in v3:
time: 21.9 us; the launch traced here: 21.8 us
  starting transfers between devices  10.3 us (47%)
  waiting for transfers between devices  4.49 us (21%)
  Pallas kernels  4.24 us (19%)
  local copies, waits for them, and re-layouts  1.41 us (6%)
  between operations  1.35 us (6%)
    ppermute x6, starting transfers between devices, peer(): return lax.ppermute(value, 'shot', [(i, i ^ k) for i in range(owners)])  7.72 us
    ppermute x6, waiting for transfers between devices, peer(): return lax.ppermute(value, 'shot', [(i, i ^ k) for i in range(owners)])  4.48 us
    ppermute x3, starting transfers between devices, on_device(): lax.ppermute(face, ('tx', 'ty'), pairs)  2.56 us
    unnamed x4, local copies, waits for them, and re-layouts  1.41 us
    pallas_call x1, Pallas kernels, on_device(): pl.pallas_call(functools.partial(inner_kernel, owners, slab), out_shape=(...  1.33 us
    pallas_call x1, Pallas kernels, on_device(): pl.pallas_call(load_kernel, out_shape=(field, field, pltpu.VMEM(velocity_...  1.12 us
    pallas_call x1, Pallas kernels, on_device(): pl.pallas_call(image_kernel, out_shape=jax.ShapeDtypeStruct((slab, cells_...  1.06 us
    pallas_call x1, Pallas kernels, on_device(): pl.pallas_call(functools.partial(next_kernel, owners), out_shape=(pltpu.V...  0.67 us
  transfers between devices with their start and end apart: 9, of which 4 were waited for; matrix products, arithmetic and copies ran while one was open for 6% of the time, Pallas kernels for 6%

profile of v3, /device:TPU:0, one launch (start us, length us, event | category | flops | bytes accessed | tf_op | source)
XLA Modules:
  0.0 21.8 jit_solution(3556663622229407532)
XLA Ops:
  0.6 0.0 copy-start
  0.6 1.1 %load_fields.1 = (f32[32,8,256]{2,1,0:T(8,128)S(1)}, f32[32,8,256]{2,1,0:T(8,128)S(1)}, bf16[32,8,256]{2,1,0:T(8,128)(2,1)S(1)}, f32[2,16,8,256]{3,2,1,0:T(8,128)S(1)}) custom-call(f32[32,8,256]{2,1,0:T(8,128)} %bitcast.16, f32[32,8,256]{2,1,0:T(8,128)} %bitcast.17, bf16[32,8,256]{2,1,0:T(8,128)(2,1)} %bitcast.18), custom_call_target="tpu_custom_call" | custom-call | tf_op jit(solution)/shard_map/load_fields/pallas_call | solution.py:328
  1.8 0.5 %collective-permute-start.3 = (f32[2,16,8,256]{3,2,1,0:T(8,128)S(1)}, f32[2,16,8,256]{3,2,1,0:T(8,128)S(1)}, u32[]{:S(2)}, u32[]{:S(2)}) collective-permute-start(f32[2,16,8,256]{3,2,1,0:T(8,128)S(1)} %get-tuple-element.24), channel_id=1, source_target_pairs={{0,1},{1,0},{2,3},{3,2},{4,5},{5,4},{6,7},{7,6},{8,9},{9,8},{10,11... | collective-permute-start | bytes 786440 | tf_op jit(solution)/shard_map/ppermute | solution.py:340
  2.3 0.0 copy-done
  2.3 3.5 %collective-permute-start.2 = (bf16[32,8,256]{2,1,0:T(8,128)(2,1)S(1)}, bf16[32,8,256]{2,1,0:T(8,128)(2,1)S(1)}, u32[]{:S(2)}, u32[]{:S(2)}) collective-permute-start(bf16[32,8,256]{2,1,0:T(8,128)(2,1)S(1)} %bitcast.19), channel_id=1, source_target_pairs={{0,24},{8,16},{16,8},{24,0},{1,25},{9,17},{17,9},{25,1},{2,26},{10... | collective-permute-start | bytes 393224 | tf_op jit(solution)/shard_map/ppermute | solution.py:320
  5.8 0.5 %collective-permute-start.1 = (bf16[32,8,256]{2,1,0:T(8,128)(2,1)S(1)}, bf16[32,8,256]{2,1,0:T(8,128)(2,1)S(1)}, u32[]{:S(2)}, u32[]{:S(2)}) collective-permute-start(bf16[32,8,256]{2,1,0:T(8,128)(2,1)S(1)} %bitcast.20), channel_id=1, source_target_pairs={{0,16},{8,24},{16,0},{24,8},{1,17},{9,25},{17,1},{25,9},{2,18},{10... | collective-permute-start | bytes 393224 | tf_op jit(solution)/shard_map/ppermute | solution.py:320
  6.3 0.1 collective-permute-start
  6.5 0.0 collective-permute-done.3._.refs_0_
  6.5 2.0 %collective-permute-start.4 = (f32[2,4,8,256]{3,2,1,0:T(8,128)S(1)}, f32[2,4,8,256]{3,2,1,0:T(8,128)S(1)}, u32[]{:S(2)}, u32[]{:S(2)}) collective-permute-start(f32[2,4,8,256]{3,2,1,0:T(8,128)S(1)} %get-tuple-element.25), channel_id=1, source_target_pairs={{0,2},{2,0},{1,3},{3,1},{4,6},{6,4},{5,7},{7,5},{8,10},{10,8},{9,1... | collective-permute-start | bytes 196616 | tf_op jit(solution)/shard_map/ppermute | solution.py:350
  8.5 0.0 collective-permute-start.5
  9.2 1.3 %inner_cells.1 = (f32[4,32,8,256]{3,2,1,0:T(8,128)S(1)}, s32[32]{0:T(128)S(4)}, s32[32]{0:T(128)S(4)}) custom-call(f32[1]{0:T(128)S(6)} %copy.15.strength_ref, s32[1,2]{1,0:T(1,128)} %source_hbm.1, s32[2,128]{1,0:T(2,128)} %bitcast.22, f32[1,128]{1,0:T(1,128)} %trace_hbm.1, s32[1,1,32]{2,1,0:T(1,128)} %ids_hbm.1, f32[32,8,256]{2,1,0:T(8,128)} %bitcast.13, ...), custom_call_target="tpu_custom_call" | custom-call | tf_op jit(solution)/shard_map/inner_cells/pallas_call | solution.py:355
  10.5 0.0 collective-permute-done.2.refs_3_
  10.5 2.2 %collective-permute-done.1.refs_2_ = bf16[32,8,256]{2,1,0:T(8,128)(2,1)S(1)} collective-permute-done((bf16[32,8,256]{2,1,0:T(8,128)(2,1)S(1)}, bf16[32,8,256]{2,1,0:T(8,128)(2,1)S(1)}, u32[]{:S(2)}, u32[]{:S(2)}) %collective-permute-start.1) | collective-permute-done | bytes 131104 | tf_op jit(solution)/shard_map/ppermute | solution.py:320
  12.7 0.3 %collective-permute-done.refs_1_ = bf16[32,8,256]{2,1,0:T(8,128)(2,1)S(1)} collective-permute-done((bf16[32,8,256]{2,1,0:T(8,128)(2,1)S(1)}, bf16[32,8,256]{2,1,0:T(8,128)(2,1)S(1)}, u32[]{:S(2)}, u32[]{:S(2)}) %collective-permute-start) | collective-permute-done | bytes 131104 | tf_op jit(solution)/shard_map/ppermute | solution.py:320
  13.0 0.1 courant_rows.1.courant_ref
  13.1 0.0 collective-permute-done.4.x_even_ref
  13.1 0.0 collective-permute-done.5.x_odd_ref
  13.1 0.7 %next_cells.1 = (f32[144,128]{1,0:T(8,128)S(1)}, s16[144,128]{1,0:T(8,128)(2,1)S(1)}, s16[144,128]{1,0:T(8,128)(2,1)S(1)}, s16[144,128]{1,0:T(8,128)(2,1)S(1)}, ...) custom-call(s32[32]{0:T(128)S(4)} %get-tuple-element.20.rows_ref, s32[32]{0:T(128)S(4)} %get-tuple-element.21.blocks_ref, ...), custom_call_target="tpu_custom_call" | custom-call | tf_op jit(solution)/shard_map/next_cells/pallas_call | solution.py:387
  13.8 1.6 %collective-permute-start.6 = (s16[144,128]{1,0:T(8,128)(2,1)S(1)}, s16[144,128]{1,0:T(8,128)(2,1)S(1)}, u32[]{:S(2)}, u32[]{:S(2)}) collective-permute-start(s16[144,128]{1,0:T(8,128)(2,1)S(1)} %get-tuple-element.30), channel_id=1, source_target_pairs={{0,8},{8,0},{16,24},{24,16},{1,9},{9,1},{17,25},{25,17},{2,10},{10... | collective-permute-start | bytes 110600 | tf_op jit(solution)/shard_map/ppermute | solution.py:320
  15.3 0.5 %collective-permute-start.7 = (s16[144,128]{1,0:T(8,128)(2,1)S(1)}, s16[144,128]{1,0:T(8,128)(2,1)S(1)}, u32[]{:S(2)}, u32[]{:S(2)}) collective-permute-start(s16[144,128]{1,0:T(8,128)(2,1)S(1)} %get-tuple-element.31), channel_id=1, source_target_pairs={{0,16},{8,24},{16,0},{24,8},{1,17},{9,25},{17,1},{25,9},{2,18},{10... | collective-permute-start | bytes 110600 | tf_op jit(solution)/shard_map/ppermute | solution.py:320
  15.9 1.5 %collective-permute-start.8 = (s16[144,128]{1,0:T(8,128)(2,1)S(1)}, s16[144,128]{1,0:T(8,128)(2,1)S(1)}, u32[]{:S(2)}, u32[]{:S(2)}) collective-permute-start(s16[144,128]{1,0:T(8,128)(2,1)S(1)} %get-tuple-element.32), channel_id=1, source_target_pairs={{0,24},{8,16},{16,8},{24,0},{1,25},{9,17},{17,9},{25,1},{2,26},{10... | collective-permute-start | bytes 110600 | tf_op jit(solution)/shard_map/ppermute | solution.py:320
  17.3 0.7 %copy.13 = f32[1,32,8,256]{3,2,1,0:T(8,128)} copy(f32[1,32,8,256]{3,2,1,0:T(8,128)S(1)} %bitcast.12) | data formatting | bytes 524288
  18.0 0.7 %copy.14 = f32[1,32,8,256]{3,2,1,0:T(8,128)} copy(f32[1,32,8,256]{3,2,1,0:T(8,128)S(1)} %bitcast.11) | data formatting | bytes 524288
  18.7 0.0 collective-permute-done.6.refs_1_
  18.7 0.7 %collective-permute-done.7.refs_2_ = s16[144,128]{1,0:T(8,128)(2,1)S(1)} collective-permute-done((s16[144,128]{1,0:T(8,128)(2,1)S(1)}, s16[144,128]{1,0:T(8,128)(2,1)S(1)}, u32[]{:S(2)}, u32[]{:S(2)}) %collective-permute-start.7) | collective-permute-done | bytes 36896 | tf_op jit(solution)/shard_map/ppermute | solution.py:320
  19.5 1.3 %collective-permute-done.8.refs_3_ = s16[144,128]{1,0:T(8,128)(2,1)S(1)} collective-permute-done((s16[144,128]{1,0:T(8,128)(2,1)S(1)}, s16[144,128]{1,0:T(8,128)(2,1)S(1)}, u32[]{:S(2)}, u32[]{:S(2)}) %collective-permute-start.8) | collective-permute-done | bytes 36896 | tf_op jit(solution)/shard_map/ppermute | solution.py:320
  20.7 1.1 %image_rows.1 = f32[32,8,256]{2,1,0:T(8,128)} custom-call(f32[144,128]{1,0:T(8,128)S(1)} %get-tuple-element.29.refs_0_, s16[144,128]{1,0:T(8,128)(2,1)S(1)} %collective-permute-done.6.refs_1_, s16[144,128]{1,0:T(8,128)(2,1)S(1)} %collective-permute-done.7.refs_2_, s16[144,128]{1,0:T(8,128)(2,1)S(1)} %collective-permute-done.8.refs_3_), custom_call_target="tpu_custom_call" | custom-call | tf_op jit(solution)/shard_map/image_rows/pallas_call | solution.py:399
  (1 shorter events, 0.0 us)
Async XLA Ops:
  0.6 1.7 %copy-start = (bf16[1,32,8,256]{3,2,1,0:T(8,128)(2,1)S(1)}, bf16[1,32,8,256]{3,2,1,0:T(8,128)(2,1)}, u32[]{:S(2)}) copy-start(bf16[1,32,8,256]{3,2,1,0:T(8,128)(2,1)} %param.14) | copy-start | bytes 393220
  1.8 4.7 %collective-permute-start.3 = (f32[2,16,8,256]{3,2,1,0:T(8,128)S(1)}, f32[2,16,8,256]{3,2,1,0:T(8,128)S(1)}, u32[]{:S(2)}, u32[]{:S(2)}) collective-permute-start(f32[2,16,8,256]{3,2,1,0:T(8,128)S(1)} %get-tuple-element.24), channel_id=1, source_target_pairs={{0,1},{1,0},{2,3},{3,2},{4,5},{5,4},{6,7},{7,6},{8,9},{9,8},{10,11... | collective-permute-start | bytes 786440 | tf_op jit(solution)/shard_map/ppermute | solution.py:340
  2.3 8.2 %collective-permute-start.2 = (bf16[32,8,256]{2,1,0:T(8,128)(2,1)S(1)}, bf16[32,8,256]{2,1,0:T(8,128)(2,1)S(1)}, u32[]{:S(2)}, u32[]{:S(2)}) collective-permute-start(bf16[32,8,256]{2,1,0:T(8,128)(2,1)S(1)} %bitcast.19), channel_id=1, source_target_pairs={{0,24},{8,16},{16,8},{24,0},{1,25},{9,17},{17,9},{25,1},{2,26},{10... | collective-permute-start | bytes 393224 | tf_op jit(solution)/shard_map/ppermute | solution.py:320
  5.8 6.9 %collective-permute-start.1 = (bf16[32,8,256]{2,1,0:T(8,128)(2,1)S(1)}, bf16[32,8,256]{2,1,0:T(8,128)(2,1)S(1)}, u32[]{:S(2)}, u32[]{:S(2)}) collective-permute-start(bf16[32,8,256]{2,1,0:T(8,128)(2,1)S(1)} %bitcast.20), channel_id=1, source_target_pairs={{0,16},{8,24},{16,0},{24,8},{1,17},{9,25},{17,1},{25,9},{2,18},{10... | collective-permute-start | bytes 393224 | tf_op jit(solution)/shard_map/ppermute | solution.py:320
  6.3 6.7 %collective-permute-start = (bf16[32,8,256]{2,1,0:T(8,128)(2,1)S(1)}, bf16[32,8,256]{2,1,0:T(8,128)(2,1)S(1)}, u32[]{:S(2)}, u32[]{:S(2)}) collective-permute-start(bf16[32,8,256]{2,1,0:T(8,128)(2,1)S(1)} %bitcast.21), channel_id=1, source_target_pairs={{0,8},{8,0},{16,24},{24,16},{1,9},{9,1},{17,25},{25,17},{2,10},{10... | collective-permute-start | bytes 393224 | tf_op jit(solution)/shard_map/ppermute | solution.py:320
  6.5 6.6 %collective-permute-start.4 = (f32[2,4,8,256]{3,2,1,0:T(8,128)S(1)}, f32[2,4,8,256]{3,2,1,0:T(8,128)S(1)}, u32[]{:S(2)}, u32[]{:S(2)}) collective-permute-start(f32[2,4,8,256]{3,2,1,0:T(8,128)S(1)} %get-tuple-element.25), channel_id=1, source_target_pairs={{0,2},{2,0},{1,3},{3,1},{4,6},{6,4},{5,7},{7,5},{8,10},{10,8},{9,1... | collective-permute-start | bytes 196616 | tf_op jit(solution)/shard_map/ppermute | solution.py:350
  8.5 4.6 %collective-permute-start.5 = (f32[2,4,8,256]{3,2,1,0:T(8,128)S(1)}, f32[2,4,8,256]{3,2,1,0:T(8,128)S(1)}, u32[]{:S(2)}, u32[]{:S(2)}) collective-permute-start(f32[2,4,8,256]{3,2,1,0:T(8,128)S(1)} %get-tuple-element.26), channel_id=1, source_target_pairs={{2,4},{4,2},{3,5},{5,3},{0,1},{1,0},{6,7},{7,6},{10,12},{12,10},{1... | collective-permute-start | bytes 196616 | tf_op jit(solution)/shard_map/ppermute | solution.py:350
  13.8 5.0 %collective-permute-start.6 = (s16[144,128]{1,0:T(8,128)(2,1)S(1)}, s16[144,128]{1,0:T(8,128)(2,1)S(1)}, u32[]{:S(2)}, u32[]{:S(2)}) collective-permute-start(s16[144,128]{1,0:T(8,128)(2,1)S(1)} %get-tuple-element.30), channel_id=1, source_target_pairs={{0,8},{8,0},{16,24},{24,16},{1,9},{9,1},{17,25},{25,17},{2,10},{10... | collective-permute-start | bytes 110600 | tf_op jit(solution)/shard_map/ppermute | solution.py:320
  15.3 4.1 %collective-permute-start.7 = (s16[144,128]{1,0:T(8,128)(2,1)S(1)}, s16[144,128]{1,0:T(8,128)(2,1)S(1)}, u32[]{:S(2)}, u32[]{:S(2)}) collective-permute-start(s16[144,128]{1,0:T(8,128)(2,1)S(1)} %get-tuple-element.31), channel_id=1, source_target_pairs={{0,16},{8,24},{16,0},{24,8},{1,17},{9,25},{17,1},{25,9},{2,18},{10... | collective-permute-start | bytes 110600 | tf_op jit(solution)/shard_map/ppermute | solution.py:320
  15.9 4.9 %collective-permute-start.8 = (s16[144,128]{1,0:T(8,128)(2,1)S(1)}, s16[144,128]{1,0:T(8,128)(2,1)S(1)}, u32[]{:S(2)}, u32[]{:S(2)}) collective-permute-start(s16[144,128]{1,0:T(8,128)(2,1)S(1)} %get-tuple-element.32), channel_id=1, source_target_pairs={{0,24},{8,16},{16,8},{24,0},{1,25},{9,17},{17,9},{25,1},{2,26},{10... | collective-permute-start | bytes 110600 | tf_op jit(solution)/shard_map/ppermute | solution.py:320

commit v4 on v3

v4 whole, which is shorter than its diff:
```python
import functools

import jax
import jax.numpy as jnp
from jax import lax
from jax.experimental import pallas as pl
from jax.experimental.pallas import tpu as pltpu
from jax.sharding import PartitionSpec as P

SURFACE_DEPTH = 8


STENCIL_WEIGHTS = (-205.0 / 72.0, 8.0 / 5.0, -1.0 / 5.0, 8.0 / 315.0, -1.0 / 560.0)
STEP_RATIO = 0.1
REACH = 4

VMEM = pl.BlockSpec(memory_space=pltpu.VMEM)
SMEM = pl.BlockSpec(memory_space=pltpu.SMEM)
HBM = pl.BlockSpec(memory_space=pltpu.HBM)
CHEAP = pl.CostEstimate(flops=0, bytes_accessed=0, transcendentals=0)
LONG = pl.CostEstimate(flops=0, bytes_accessed=60000000, transcendentals=0)
HEAVY = pl.CostEstimate(flops=10**10, bytes_accessed=10**8, transcendentals=10**8)
PARAMS = pltpu.CompilerParams(vmem_limit_bytes=16 * 1024 * 1024)
F32, BF16 = jnp.float32, jnp.bfloat16


def swaps(axis, other):
    count, others = lax.axis_size(axis), lax.axis_size(other)
    even = [(i, i + 1) for i in range(0, count - 1, 2)]
    odd = [(i, i + 1) for i in range(1, count - 1, 2)]

    def rank(a, o):
        return a * others + o if axis == "tx" else o * count + a

    def ranks(pairs):
        return [(rank(a, o), rank(b, o)) for a, b in pairs for o in range(others)]

    idle = [i for i in range(count) if i not in {end for pair in odd for end in pair}]
    idle = [(rank(i, o), rank(i, o + 1)) for i in idle for o in range(0, others - 1, 2)]
    return [[way for a, b in pairs for way in ((a, b), (b, a))] for pairs in (ranks(even), ranks(odd) + idle)]


def has_odd(axis):
    at = lax.axis_index(axis)
    return jnp.where(at % 2 == 0, at > 0, at < lax.axis_size(axis) - 1)


def halves(value):
    high = value.astype(BF16)
    return high, (value - high.astype(F32)).astype(BF16)


def product(left, right):
    (a, b), (c, d) = left, right

    def dot(x, y):
        return jnp.dot(x, y, preferred_element_type=F32)

    return dot(a, c) + (dot(a, d) + dot(b, c))


def by_distance(gap, stride=1):
    weights = jnp.zeros(gap.shape, F32)
    for offset in range(1, REACH + 1):
        weights = jnp.where(gap == offset * stride, STENCIL_WEIGHTS[offset], weights)
    return weights


def load_kernel(owners, slab, f_hbm, a_hbm, v_hbm, source_hbm, receiver_hbm, trace_hbm, ids_hbm, *refs):
    results, (ids_ref, taken_ref, sems) = refs[:-3], refs[-3:]
    f_ref, a_ref, v_ref, source_ref, receiver_ref, trace_ref, along_z_ref, along_xy_ref = results[:8]
    from_y_ref, rows_ref, blocks_ref = results[8:11]
    faces = results[11:]
    pairs = [(ids_hbm, ids_ref), (f_hbm, f_ref), (a_hbm, a_ref), (v_hbm, v_ref)]
    pairs += [(source_hbm, source_ref), (receiver_hbm, receiver_ref), (trace_hbm, trace_ref)]
    copies = [pltpu.make_async_copy(src, dst, sems.at[n]) for n, (src, dst) in enumerate(pairs)]
    for copy in copies:
        copy.start()
    cells_x, cells_y, cells_z = f_ref.shape
    cells = cells_x * cells_y
    capacity = cells_x // owners
    half = cells_x // 2
    row = lax.broadcasted_iota(jnp.int32, (cells_z, cells_z), 0)
    col = lax.broadcasted_iota(jnp.int32, (cells_z, cells_z), 1)
    along_z_ref[0], along_z_ref[1] = halves(by_distance(jnp.abs(row - col)))
    row = lax.broadcasted_iota(jnp.int32, (cells, cells), 0)
    col = lax.broadcasted_iota(jnp.int32, (cells, cells), 1)
    gap = jnp.abs(row - col)
    along_y = jnp.where(row // cells_y == col // cells_y, by_distance(gap), 0.0)
    along_xy_ref[0], along_xy_ref[1] = halves(along_y + by_distance(gap, cells_y))
    at_even = lax.axis_index("ty") % 2 == 0
    row = lax.broadcasted_iota(jnp.int32, (cells, half * cells_y), 0)
    col = lax.broadcasted_iota(jnp.int32, (cells, half * cells_y), 1)
    sub = col % cells_y
    same = row // cells_y == col // cells_y + half * (sub // REACH)
    layer, y = sub % REACH, row % cells_y
    after, before = cells_y + layer - y, y + REACH - layer
    from_y_ref[0], from_y_ref[1] = halves(by_distance(jnp.where(same, jnp.where(at_even, after, before), 0)))
    if len(faces) > 1:
        same &= has_odd("ty")
        from_y_ref[2], from_y_ref[3] = halves(by_distance(jnp.where(same, jnp.where(at_even, before, after), 0)))

    copies[0].wait()
    for owner in range(owners):
        taken_ref[owner] = 0

    def one_row(r, _):
        owner = ids_ref[0, 0, r] // slab
        slot = taken_ref[owner]
        rows_ref[owner * capacity + slot] = r
        blocks_ref[owner * capacity + slot] = ids_ref[0, 0, r] - owner * slab
        taken_ref[owner] = slot + 1
        return 0

    lax.fori_loop(0, cells_x, one_row, 0, unroll=4)
    low = (lax.broadcasted_iota(jnp.int32, (half, cells_y, cells_z), 1) < REACH).astype(jnp.int32)
    for field, ref in enumerate((f_ref, a_ref)):
        copies[1 + field].wait()
        for face, tails in zip(faces, (at_even, jnp.logical_not(at_even))):
            turn = jnp.where(tails, 0, half)
            turned = pltpu.roll(ref[pl.ds(turn, half)], REACH, 1)
            straight = ref[pl.ds(half - turn, half)]
            face[field] = jnp.where(low == tails.astype(jnp.int32), turned, straight).astype(BF16)
    for copy in copies[3:]:
        copy.wait()


def face_kernel(f_ref, a_ref, _, even_ref, odd_ref):
    at_even = lax.axis_index("tx") % 2 == 0
    tail, head = f_ref.shape[0] - REACH, 0
    for field, ref in enumerate((f_ref, a_ref)):
        even_ref[field] = ref[pl.ds(jnp.where(at_even, tail, head), REACH)].astype(BF16)
        odd_ref[field] = ref[pl.ds(jnp.where(at_even, head, tail), REACH)].astype(BF16)


def inner_kernel(
    strength_ref, source_ref, receiver_ref, trace_ref, along_z_ref, along_xy_ref, from_y_ref,
    fp_ref, ap_ref, fn_ref, an_ref, *refs,
):
    faces, out_ref = refs[:-1], refs[-1]
    cells_x, cells_y, cells_z = fn_ref.shape
    cells = cells_x * cells_y
    along_z = (along_z_ref[0], along_z_ref[1])
    along_xy = (along_xy_ref[0], along_xy_ref[1])
    for field, (prev_ref, now_ref) in enumerate(((fp_ref, fn_ref), (ap_ref, an_ref))):
        now = now_ref[...].reshape(cells, cells_z)
        parts = halves(now)
        total = product(parts, along_z) + product(along_xy, parts)
        total = total + (3.0 * STENCIL_WEIGHTS[0]) * now
        for side, ref in enumerate(faces):
            face = ref[field].astype(F32).reshape(cells // 2, cells_z).astype(BF16)
            for part in range(2):
                total = total + jnp.dot(from_y_ref[2 * side + part], face, preferred_element_type=F32)
        out_ref[2 + field] = total.reshape(cells_x, cells_y, cells_z)
        out_ref[field] = 2.0 * now_ref[...] - prev_ref[...]

    start_x = lax.axis_index("tx") * cells_x
    start_y = lax.axis_index("ty") * cells_y
    near_x = receiver_ref[0:1, :] - start_x
    near_y = receiver_ref[1:2, :] - start_y
    cell_x = lax.broadcasted_iota(jnp.int32, (cells_x, cells_y, near_x.shape[1]), 0)
    cell_y = lax.broadcasted_iota(jnp.int32, cell_x.shape, 1)
    hit = jnp.where((cell_x == near_x[None]) & (cell_y == near_y[None]), trace_ref[...][None], 0.0)
    surface = jnp.sum(hit, axis=2, keepdims=True)
    lanes = min(cells_z, 128)
    depth = lax.broadcasted_iota(jnp.int32, (cells_x, cells_y, lanes), 2) == SURFACE_DEPTH
    out_ref[3, :, :, :lanes] = out_ref[3, :, :, :lanes] + jnp.where(depth, surface, 0.0)
    source_x = source_ref[0, 0] - start_x
    source_y = source_ref[0, 1] - start_y

    @pl.when((source_x >= 0) & (source_x < cells_x))
    def _():
        sub = lax.broadcasted_iota(jnp.int32, (cells_y, cells_z), 0)
        lane = lax.broadcasted_iota(jnp.int32, (cells_y, cells_z), 1)
        mark = (sub == source_y) & (lane == SURFACE_DEPTH)
        out_ref[2, source_x] = out_ref[2, source_x] + jnp.where(mark, strength_ref[...], 0.0)


def edge_kernel(_, x_even_ref, x_odd_ref, state_ref):
    cells_x = state_ref.shape[1]
    at_even = lax.axis_index("tx") % 2 == 0
    for field in range(2):
        x_even = x_even_ref[field].astype(F32)
        x_odd = jnp.where(has_odd("tx"), x_odd_ref[field].astype(F32), 0.0)
        before_x = jnp.where(at_even, x_odd, x_even)
        after_x = jnp.where(at_even, x_even, x_odd)
        for place in range(REACH):
            low = state_ref[2 + field, place]
            high = state_ref[2 + field, cells_x - REACH + place]
            for layer in range(REACH):
                if place + REACH - layer <= REACH:
                    low = low + STENCIL_WEIGHTS[place + REACH - layer] * before_x[layer]
                if layer + REACH - place <= REACH:
                    high = high + STENCIL_WEIGHTS[layer + REACH - place] * after_x[layer]
            state_ref[2 + field, place] = low
            state_ref[2 + field, cells_x - REACH + place] = high


def scale_code(largest):
    least = jnp.maximum(largest, 2.0**-78) * (1.0 / 32752.0)
    exponent = jnp.floor(jnp.log2(least) + 1e-4)
    mantissa = jnp.ceil(least * jnp.exp2(7.0 - exponent))
    code = (exponent.astype(jnp.int32) + 30) * 512 + mantissa.astype(jnp.int32)
    return mantissa * jnp.exp2(exponent - 7.0), code


def scale_of(code):
    exponent = (code >> 9) - 37
    return (code & 511).astype(F32) * jnp.exp2(exponent.astype(F32))


def next_row(slot, rows_ref, blocks_ref, state_ref, slab_ref):
    r, block = rows_ref[slot], blocks_ref[slot]
    scaled = slab_ref[block].astype(F32) * STEP_RATIO
    courant = scaled * scaled
    f_next = state_ref[0, r] + courant * state_ref[2, r]
    a_next = state_ref[1, r] + courant * state_ref[3, r]
    return r, block, f_next, a_next


def send_kernel(k, rows_ref, blocks_ref, state_ref, slab_ref, message_ref, f_ref, a_ref):
    capacity, cells_y, cells_z = f_ref.shape
    lanes = message_ref.shape[1]
    parts = cells_z // lanes
    count = capacity * cells_y
    owner = lax.axis_index("shot") ^ k
    lane = lax.broadcasted_iota(jnp.int32, (cells_y, lanes), 1) // cells_y
    place = jnp.zeros((cells_y, lanes), jnp.int32)
    scales = jnp.zeros((cells_y, lanes), jnp.int32)
    images = []
    for j in range(capacity):
        _, block, f_next, a_next = next_row(owner * capacity + j, rows_ref, blocks_ref, state_ref, slab_ref)
        f_ref[j] = f_next
        a_ref[j] = a_next
        images.append(f_next * a_next)
        place = jnp.where(lane == j, block, place)
    image = jnp.concatenate(images, axis=0)
    scale, code = scale_code(jnp.max(jnp.abs(image), axis=1, keepdims=True))
    image = jnp.round(image * (1.0 / scale)).astype(jnp.int32)
    for j in range(capacity):
        scales = jnp.where(lane == j, code[j * cells_y : (j + 1) * cells_y], scales)
    for part in range(parts):
        columns = image[:, part * lanes : (part + 1) * lanes]
        message_ref[part * count : (part + 1) * count, :] = columns.astype(jnp.int16)
    message_ref[parts * count :, :] = jnp.concatenate([scales, place], axis=0).astype(jnp.int16)


def output_kernel(owners, rows_ref, blocks_ref, state_ref, slab_ref, *refs):
    others, (f_out_ref, a_out_ref, image_ref, place_ref) = refs[:-4], refs[-4:]
    cells_x, cells_y, cells_z = f_out_ref.shape
    capacity = cells_x // owners
    me = lax.axis_index("shot")
    lane = lax.broadcasted_iota(jnp.int32, place_ref.shape, 1) // cells_y
    place = jnp.zeros(place_ref.shape, jnp.int32)
    for j in range(capacity):
        r, block, f_next, a_next = next_row(me * capacity + j, rows_ref, blocks_ref, state_ref, slab_ref)
        f_out_ref[r] = f_next
        a_out_ref[r] = a_next
        image_ref[j] = f_next * a_next
        place = jnp.where(lane == j, block, place)
    place_ref[...] = place
    for n, k in enumerate(range(1, owners)):
        for j in range(capacity):
            r = rows_ref[(me ^ k) * capacity + j]
            f_out_ref[r] = others[2 * n][j]
            a_out_ref[r] = others[2 * n + 1][j]


def image_kernel(own_ref, own_place_ref, *refs):
    messages, (out_hbm, out_ref, sems) = refs[:-3], refs[-3:]
    slab, cells_y, cells_z = out_ref.shape
    lanes = messages[0].shape[1]
    parts = cells_z // lanes
    count = own_ref.shape[0] * cells_y
    scales, places = [jnp.ones((cells_y, count), F32)], [own_place_ref[:, :count]]
    for ref in messages:
        tail = ref[parts * count :, :count].astype(jnp.int32)
        scales.append(scale_of(tail[:cells_y]))
        places.append(tail[cells_y:])
    scales, places = jnp.concatenate(scales, axis=1), jnp.concatenate(places, axis=1)
    shape = (slab,) + places.shape
    block = lax.broadcasted_iota(jnp.int32, shape, 0)
    y = lax.broadcasted_iota(jnp.int32, shape, 1)
    y_of_row = lax.broadcasted_iota(jnp.int32, shape, 2) % cells_y
    chosen = jnp.where((block == places[None]) & (y == y_of_row), scales[None], 0.0)
    chosen = chosen.reshape(slab * cells_y, places.shape[1]).astype(BF16)
    rows = [own_ref[...].reshape(count, cells_z)]
    for ref in messages:
        columns = [ref[part * count : (part + 1) * count, :] for part in range(parts)]
        rows.append(jnp.concatenate(columns, axis=1).astype(F32))
    high, low = halves(jnp.concatenate(rows, axis=0))
    half = slab // 2
    copies = []
    for n in range(2):
        some = chosen[n * half * cells_y : (n + 1) * half * cells_y]
        total = jnp.dot(some, high, preferred_element_type=F32) + jnp.dot(some, low, preferred_element_type=F32)
        blocks = pl.ds(n * half, half)
        out_ref[blocks] = total.reshape(half, cells_y, cells_z)
        copies.append(pltpu.make_async_copy(out_ref.at[blocks], out_hbm.at[blocks], sems.at[n]))
        copies[n].start()
    for copy in copies:
        copy.wait()


def in_vmem(value):
    return pltpu.with_memory_space_constraint(value, pltpu.VMEM)


def in_hbm(value):
    return pltpu.with_memory_space_constraint(value, pltpu.HBM)


def in_smem(value):
    return pltpu.with_memory_space_constraint(value, pltpu.SMEM)


def on_device(
    forward_prev,
    forward_now,
    adjoint_prev,
    adjoint_now,
    velocity_model,
    aperture,
    source_cell,
    source_strength,
    receiver_cell,
    receiver_trace,
):
    owners = lax.axis_size("shot")
    count_y = lax.axis_size("ty")
    cells_x, cells_y, cells_z = forward_now.shape[1:]
    slab = velocity_model.shape[1]
    capacity = cells_x // owners

    def peer(value, k):
        return lax.ppermute(value, "shot", [(i, i ^ k) for i in range(owners)])

    others = list(range(1, owners))
    slabs = {k: peer(velocity_model[0], k) for k in others}

    sides = 2 if count_y > 2 else 1
    field = pltpu.VMEM((cells_x, cells_y, cells_z), F32)
    x_face = pltpu.VMEM((2, REACH, cells_y, cells_z), BF16)
    y_face = pltpu.VMEM((2, cells_x // 2, cells_y, cells_z), BF16)
    table = pltpu.SMEM((cells_x,), jnp.int32)
    sources = [forward_now[0], adjoint_now[0], velocity_model[0]]
    sources += [source_cell, receiver_cell[0].T, receiver_trace, aperture]
    forward_now, adjoint_now, own_slab, source, receiver, trace, along_z, along_xy, from_y, rows, blocks, *faces = (
        pl.pallas_call(
        functools.partial(load_kernel, owners, slab),
        out_shape=(
            field,
            field,
            pltpu.VMEM(velocity_model.shape[1:], BF16),
            pltpu.SMEM(source_cell.shape, jnp.int32),
            pltpu.VMEM(sources[4].shape, jnp.int32),
            pltpu.VMEM(receiver_trace.shape, F32),
            pltpu.VMEM((2, cells_z, cells_z), BF16),
            pltpu.VMEM((2, cells_x * cells_y, cells_x * cells_y), BF16),
            pltpu.VMEM((2 * sides, cells_x * cells_y, cells_x // 2 * cells_y), BF16),
            table,
            table,
        )
        + (y_face,) * sides,
        in_specs=[HBM] * 7,
        out_specs=(VMEM,) * 3 + (SMEM,) + (VMEM,) * 5 + (SMEM,) * 2 + (VMEM,) * sides,
        scratch_shapes=[
            pltpu.SMEM(aperture.shape, jnp.int32),
            pltpu.SMEM((owners,), jnp.int32),
            pltpu.SemaphoreType.DMA((7,)),
        ],
        compiler_params=PARAMS,
        cost_estimate=CHEAP,
        name="load_fields",
    )(*[in_hbm(value) for value in sources])
    )
    forward_now, adjoint_now = in_vmem(forward_now), in_vmem(adjoint_now)
    rows, blocks = in_smem(rows), in_smem(blocks)
    slabs[0] = own_slab
    y_halos = [in_vmem(lax.ppermute(face, ("tx", "ty"), pairs)) for face, pairs in zip(faces, swaps("ty", "tx"))]
    faces = pl.pallas_call(
        face_kernel,
        out_shape=(x_face, x_face),
        in_specs=[VMEM] * 3,
        out_specs=(VMEM, VMEM),
        compiler_params=PARAMS,
        cost_estimate=CHEAP,
        name="faces_along_x",
    )(forward_now, adjoint_now, y_halos[0])
    x_even, x_odd = swaps("tx", "ty")
    from_odd = lax.ppermute(faces[1], ("tx", "ty"), x_odd)
    from_even = lax.ppermute(faces[0], ("tx", "ty"), x_even)

    state = pl.pallas_call(
        inner_kernel,
        out_shape=pltpu.VMEM((4, cells_x, cells_y, cells_z), F32),
        in_specs=[VMEM, SMEM] + [VMEM] * (9 + sides),
        out_specs=VMEM,
        compiler_params=PARAMS,
        cost_estimate=LONG,
        name="inner_cells",
    )(
        source_strength[None],
        in_smem(source),
        in_vmem(receiver),
        in_vmem(trace),
        in_vmem(along_z),
        in_vmem(along_xy),
        in_vmem(from_y),
        forward_prev[0],
        adjoint_prev[0],
        forward_now,
        adjoint_now,
        *y_halos,
    )
    state = in_vmem(
        pl.pallas_call(
            edge_kernel,
            out_shape=pltpu.VMEM(state.shape, F32),
            in_specs=[VMEM] * 3,
            out_specs=VMEM,
            input_output_aliases={0: 0},
            compiler_params=PARAMS,
            cost_estimate=CHEAP,
            name="edge_cells",
        )(in_vmem(state), in_vmem(from_even), in_vmem(from_odd))
    )

    lanes = min(cells_z, 128)
    message = pltpu.VMEM(((cells_z // lanes) * capacity * cells_y + 2 * cells_y, lanes), jnp.int16)
    some_rows = pltpu.VMEM((capacity, cells_y, cells_z), F32)
    arrived, rows_of_others = [], []
    for k in others:
        rows_out, *fields = pl.pallas_call(
            functools.partial(send_kernel, k),
            out_shape=(message, some_rows, some_rows),
            in_specs=[SMEM] * 2 + [VMEM] * 2,
            out_specs=(VMEM,) * 3,
            compiler_params=PARAMS,
            cost_estimate=HEAVY if k == others[-2] else CHEAP,
            name="rows_to_send",
        )(rows, blocks, state, in_vmem(slabs[k]))
        arrived.append(peer(rows_out, k))
        rows_of_others += fields

    whole = jax.ShapeDtypeStruct((cells_x, cells_y, cells_z), F32)
    forward_next, adjoint_next, own_image, own_place = pl.pallas_call(
        functools.partial(output_kernel, owners),
        out_shape=(whole, whole, some_rows, pltpu.VMEM((cells_y, lanes), jnp.int32)),
        in_specs=[SMEM] * 2 + [VMEM] * (2 + len(rows_of_others)),
        out_specs=(VMEM,) * 4,
        compiler_params=PARAMS,
        cost_estimate=LONG,
        name="next_fields",
    )(rows, blocks, state, in_vmem(slabs[0]), *[in_vmem(other) for other in rows_of_others])

    image = pl.pallas_call(
        image_kernel,
        out_shape=jax.ShapeDtypeStruct((slab, cells_y, cells_z), F32),
        in_specs=[VMEM] * (1 + owners),
        out_specs=HBM,
        scratch_shapes=[pltpu.VMEM((slab, cells_y, cells_z), F32), pltpu.SemaphoreType.DMA((2,))],
        compiler_params=PARAMS,
        name="image_rows",
    )(in_vmem(own_image), in_vmem(own_place), *[in_vmem(value) for value in arrived])
    return forward_next[None], adjoint_next[None], image[None]


def solution(mesh):
    in_specs = (
        P("shot", "tx", "ty", None),
        P("shot", "tx", "ty", None),
        P("shot", "tx", "ty", None),
        P("shot", "tx", "ty", None),
        P(("tx", "ty"), "shot", None, None),
        P("shot", ("tx", "ty"), None),
        P("shot", None),
        P("shot"),
        P("shot", None, None),
        P("shot", None),
    )
    out_specs = (
        P("shot", "tx", "ty", None),
        P("shot", "tx", "ty", None),
        P(("tx", "ty"), "shot", None, None),
    )
    return jax.shard_map(
        on_device, mesh=mesh, in_specs=in_specs, out_specs=out_specs, check_vma=False
    )
```

time: 21.9 us -> 20.1 us (0.918)
  waiting for transfers between devices: 4.49 us -> 2.9 us
  local copies, waits for them, and re-layouts: 1.41 us -> 0.01 us
  starting transfers between devices: 10.3 us -> 11.3 us
    ppermute x3 -> x1, starting transfers between devices: 2.56 us -> 0.52 us  [on_device(): lax.ppermute(face, ('tx', 'ty'), pairs)]
    ppermute x6, waiting for transfers between devices: 4.48 us -> 2.52 us  [peer(): return lax.ppermute(value, 'shot', [(i, i ^ k) for i in range(owners)])]
    ppermute x0 -> x2, starting transfers between devices: none -> 1.64 us  [the longest x1 1.64 us: on_device(): from_even = lax.ppermute(faces[0], ('tx', 'ty'), x_even)]
    ppermute x6, starting transfers between devices: 7.72 us -> 9.17 us  [peer(): return lax.ppermute(value, 'shot', [(i, i ^ k) for i in range(owners)])]
    unnamed x4 -> x6, local copies, waits for them, and re-layouts: 1.41 us -> 0.01 us
    ppermute x0 -> x2, waiting for transfers between devices: none -> 0.37 us  [the longest x1 0.37 us: on_device(): from_even = lax.ppermute(faces[0], ('tx', 'ty'), x_even)]
    pallas_call x4 -> x7, Pallas kernels: 3.17 us -> 3.3 us  [the longest x1 1.21 us: on_device(): pl.pallas_call(functools.partial(load_kernel, owners, slab), out_shape=(f...]
  transfers between devices with their start and end apart: 9 -> 9, of which waited for: 4 -> 3; matrix products, arithmetic and copies ran while one was open for 6% -> 0% of each run, Pallas kernels for 6% -> 11%
where the time goes in v4:
time: 20.1 us; the launch traced here: 19.9 us
  starting transfers between devices  11.3 us (56%)
  Pallas kernels  4.31 us (21%)
  waiting for transfers between devices  2.9 us (14%)
  between operations  1.36 us (7%)
    ppermute x6, starting transfers between devices, peer(): return lax.ppermute(value, 'shot', [(i, i ^ k) for i in range(owners)])  9.17 us
    ppermute x6, waiting for transfers between devices, peer(): return lax.ppermute(value, 'shot', [(i, i ^ k) for i in range(owners)])  2.52 us
    ppermute x1, starting transfers between devices, on_device(): from_even = lax.ppermute(faces[0], ('tx', 'ty'), x_even)  1.64 us
    pallas_call x1, Pallas kernels, on_device(): pl.pallas_call(functools.partial(load_kernel, owners, slab), out_shape=(f...  1.21 us
    pallas_call x1, Pallas kernels, on_device(): pl.pallas_call(image_kernel, out_shape=jax.ShapeDtypeStruct((slab, cells_...  1 us
    pallas_call x1, Pallas kernels, on_device(): pl.pallas_call(functools.partial(output_kernel, owners), out_shape=(whole...  0.86 us
    pallas_call x1, Pallas kernels, on_device(): pl.pallas_call(inner_kernel, out_shape=pltpu.VMEM((4, cells_x, cells_y, c...  0.75 us
    ppermute x1, starting transfers between devices, on_device(): lax.ppermute(face, ('tx', 'ty'), pairs)  0.52 us
  transfers between devices with their start and end apart: 9, of which 3 were waited for; matrix products, arithmetic and copies ran while one was open for 0% of the time, Pallas kernels for 11%

profile of v4, /device:TPU:0, one launch (start us, length us, event | category | flops | bytes accessed | tf_op | source)
XLA Modules:
  0.0 19.9 jit_solution(6520473595934568796)
XLA Ops:
  0.6 0.0 copy-start.2
  0.6 1.2 %load_fields.1 = (f32[32,8,256]{2,1,0:T(8,128)S(1)}, f32[32,8,256]{2,1,0:T(8,128)S(1)}, bf16[32,8,256]{2,1,0:T(8,128)(2,1)S(1)}, s32[1,2]{1,0:T(1,128)S(4)}, s32...) custom-call(f32[32,8,256]{2,1,0:T(8,128)} %bitcast.16, ...), custom_call_target="tpu_custom_call" | custom-call | tf_op jit(solution)/shard_map/load_fields/pallas_call | solution.py:349
  1.9 0.5 %collective-permute-start = (bf16[2,16,8,256]{3,2,1,0:T(8,128)(2,1)S(1)}, bf16[2,16,8,256]{3,2,1,0:T(8,128)(2,1)S(1)}, u32[]{:S(2)}, u32[]{:S(2)}) collective-permute-start(bf16[2,16,8,256]{3,2,1,0:T(8,128)(2,1)S(1)} %get-tuple-element.40), channel_id=1, source_target_pairs={{0,1},{1,0},{2,3},{3,2},{4,5},{5,4},{6,7},{7,6},{8,9},{9,8},{10,11... | collective-permute-start | bytes 393224 | tf_op jit(solution)/shard_map/ppermute | solution.py:380
  2.4 0.0 copy-done.2
  2.4 3.5 %collective-permute-start.5 = (bf16[32,8,256]{2,1,0:T(8,128)(2,1)S(1)}, bf16[32,8,256]{2,1,0:T(8,128)(2,1)S(1)}, u32[]{:S(2)}, u32[]{:S(2)}) collective-permute-start(bf16[32,8,256]{2,1,0:T(8,128)(2,1)S(1)} %bitcast.19), channel_id=1, source_target_pairs={{0,24},{8,16},{16,8},{24,0},{1,25},{9,17},{17,9},{25,1},{2,26},{10... | collective-permute-start | bytes 393224 | tf_op jit(solution)/shard_map/ppermute | solution.py:336
  5.9 0.5 %collective-permute-start.4 = (bf16[32,8,256]{2,1,0:T(8,128)(2,1)S(1)}, bf16[32,8,256]{2,1,0:T(8,128)(2,1)S(1)}, u32[]{:S(2)}, u32[]{:S(2)}) collective-permute-start(bf16[32,8,256]{2,1,0:T(8,128)(2,1)S(1)} %bitcast.20), channel_id=1, source_target_pairs={{0,16},{8,24},{16,0},{24,8},{1,17},{9,25},{17,1},{25,9},{2,18},{10... | collective-permute-start | bytes 393224 | tf_op jit(solution)/shard_map/ppermute | solution.py:336
  6.4 0.0 collective-permute-done.refs_0_._
  6.4 0.0 copy-start
  6.4 0.0 copy-start.1
  6.4 1.6 %collective-permute-start.1 = (bf16[2,4,8,256]{3,2,1,0:T(8,128)(2,1)S(1)}, bf16[2,4,8,256]{3,2,1,0:T(8,128)(2,1)S(1)}, u32[]{:S(2)}, u32[]{:S(2)}) collective-permute-start(bf16[2,4,8,256]{3,2,1,0:T(8,128)(2,1)S(1)} %get-tuple-element.41), channel_id=1, source_target_pairs={{0,2},{2,0},{1,3},{3,1},{4,6},{6,4},{5,7},{7,5},{8,10},{10,8},{9,1... | collective-permute-start | bytes 98312 | tf_op jit(solution)/shard_map/ppermute | solution.py:392
  8.1 0.0 collective-permute-start.2
  8.1 0.5 %collective-permute-start.3 = (bf16[32,8,256]{2,1,0:T(8,128)(2,1)S(1)}, bf16[32,8,256]{2,1,0:T(8,128)(2,1)S(1)}, u32[]{:S(2)}, u32[]{:S(2)}) collective-permute-start(bf16[32,8,256]{2,1,0:T(8,128)(2,1)S(1)} %bitcast.21), channel_id=1, source_target_pairs={{0,8},{8,0},{16,24},{24,16},{1,9},{9,1},{17,25},{25,17},{2,10},{10... | collective-permute-start | bytes 393224 | tf_op jit(solution)/shard_map/ppermute | solution.py:336
  9.3 0.0 copy-done
  9.3 0.0 copy-done.1
  9.3 0.7 %inner_cells.1._ = f32[4,32,8,256]{3,2,1,0:T(8,128)S(1)} custom-call(f32[1,1]{1,0:T(1,128)} %bitcast.12.strength_ref, s32[1,2]{1,0:T(1,128)S(4)} %get-tuple-element.32.source_ref, s32[2,128]{1,0:T(2,128)S(1)} %get-tuple-element.33.receiver_ref, f32[1,128]{1,0:T(1,128)S(1)} %get-tuple-element.34.trace_ref, ...), custom_call_target="tpu_custom_call" | custom-call | bytes 60000000 | tf_op jit(solution)/shard_map/inner_cells/pallas_call | solution.py:394
  10.0 0.4 %collective-permute-done.1.x_even_ref = bf16[2,4,8,256]{3,2,1,0:T(8,128)(2,1)S(1)} collective-permute-done((bf16[2,4,8,256]{3,2,1,0:T(8,128)(2,1)S(1)}, bf16[2,4,8,256]{3,2,1,0:T(8,128)(2,1)S(1)}, u32[]{:S(2)}, u32[]{:S(2)}) %collective-permute-start.1) | collective-permute-done | bytes 32800 | tf_op jit(solution)/shard_map/ppermute | solution.py:392
  10.4 0.0 collective-permute-done.2.x_odd_ref
  10.5 0.0 collective-permute-done.5.slab_ref
  10.5 0.2 rows_to_send.5
  10.6 2.3 %collective-permute-start.8 = (s16[144,128]{1,0:T(8,128)(2,1)S(1)}, s16[144,128]{1,0:T(8,128)(2,1)S(1)}, u32[]{:S(2)}, u32[]{:S(2)}) collective-permute-start(s16[144,128]{1,0:T(8,128)(2,1)S(1)} %get-tuple-element.56), channel_id=1, source_target_pairs={{0,24},{8,16},{16,8},{24,0},{1,25},{9,17},{17,9},{25,1},{2,26},{10... | collective-permute-start | bytes 110600 | tf_op jit(solution)/shard_map/ppermute | solution.py:336
  13.0 0.0 collective-permute-done.4.slab_ref
  13.0 0.1 rows_to_send.4
  13.1 1.6 %collective-permute-start.7 = (s16[144,128]{1,0:T(8,128)(2,1)S(1)}, s16[144,128]{1,0:T(8,128)(2,1)S(1)}, u32[]{:S(2)}, u32[]{:S(2)}) collective-permute-start(s16[144,128]{1,0:T(8,128)(2,1)S(1)} %get-tuple-element.55), channel_id=1, source_target_pairs={{0,16},{8,24},{16,0},{24,8},{1,17},{9,25},{17,1},{25,9},{2,18},{10... | collective-permute-start | bytes 110600 | tf_op jit(solution)/shard_map/ppermute | solution.py:336
  14.7 0.0 collective-permute-done.3.slab_ref
  14.7 0.1 rows_to_send.3
  14.9 0.6 %collective-permute-start.6 = (s16[144,128]{1,0:T(8,128)(2,1)S(1)}, s16[144,128]{1,0:T(8,128)(2,1)S(1)}, u32[]{:S(2)}, u32[]{:S(2)}) collective-permute-start(s16[144,128]{1,0:T(8,128)(2,1)S(1)} %get-tuple-element.54), channel_id=1, source_target_pairs={{0,8},{8,0},{16,24},{24,16},{1,9},{9,1},{17,25},{25,17},{2,10},{10... | collective-permute-start | bytes 110600 | tf_op jit(solution)/shard_map/ppermute | solution.py:336
  15.5 0.9 %next_fields.1 = (f32[32,8,256]{2,1,0:T(8,128)}, f32[32,8,256]{2,1,0:T(8,128)}, f32[8,8,256]{2,1,0:T(8,128)S(1)}, s32[8,128]{1,0:T(8,128)S(1)}) custom-call(s32[32]{0:T(128)S(4)} %get-tuple-element.30.rows_ref, s32[32]{0:T(128)S(4)} %get-tuple-element.31.blocks_ref, f32[4,32,8,256]{3,2,1,0:T(8,128)S(1)} %edge_cells.1.state_ref, ...), custom_call_target="tpu_custom_call" | custom-call | bytes 60000000 | tf_op jit(solution)/shard_map/next_fields/pallas_call | solution.py:447
  16.4 0.0 collective-permute-done.8.refs_2_
  16.4 0.7 %collective-permute-done.7.refs_1_ = s16[144,128]{1,0:T(8,128)(2,1)S(1)} collective-permute-done((s16[144,128]{1,0:T(8,128)(2,1)S(1)}, s16[144,128]{1,0:T(8,128)(2,1)S(1)}, u32[]{:S(2)}, u32[]{:S(2)}) %collective-permute-start.7) | collective-permute-done | bytes 36896 | tf_op jit(solution)/shard_map/ppermute | solution.py:336
  17.1 1.8 %collective-permute-done.6.refs_0_ = s16[144,128]{1,0:T(8,128)(2,1)S(1)} collective-permute-done((s16[144,128]{1,0:T(8,128)(2,1)S(1)}, s16[144,128]{1,0:T(8,128)(2,1)S(1)}, u32[]{:S(2)}, u32[]{:S(2)}) %collective-permute-start.6) | collective-permute-done | bytes 36896 | tf_op jit(solution)/shard_map/ppermute | solution.py:336
  18.9 1.0 %image_rows.1 = f32[32,8,256]{2,1,0:T(8,128)} custom-call(f32[8,8,256]{2,1,0:T(8,128)S(1)} %get-tuple-element.52.own_ref, s32[8,128]{1,0:T(8,128)S(1)} %get-tuple-element.53.own_place_ref, s16[144,128]{1,0:T(8,128)(2,1)S(1)} %collective-permute-done.6.refs_0_, s16[144,128]{1,0:T(8,128)(2,1)S(1)} %collective-permute-done.7.refs_1_, ...), custom_call_target="tpu_custom_call" | custom-call | tf_op jit(solution)/shard_map/image_rows/pallas_call | solution.py:457
  (2 shorter events, 0.1 us)
Async XLA Ops:
  0.6 1.7 %copy-start.2 = (bf16[1,32,8,256]{3,2,1,0:T(8,128)(2,1)S(1)}, bf16[1,32,8,256]{3,2,1,0:T(8,128)(2,1)}, u32[]{:S(2)}) copy-start(bf16[1,32,8,256]{3,2,1,0:T(8,128)(2,1)} %param.14) | copy-start | bytes 393220
  1.9 4.6 %collective-permute-start = (bf16[2,16,8,256]{3,2,1,0:T(8,128)(2,1)S(1)}, bf16[2,16,8,256]{3,2,1,0:T(8,128)(2,1)S(1)}, u32[]{:S(2)}, u32[]{:S(2)}) collective-permute-start(bf16[2,16,8,256]{3,2,1,0:T(8,128)(2,1)S(1)} %get-tuple-element.40), channel_id=1, source_target_pairs={{0,1},{1,0},{2,3},{3,2},{4,5},{5,4},{6,7},{7,6},{8,9},{9,8},{10,11... | collective-permute-start | bytes 393224 | tf_op jit(solution)/shard_map/ppermute | solution.py:380
  2.4 8.1 %collective-permute-start.5 = (bf16[32,8,256]{2,1,0:T(8,128)(2,1)S(1)}, bf16[32,8,256]{2,1,0:T(8,128)(2,1)S(1)}, u32[]{:S(2)}, u32[]{:S(2)}) collective-permute-start(bf16[32,8,256]{2,1,0:T(8,128)(2,1)S(1)} %bitcast.19), channel_id=1, source_target_pairs={{0,24},{8,16},{16,8},{24,0},{1,25},{9,17},{17,9},{25,1},{2,26},{10... | collective-permute-start | bytes 393224 | tf_op jit(solution)/shard_map/ppermute | solution.py:336
  5.9 7.1 %collective-permute-start.4 = (bf16[32,8,256]{2,1,0:T(8,128)(2,1)S(1)}, bf16[32,8,256]{2,1,0:T(8,128)(2,1)S(1)}, u32[]{:S(2)}, u32[]{:S(2)}) collective-permute-start(bf16[32,8,256]{2,1,0:T(8,128)(2,1)S(1)} %bitcast.20), channel_id=1, source_target_pairs={{0,16},{8,24},{16,0},{24,8},{1,17},{9,25},{17,1},{25,9},{2,18},{10... | collective-permute-start | bytes 393224 | tf_op jit(solution)/shard_map/ppermute | solution.py:336
  6.4 2.9 %copy-start = (f32[1,32,8,256]{3,2,1,0:T(8,128)S(1)}, f32[1,32,8,256]{3,2,1,0:T(8,128)}, u32[]{:S(2)}) copy-start(f32[1,32,8,256]{3,2,1,0:T(8,128)} %param.10) | copy-start | bytes 786436
  6.4 2.9 %copy-start.1 = (f32[1,32,8,256]{3,2,1,0:T(8,128)S(1)}, f32[1,32,8,256]{3,2,1,0:T(8,128)}, u32[]{:S(2)}) copy-start(f32[1,32,8,256]{3,2,1,0:T(8,128)} %param.12) | copy-start | bytes 786436
  6.4 4.0 %collective-permute-start.1 = (bf16[2,4,8,256]{3,2,1,0:T(8,128)(2,1)S(1)}, bf16[2,4,8,256]{3,2,1,0:T(8,128)(2,1)S(1)}, u32[]{:S(2)}, u32[]{:S(2)}) collective-permute-start(bf16[2,4,8,256]{3,2,1,0:T(8,128)(2,1)S(1)} %get-tuple-element.41), channel_id=1, source_target_pairs={{0,2},{2,0},{1,3},{3,1},{4,6},{6,4},{5,7},{7,5},{8,10},{10,8},{9,1... | collective-permute-start | bytes 98312 | tf_op jit(solution)/shard_map/ppermute | solution.py:392
  8.1 2.3 %collective-permute-start.2 = (bf16[2,4,8,256]{3,2,1,0:T(8,128)(2,1)S(1)}, bf16[2,4,8,256]{3,2,1,0:T(8,128)(2,1)S(1)}, u32[]{:S(2)}, u32[]{:S(2)}) collective-permute-start(bf16[2,4,8,256]{3,2,1,0:T(8,128)(2,1)S(1)} %get-tuple-element.42), channel_id=1, source_target_pairs={{2,4},{4,2},{3,5},{5,3},{0,1},{1,0},{6,7},{7,6},{10,12},{12,10},{1... | collective-permute-start | bytes 98312 | tf_op jit(solution)/shard_map/ppermute | solution.py:391
  8.1 6.7 %collective-permute-start.3 = (bf16[32,8,256]{2,1,0:T(8,128)(2,1)S(1)}, bf16[32,8,256]{2,1,0:T(8,128)(2,1)S(1)}, u32[]{:S(2)}, u32[]{:S(2)}) collective-permute-start(bf16[32,8,256]{2,1,0:T(8,128)(2,1)S(1)} %bitcast.21), channel_id=1, source_target_pairs={{0,8},{8,0},{16,24},{24,16},{1,9},{9,1},{17,25},{25,17},{2,10},{10... | collective-permute-start | bytes 393224 | tf_op jit(solution)/shard_map/ppermute | solution.py:336
  10.6 5.8 %collective-permute-start.8 = (s16[144,128]{1,0:T(8,128)(2,1)S(1)}, s16[144,128]{1,0:T(8,128)(2,1)S(1)}, u32[]{:S(2)}, u32[]{:S(2)}) collective-permute-start(s16[144,128]{1,0:T(8,128)(2,1)S(1)} %get-tuple-element.56), channel_id=1, source_target_pairs={{0,24},{8,16},{16,8},{24,0},{1,25},{9,17},{17,9},{25,1},{2,26},{10... | collective-permute-start | bytes 110600 | tf_op jit(solution)/shard_map/ppermute | solution.py:336
  13.1 4.0 %collective-permute-start.7 = (s16[144,128]{1,0:T(8,128)(2,1)S(1)}, s16[144,128]{1,0:T(8,128)(2,1)S(1)}, u32[]{:S(2)}, u32[]{:S(2)}) collective-permute-start(s16[144,128]{1,0:T(8,128)(2,1)S(1)} %get-tuple-element.55), channel_id=1, source_target_pairs={{0,16},{8,24},{16,0},{24,8},{1,17},{9,25},{17,1},{25,9},{2,18},{10... | collective-permute-start | bytes 110600 | tf_op jit(solution)/shard_map/ppermute | solution.py:336
  14.9 4.0 %collective-permute-start.6 = (s16[144,128]{1,0:T(8,128)(2,1)S(1)}, s16[144,128]{1,0:T(8,128)(2,1)S(1)}, u32[]{:S(2)}, u32[]{:S(2)}) collective-permute-start(s16[144,128]{1,0:T(8,128)(2,1)S(1)} %get-tuple-element.54), channel_id=1, source_target_pairs={{0,8},{8,0},{16,24},{24,16},{1,9},{9,1},{17,25},{25,17},{2,10},{10... | collective-permute-start | bytes 110600 | tf_op jit(solution)/shard_map/ppermute | solution.py:336

commit v5 on v4

--- a/solution.py
+++ b/solution.py
@@ -67,7 +67,7 @@
 
 
 def load_kernel(owners, slab, f_hbm, a_hbm, v_hbm, source_hbm, receiver_hbm, trace_hbm, ids_hbm, *refs):
-    results, (ids_ref, taken_ref, sems) = refs[:-3], refs[-3:]
+    results, (ids_ref, sems) = refs[:-2], refs[-2:]
     f_ref, a_ref, v_ref, source_ref, receiver_ref, trace_ref, along_z_ref, along_xy_ref = results[:8]
     from_y_ref, rows_ref, blocks_ref = results[8:11]
     faces = results[11:]
@@ -101,18 +101,15 @@
         from_y_ref[2], from_y_ref[3] = halves(by_distance(jnp.where(same, jnp.where(at_even, before, after), 0)))
 
     copies[0].wait()
-    for owner in range(owners):
-        taken_ref[owner] = 0
-
-    def one_row(r, _):
-        owner = ids_ref[0, 0, r] // slab
-        slot = taken_ref[owner]
-        rows_ref[owner * capacity + slot] = r
-        blocks_ref[owner * capacity + slot] = ids_ref[0, 0, r] - owner * slab
-        taken_ref[owner] = slot + 1
-        return 0
-
-    lax.fori_loop(0, cells_x, one_row, 0, unroll=4)
+    bits = 32 // owners
+    taken = jnp.int32(0)
+    for r in range(cells_x):
+        block = ids_ref[0, 0, r]
+        owner = block // slab
+        slot = owner * capacity + ((taken >> (owner * bits)) & (2**bits - 1))
+        rows_ref[slot] = r
+        blocks_ref[slot] = block - owner * slab
+        taken = taken + (1 << (owner * bits))
     low = (lax.broadcasted_iota(jnp.int32, (half, cells_y, cells_z), 1) < REACH).astype(jnp.int32)
     for field, ref in enumerate((f_ref, a_ref)):
         copies[1 + field].wait()
@@ -125,7 +122,11 @@
         copy.wait()
 
 
-def face_kernel(f_ref, a_ref, _, even_ref, odd_ref):
+def after_kernel(in_ref, _, out_ref):
+    out_ref[...] = in_ref[...]
+
+
+def face_kernel(f_ref, a_ref, even_ref, odd_ref):
     at_even = lax.axis_index("tx") % 2 == 0
     tail, head = f_ref.shape[0] - REACH, 0
     for field, ref in enumerate((f_ref, a_ref)):
@@ -266,36 +267,49 @@
             a_out_ref[r] = others[2 * n + 1][j]
 
 
-def image_kernel(own_ref, own_place_ref, *refs):
-    messages, (out_hbm, out_ref, sems) = refs[:-3], refs[-3:]
-    slab, cells_y, cells_z = out_ref.shape
-    lanes = messages[0].shape[1]
-    parts = cells_z // lanes
-    count = own_ref.shape[0] * cells_y
-    scales, places = [jnp.ones((cells_y, count), F32)], [own_place_ref[:, :count]]
-    for ref in messages:
-        tail = ref[parts * count :, :count].astype(jnp.int32)
-        scales.append(scale_of(tail[:cells_y]))
-        places.append(tail[cells_y:])
-    scales, places = jnp.concatenate(scales, axis=1), jnp.concatenate(places, axis=1)
+def chosen_matrix(scales, places, slab, cells_y):
     shape = (slab,) + places.shape
     block = lax.broadcasted_iota(jnp.int32, shape, 0)
     y = lax.broadcasted_iota(jnp.int32, shape, 1)
     y_of_row = lax.broadcasted_iota(jnp.int32, shape, 2) % cells_y
     chosen = jnp.where((block == places[None]) & (y == y_of_row), scales[None], 0.0)
-    chosen = chosen.reshape(slab * cells_y, places.shape[1]).astype(BF16)
-    rows = [own_ref[...].reshape(count, cells_z)]
-    for ref in messages:
-        columns = [ref[part * count : (part + 1) * count, :] for part in range(parts)]
-        rows.append(jnp.concatenate(columns, axis=1).astype(F32))
+    return chosen.reshape(slab * cells_y, places.shape[1]).astype(BF16)
+
+
+def message_parts(ref, count, cells_y, cells_z):
+    lanes = ref.shape[1]
+    parts = cells_z // lanes
+    tail = ref[parts * count :, :count].astype(jnp.int32)
+    columns = [ref[part * count : (part + 1) * count, :] for part in range(parts)]
+    return scale_of(tail[:cells_y]), tail[cells_y:], jnp.concatenate(columns, axis=1).astype(F32)
+
+
+def first_image_kernel(own_ref, own_place_ref, *refs):
+    messages, out_ref = refs[:-1], refs[-1]
+    slab, cells_y, cells_z = out_ref.shape
+    count = own_ref.shape[0] * cells_y
+    own = own_ref[...].reshape(count, cells_z)
+    parts = [(jnp.ones((cells_y, count), F32), own_place_ref[:, :count], own)]
+    parts += [message_parts(ref, count, cells_y, cells_z) for ref in messages]
+    scales, places, rows = zip(*parts)
+    chosen = chosen_matrix(jnp.concatenate(scales, axis=1), jnp.concatenate(places, axis=1), slab, cells_y)
     high, low = halves(jnp.concatenate(rows, axis=0))
+    total = jnp.dot(chosen, high, preferred_element_type=F32) + jnp.dot(chosen, low, preferred_element_type=F32)
+    out_ref[...] = total.reshape(slab, cells_y, cells_z)
+
+
+def last_image_kernel(count, in_ref, message_ref, out_hbm, out_ref, sems):
+    slab, cells_y, cells_z = in_ref.shape
+    scales, places, rows = message_parts(message_ref, count, cells_y, cells_z)
+    chosen = chosen_matrix(scales, places, slab, cells_y)
+    high, low = halves(rows)
     half = slab // 2
     copies = []
     for n in range(2):
         some = chosen[n * half * cells_y : (n + 1) * half * cells_y]
         total = jnp.dot(some, high, preferred_element_type=F32) + jnp.dot(some, low, preferred_element_type=F32)
         blocks = pl.ds(n * half, half)
-        out_ref[blocks] = total.reshape(half, cells_y, cells_z)
+        out_ref[blocks] = in_ref[blocks] + total.reshape(half, cells_y, cells_z)
         copies.append(pltpu.make_async_copy(out_ref.at[blocks], out_hbm.at[blocks], sems.at[n]))
         copies[n].start()
     for copy in copies:
@@ -366,7 +380,6 @@
         out_specs=(VMEM,) * 3 + (SMEM,) + (VMEM,) * 5 + (SMEM,) * 2 + (VMEM,) * sides,
         scratch_shapes=[
             pltpu.SMEM(aperture.shape, jnp.int32),
-            pltpu.SMEM((owners,), jnp.int32),
             pltpu.SemaphoreType.DMA((7,)),
         ],
         compiler_params=PARAMS,
@@ -381,14 +394,23 @@
     faces = pl.pallas_call(
         face_kernel,
         out_shape=(x_face, x_face),
-        in_specs=[VMEM] * 3,
+        in_specs=[VMEM] * 2,
         out_specs=(VMEM, VMEM),
         compiler_params=PARAMS,
+        cost_estimate=HEAVY,
+        name="faces_along_x",
+    )(forward_now, adjoint_now)
+    odd_face = pl.pallas_call(
+        after_kernel,
+        out_shape=x_face,
+        in_specs=[VMEM] * 2,
+        out_specs=VMEM,
+        compiler_params=PARAMS,
         cost_estimate=CHEAP,
-        name="faces_along_x",
-    )(forward_now, adjoint_now, y_halos[0])
+        name="odd_face_after_y",
+    )(in_vmem(faces[1]), y_halos[0])
     x_even, x_odd = swaps("tx", "ty")
-    from_odd = lax.ppermute(faces[1], ("tx", "ty"), x_odd)
+    from_odd = lax.ppermute(odd_face, ("tx", "ty"), x_odd)
     from_even = lax.ppermute(faces[0], ("tx", "ty"), x_even)
 
     state = pl.pallas_call(
@@ -454,15 +476,26 @@
         name="next_fields",
     )(rows, blocks, state, in_vmem(slabs[0]), *[in_vmem(other) for other in rows_of_others])
 
+    arrived = [in_vmem(value) for value in arrived]
+    image_shape = (slab, cells_y, cells_z)
     image = pl.pallas_call(
-        image_kernel,
-        out_shape=jax.ShapeDtypeStruct((slab, cells_y, cells_z), F32),
-        in_specs=[VMEM] * (1 + owners),
+        first_image_kernel,
+        out_shape=pltpu.VMEM(image_shape, F32),
+        in_specs=[VMEM] * owners,
+        out_specs=VMEM,
+        compiler_params=PARAMS,
+        cost_estimate=CHEAP,
+        name="image_of_first",
+    )(in_vmem(own_image), in_vmem(own_place), *arrived[1:])
+    image = pl.pallas_call(
+        functools.partial(last_image_kernel, capacity * cells_y),
+        out_shape=jax.ShapeDtypeStruct(image_shape, F32),
+        in_specs=[VMEM] * 2,
         out_specs=HBM,
-        scratch_shapes=[pltpu.VMEM((slab, cells_y, cells_z), F32), pltpu.SemaphoreType.DMA((2,))],
+        scratch_shapes=[pltpu.VMEM(image_shape, F32), pltpu.SemaphoreType.DMA((2,))],
         compiler_params=PARAMS,
         name="image_rows",
-    )(in_vmem(own_image), in_vmem(own_place), *[in_vmem(value) for value in arrived])
+    )(in_vmem(image), arrived[0])
     return forward_next[None], adjoint_next[None], image[None]
 
 

time: 20.1 us -> 19.2 us (0.955)
  starting transfers between devices: 11.3 us -> 10.4 us
    ppermute x6, starting transfers between devices: 9.17 us -> 8.53 us  [peer(): return lax.ppermute(value, 'shot', [(i, i ^ k) for i in range(owners)])]
    ppermute x1, starting transfers between devices: 0.52 us -> 0.07 us  [on_device(): lax.ppermute(face, ('tx', 'ty'), pairs)]
    pallas_call x1 -> x3, Pallas kernels: 1 us -> 1.2 us  [the longest x1 0.92 us: on_device(): pl.pallas_call(functools.partial(last_image_kernel, capacity * cells_y),...]
  transfers between devices with their start and end apart: 9 -> 9, of which waited for: 3 -> 5; matrix products, arithmetic and copies ran while one was open for 0% -> 0% of each run, Pallas kernels for 11% -> 19%
where the time goes in v5:
time: 19.2 us; the launch traced here: 19.1 us
  starting transfers between devices  10.4 us (54%)
  Pallas kernels  4.46 us (23%)
  waiting for transfers between devices  2.76 us (14%)
  between operations  1.39 us (7%)
    ppermute x6, starting transfers between devices, peer(): return lax.ppermute(value, 'shot', [(i, i ^ k) for i in range(owners)])  8.53 us
    ppermute x6, waiting for transfers between devices, peer(): return lax.ppermute(value, 'shot', [(i, i ^ k) for i in range(owners)])  2.58 us
    ppermute x1, starting transfers between devices, on_device(): from_even = lax.ppermute(faces[0], ('tx', 'ty'), x_even)  1.64 us
    pallas_call x1, Pallas kernels, on_device(): pl.pallas_call(functools.partial(load_kernel, owners, slab), out_shape=(f...  1.14 us
    pallas_call x1, Pallas kernels, on_device(): pl.pallas_call(functools.partial(last_image_kernel, capacity * cells_y),...  0.92 us
    pallas_call x1, Pallas kernels, on_device(): pl.pallas_call(functools.partial(output_kernel, owners), out_shape=(whole...  0.86 us
    pallas_call x1, Pallas kernels, on_device(): pl.pallas_call(inner_kernel, out_shape=pltpu.VMEM((4, cells_x, cells_y, c...  0.76 us
    pallas_call x3, Pallas kernels, on_device(): pl.pallas_call(functools.partial(send_kernel, k), out_shape=(message, som...  0.44 us
  transfers between devices with their start and end apart: 9, of which 5 were waited for; matrix products, arithmetic and copies ran while one was open for 0% of the time, Pallas kernels for 19%

profile of v5, /device:TPU:0, one launch (start us, length us, event | category | flops | bytes accessed | tf_op | source)
XLA Modules:
  0.0 19.1 jit_solution(7841963133750724781)
XLA Ops:
  0.6 4.0 %collective-permute-start.5 = (bf16[32,8,256]{2,1,0:T(8,128)(2,1)}, bf16[32,8,256]{2,1,0:T(8,128)(2,1)S(1)}, u32[]{:S(2)}, u32[]{:S(2)}) collective-permute-start(bf16[32,8,256]{2,1,0:T(8,128)(2,1)} %bitcast.18), channel_id=1, source_target_pairs={{0,24},{8,16},{16,8},{24,0},{1,25},{9,17},{17,9},{25,1},{2,26},{10... | collective-permute-start | bytes 393224 | tf_op jit(solution)/shard_map/ppermute | solution.py:350
  4.6 0.5 %collective-permute-start.4 = (bf16[32,8,256]{2,1,0:T(8,128)(2,1)}, bf16[32,8,256]{2,1,0:T(8,128)(2,1)S(1)}, u32[]{:S(2)}, u32[]{:S(2)}) collective-permute-start(bf16[32,8,256]{2,1,0:T(8,128)(2,1)} %bitcast.19), channel_id=1, source_target_pairs={{0,16},{8,24},{16,0},{24,8},{1,17},{9,25},{17,1},{25,9},{2,18},{10... | collective-permute-start | bytes 393224 | tf_op jit(solution)/shard_map/ppermute | solution.py:350
  5.1 1.1 %load_fields.1 = (f32[32,8,256]{2,1,0:T(8,128)S(1)}, f32[32,8,256]{2,1,0:T(8,128)S(1)}, bf16[32,8,256]{2,1,0:T(8,128)(2,1)S(1)}, s32[1,2]{1,0:T(1,128)S(4)}, s32...) custom-call(f32[32,8,256]{2,1,0:T(8,128)} %bitcast.15, ...), custom_call_target="tpu_custom_call" | custom-call | tf_op jit(solution)/shard_map/load_fields/pallas_call | solution.py:363
  6.2 0.1 collective-permute-start
  6.3 0.0 copy-start
  6.3 0.0 copy-start.1
  6.4 0.0 copy-start.2
  6.4 1.6 %collective-permute-start.1 = (bf16[2,4,8,256]{3,2,1,0:T(8,128)(2,1)S(1)}, bf16[2,4,8,256]{3,2,1,0:T(8,128)(2,1)S(1)}, u32[]{:S(2)}, u32[]{:S(2)}) collective-permute-start(bf16[2,4,8,256]{3,2,1,0:T(8,128)(2,1)S(1)} %get-tuple-element.41), channel_id=1, source_target_pairs={{0,2},{2,0},{1,3},{3,1},{4,6},{6,4},{5,7},{7,5},{8,10},{10,8},{9,1... | collective-permute-start | bytes 98312 | tf_op jit(solution)/shard_map/ppermute | solution.py:414
  8.0 0.0 collective-permute-done.refs_0_._
  8.0 0.2 collective-permute-start.2
  8.2 0.0 copy-done.2
  8.2 0.5 %collective-permute-start.3 = (bf16[32,8,256]{2,1,0:T(8,128)(2,1)S(1)}, bf16[32,8,256]{2,1,0:T(8,128)(2,1)S(1)}, u32[]{:S(2)}, u32[]{:S(2)}) collective-permute-start(bf16[32,8,256]{2,1,0:T(8,128)(2,1)S(1)} %bitcast.21), channel_id=1, source_target_pairs={{0,8},{8,0},{16,24},{24,16},{1,9},{9,1},{17,25},{25,17},{2,10},{10... | collective-permute-start | bytes 393224 | tf_op jit(solution)/shard_map/ppermute | solution.py:350
  9.4 0.0 copy-done
  9.4 0.0 copy-done.1
  9.4 0.8 %inner_cells.1._ = f32[4,32,8,256]{3,2,1,0:T(8,128)S(1)} custom-call(f32[1,1]{1,0:T(1,128)} %bitcast.12.strength_ref, s32[1,2]{1,0:T(1,128)S(4)} %get-tuple-element.32.source_ref, s32[2,128]{1,0:T(2,128)S(1)} %get-tuple-element.33.receiver_ref, f32[1,128]{1,0:T(1,128)S(1)} %get-tuple-element.34.trace_ref, ...), custom_call_target="tpu_custom_call" | custom-call | bytes 60000000 | tf_op jit(solution)/shard_map/inner_cells/pallas_call | solution.py:416
  10.2 0.2 collective-permute-done.1.x_even_ref
  10.4 0.0 collective-permute-done.2.x_odd_ref
  10.4 0.0 collective-permute-done.5.slab_ref
  10.4 0.2 rows_to_send.5
  10.6 2.4 %collective-permute-start.7 = (s16[144,128]{1,0:T(8,128)(2,1)S(1)}, s16[144,128]{1,0:T(8,128)(2,1)S(1)}, u32[]{:S(2)}, u32[]{:S(2)}) collective-permute-start(s16[144,128]{1,0:T(8,128)(2,1)S(1)} %get-tuple-element.55), channel_id=1, source_target_pairs={{0,24},{8,16},{16,8},{24,0},{1,25},{9,17},{17,9},{25,1},{2,26},{10... | collective-permute-start | bytes 110600 | tf_op jit(solution)/shard_map/ppermute | solution.py:350
  13.0 0.0 collective-permute-done.4.slab_ref
  13.0 0.1 rows_to_send.4
  13.1 0.5 %collective-permute-start.6 = (s16[144,128]{1,0:T(8,128)(2,1)S(1)}, s16[144,128]{1,0:T(8,128)(2,1)S(1)}, u32[]{:S(2)}, u32[]{:S(2)}) collective-permute-start(s16[144,128]{1,0:T(8,128)(2,1)S(1)} %get-tuple-element.54), channel_id=1, source_target_pairs={{0,16},{8,24},{16,0},{24,8},{1,17},{9,25},{17,1},{25,9},{2,18},{10... | collective-permute-start | bytes 110600 | tf_op jit(solution)/shard_map/ppermute | solution.py:350
  13.7 0.3 %collective-permute-done.3.slab_ref = bf16[32,8,256]{2,1,0:T(8,128)(2,1)S(1)} collective-permute-done((bf16[32,8,256]{2,1,0:T(8,128)(2,1)S(1)}, bf16[32,8,256]{2,1,0:T(8,128)(2,1)S(1)}, u32[]{:S(2)}, u32[]{:S(2)}) %collective-permute-start.3) | collective-permute-done | bytes 131104 | tf_op jit(solution)/shard_map/ppermute | solution.py:350
  14.0 0.1 rows_to_send.3
  14.1 0.6 %collective-permute-start.8 = (s16[144,128]{1,0:T(8,128)(2,1)S(1)}, s16[144,128]{1,0:T(8,128)(2,1)S(1)}, u32[]{:S(2)}, u32[]{:S(2)}) collective-permute-start(s16[144,128]{1,0:T(8,128)(2,1)S(1)} %get-tuple-element.56), channel_id=1, source_target_pairs={{0,8},{8,0},{16,24},{24,16},{1,9},{9,1},{17,25},{25,17},{2,10},{10... | collective-permute-start | bytes 110600 | tf_op jit(solution)/shard_map/ppermute | solution.py:350
  14.7 0.9 %next_fields.1 = (f32[32,8,256]{2,1,0:T(8,128)}, f32[32,8,256]{2,1,0:T(8,128)}, f32[8,8,256]{2,1,0:T(8,128)S(1)}, s32[8,128]{1,0:T(8,128)S(1)}) custom-call(s32[32]{0:T(128)S(4)} %get-tuple-element.30.rows_ref, s32[32]{0:T(128)S(4)} %get-tuple-element.31.blocks_ref, f32[4,32,8,256]{3,2,1,0:T(8,128)S(1)} %edge_cells.1.state_ref, ...), custom_call_target="tpu_custom_call" | custom-call | bytes 60000000 | tf_op jit(solution)/shard_map/next_fields/pallas_call | solution.py:469
  15.6 0.2 collective-permute-done.7.refs_1_
  15.7 1.4 %collective-permute-done.6.refs_0_ = s16[144,128]{1,0:T(8,128)(2,1)S(1)} collective-permute-done((s16[144,128]{1,0:T(8,128)(2,1)S(1)}, s16[144,128]{1,0:T(8,128)(2,1)S(1)}, u32[]{:S(2)}, u32[]{:S(2)}) %collective-permute-start.6) | collective-permute-done | bytes 36896 | tf_op jit(solution)/shard_map/ppermute | solution.py:350
  17.2 0.3 %image_of_first.1.in_ref = f32[32,8,256]{2,1,0:T(8,128)S(1)} custom-call(f32[8,8,256]{2,1,0:T(8,128)S(1)} %get-tuple-element.52.own_ref, s32[8,128]{1,0:T(8,128)S(1)} %get-tuple-element.53.own_place_ref, s16[144,128]{1,0:T(8,128)(2,1)S(1)} %collective-permute-done.6.refs_0_, s16[144,128]{1,0:T(8,128)(2,1)S(1)} %collective-permute-done.7.refs_1_), custom_call_target="tpu_custom_call" | custom-call | tf_op jit(solution)/shard_map/image_of_first/pallas_call | solution.py:481
  17.4 0.7 %collective-permute-done.8.message_ref = s16[144,128]{1,0:T(8,128)(2,1)S(1)} collective-permute-done((s16[144,128]{1,0:T(8,128)(2,1)S(1)}, s16[144,128]{1,0:T(8,128)(2,1)S(1)}, u32[]{:S(2)}, u32[]{:S(2)}) %collective-permute-start.8) | collective-permute-done | bytes 36896 | tf_op jit(solution)/shard_map/ppermute | solution.py:350
  18.1 0.9 %image_rows.1 = f32[32,8,256]{2,1,0:T(8,128)} custom-call(f32[32,8,256]{2,1,0:T(8,128)S(1)} %image_of_first.1.in_ref, s16[144,128]{1,0:T(8,128)(2,1)S(1)} %collective-permute-done.8.message_ref), custom_call_target="tpu_custom_call" | custom-call | tf_op jit(solution)/shard_map/image_rows/pallas_call | solution.py:490
  (3 shorter events, 0.1 us)
Async XLA Ops:
  0.6 9.8 %collective-permute-start.5 = (bf16[32,8,256]{2,1,0:T(8,128)(2,1)}, bf16[32,8,256]{2,1,0:T(8,128)(2,1)S(1)}, u32[]{:S(2)}, u32[]{:S(2)}) collective-permute-start(bf16[32,8,256]{2,1,0:T(8,128)(2,1)} %bitcast.18), channel_id=1, source_target_pairs={{0,24},{8,16},{16,8},{24,0},{1,25},{9,17},{17,9},{25,1},{2,26},{10... | collective-permute-start | bytes 393224 | tf_op jit(solution)/shard_map/ppermute | solution.py:350
  4.6 8.4 %collective-permute-start.4 = (bf16[32,8,256]{2,1,0:T(8,128)(2,1)}, bf16[32,8,256]{2,1,0:T(8,128)(2,1)S(1)}, u32[]{:S(2)}, u32[]{:S(2)}) collective-permute-start(bf16[32,8,256]{2,1,0:T(8,128)(2,1)} %bitcast.19), channel_id=1, source_target_pairs={{0,16},{8,24},{16,0},{24,8},{1,17},{9,25},{17,1},{25,9},{2,18},{10... | collective-permute-start | bytes 393224 | tf_op jit(solution)/shard_map/ppermute | solution.py:350
  6.2 1.8 %collective-permute-start = (bf16[2,16,8,256]{3,2,1,0:T(8,128)(2,1)S(1)}, bf16[2,16,8,256]{3,2,1,0:T(8,128)(2,1)S(1)}, u32[]{:S(2)}, u32[]{:S(2)}) collective-permute-start(bf16[2,16,8,256]{3,2,1,0:T(8,128)(2,1)S(1)} %get-tuple-element.40), channel_id=1, source_target_pairs={{0,1},{1,0},{2,3},{3,2},{4,5},{5,4},{6,7},{7,6},{8,9},{9,8},{10,11... | collective-permute-start | bytes 393224 | tf_op jit(solution)/shard_map/ppermute | solution.py:393
  6.3 3.1 %copy-start = (f32[1,32,8,256]{3,2,1,0:T(8,128)S(1)}, f32[1,32,8,256]{3,2,1,0:T(8,128)}, u32[]{:S(2)}) copy-start(f32[1,32,8,256]{3,2,1,0:T(8,128)} %param.10) | copy-start | bytes 786436
  6.3 3.1 %copy-start.1 = (f32[1,32,8,256]{3,2,1,0:T(8,128)S(1)}, f32[1,32,8,256]{3,2,1,0:T(8,128)}, u32[]{:S(2)}) copy-start(f32[1,32,8,256]{3,2,1,0:T(8,128)} %param.12) | copy-start | bytes 786436
  6.4 1.8 %copy-start.2 = (bf16[1,32,8,256]{3,2,1,0:T(8,128)(2,1)S(1)}, bf16[1,32,8,256]{3,2,1,0:T(8,128)(2,1)}, u32[]{:S(2)}) copy-start(bf16[1,32,8,256]{3,2,1,0:T(8,128)(2,1)} %param.14) | copy-start | bytes 393220
  6.4 4.0 %collective-permute-start.1 = (bf16[2,4,8,256]{3,2,1,0:T(8,128)(2,1)S(1)}, bf16[2,4,8,256]{3,2,1,0:T(8,128)(2,1)S(1)}, u32[]{:S(2)}, u32[]{:S(2)}) collective-permute-start(bf16[2,4,8,256]{3,2,1,0:T(8,128)(2,1)S(1)} %get-tuple-element.41), channel_id=1, source_target_pairs={{0,2},{2,0},{1,3},{3,1},{4,6},{6,4},{5,7},{7,5},{8,10},{10,8},{9,1... | collective-permute-start | bytes 98312 | tf_op jit(solution)/shard_map/ppermute | solution.py:414
  8.0 2.3 %collective-permute-start.2 = (bf16[2,4,8,256]{3,2,1,0:T(8,128)(2,1)S(1)}, bf16[2,4,8,256]{3,2,1,0:T(8,128)(2,1)S(1)}, u32[]{:S(2)}, u32[]{:S(2)}) collective-permute-start(bf16[2,4,8,256]{3,2,1,0:T(8,128)(2,1)S(1)} %odd_face_after_y.1), channel_id=1, source_target_pairs={{2,4},{4,2},{3,5},{5,3},{0,1},{1,0},{6,7},{7,6},{10,12},{12,10},{1... | collective-permute-start | bytes 98312 | tf_op jit(solution)/shard_map/ppermute | solution.py:413
  8.2 5.7 %collective-permute-start.3 = (bf16[32,8,256]{2,1,0:T(8,128)(2,1)S(1)}, bf16[32,8,256]{2,1,0:T(8,128)(2,1)S(1)}, u32[]{:S(2)}, u32[]{:S(2)}) collective-permute-start(bf16[32,8,256]{2,1,0:T(8,128)(2,1)S(1)} %bitcast.21), channel_id=1, source_target_pairs={{0,8},{8,0},{16,24},{24,16},{1,9},{9,1},{17,25},{25,17},{2,10},{10... | collective-permute-start | bytes 393224 | tf_op jit(solution)/shard_map/ppermute | solution.py:350
  10.6 5.1 %collective-permute-start.7 = (s16[144,128]{1,0:T(8,128)(2,1)S(1)}, s16[144,128]{1,0:T(8,128)(2,1)S(1)}, u32[]{:S(2)}, u32[]{:S(2)}) collective-permute-start(s16[144,128]{1,0:T(8,128)(2,1)S(1)} %get-tuple-element.55), channel_id=1, source_target_pairs={{0,24},{8,16},{16,8},{24,0},{1,25},{9,17},{17,9},{25,1},{2,26},{10... | collective-permute-start | bytes 110600 | tf_op jit(solution)/shard_map/ppermute | solution.py:350
  13.1 4.0 %collective-permute-start.6 = (s16[144,128]{1,0:T(8,128)(2,1)S(1)}, s16[144,128]{1,0:T(8,128)(2,1)S(1)}, u32[]{:S(2)}, u32[]{:S(2)}) collective-permute-start(s16[144,128]{1,0:T(8,128)(2,1)S(1)} %get-tuple-element.54), channel_id=1, source_target_pairs={{0,16},{8,24},{16,0},{24,8},{1,17},{9,25},{17,1},{25,9},{2,18},{10... | collective-permute-start | bytes 110600 | tf_op jit(solution)/shard_map/ppermute | solution.py:350
  14.1 4.0 %collective-permute-start.8 = (s16[144,128]{1,0:T(8,128)(2,1)S(1)}, s16[144,128]{1,0:T(8,128)(2,1)S(1)}, u32[]{:S(2)}, u32[]{:S(2)}) collective-permute-start(s16[144,128]{1,0:T(8,128)(2,1)S(1)} %get-tuple-element.56), channel_id=1, source_target_pairs={{0,8},{8,0},{16,24},{24,16},{1,9},{9,1},{17,25},{25,17},{2,10},{10... | collective-permute-start | bytes 110600 | tf_op jit(solution)/shard_map/ppermute | solution.py:350

commit v6 on v5

--- a/solution.py
+++ b/solution.py
@@ -74,7 +74,7 @@
     pairs = [(ids_hbm, ids_ref), (f_hbm, f_ref), (a_hbm, a_ref), (v_hbm, v_ref)]
     pairs += [(source_hbm, source_ref), (receiver_hbm, receiver_ref), (trace_hbm, trace_ref)]
     copies = [pltpu.make_async_copy(src, dst, sems.at[n]) for n, (src, dst) in enumerate(pairs)]
-    for copy in copies:
+    for copy in copies[1:3] + copies[:1] + copies[3:]:
         copy.start()
     cells_x, cells_y, cells_z = f_ref.shape
     cells = cells_x * cells_y

time: 19.2 us -> 19.2 us (level)
  no operation moved by 1% of the time
where the time goes in v6:
time: 19.2 us; the launch traced here: 19.1 us
  starting transfers between devices  10.4 us (54%)
  Pallas kernels  4.49 us (23%)
  waiting for transfers between devices  2.76 us (14%)
  between operations  1.39 us (7%)
    ppermute x6, starting transfers between devices, peer(): return lax.ppermute(value, 'shot', [(i, i ^ k) for i in range(owners)])  8.53 us
    ppermute x6, waiting for transfers between devices, peer(): return lax.ppermute(value, 'shot', [(i, i ^ k) for i in range(owners)])  2.58 us
    ppermute x1, starting transfers between devices, on_device(): from_even = lax.ppermute(faces[0], ('tx', 'ty'), x_even)  1.64 us
    pallas_call x1, Pallas kernels, on_device(): pl.pallas_call(functools.partial(load_kernel, owners, slab), out_shape=(f...  1.17 us
    pallas_call x1, Pallas kernels, on_device(): pl.pallas_call(functools.partial(last_image_kernel, capacity * cells_y),...  0.92 us
    pallas_call x1, Pallas kernels, on_device(): pl.pallas_call(functools.partial(output_kernel, owners), out_shape=(whole...  0.86 us
    pallas_call x1, Pallas kernels, on_device(): pl.pallas_call(inner_kernel, out_shape=pltpu.VMEM((4, cells_x, cells_y, c...  0.76 us
    pallas_call x3, Pallas kernels, on_device(): pl.pallas_call(functools.partial(send_kernel, k), out_shape=(message, som...  0.44 us
  transfers between devices with their start and end apart: 9, of which 5 were waited for; matrix products, arithmetic and copies ran while one was open for 0% of the time, Pallas kernels for 19%

profile of v6, /device:TPU:0, one launch (start us, length us, event | category | flops | bytes accessed | tf_op | source)
XLA Modules:
  0.0 19.1 jit_solution(16483609763685555456)
XLA Ops:
  0.6 4.0 %collective-permute-start.5 = (bf16[32,8,256]{2,1,0:T(8,128)(2,1)}, bf16[32,8,256]{2,1,0:T(8,128)(2,1)S(1)}, u32[]{:S(2)}, u32[]{:S(2)}) collective-permute-start(bf16[32,8,256]{2,1,0:T(8,128)(2,1)} %bitcast.18), channel_id=1, source_target_pairs={{0,24},{8,16},{16,8},{24,0},{1,25},{9,17},{17,9},{25,1},{2,26},{10... | collective-permute-start | bytes 393224 | tf_op jit(solution)/shard_map/ppermute | solution.py:350
  4.6 0.5 %collective-permute-start.4 = (bf16[32,8,256]{2,1,0:T(8,128)(2,1)}, bf16[32,8,256]{2,1,0:T(8,128)(2,1)S(1)}, u32[]{:S(2)}, u32[]{:S(2)}) collective-permute-start(bf16[32,8,256]{2,1,0:T(8,128)(2,1)} %bitcast.19), channel_id=1, source_target_pairs={{0,16},{8,24},{16,0},{24,8},{1,17},{9,25},{17,1},{25,9},{2,18},{10... | collective-permute-start | bytes 393224 | tf_op jit(solution)/shard_map/ppermute | solution.py:350
  5.1 1.2 %load_fields.1 = (f32[32,8,256]{2,1,0:T(8,128)S(1)}, f32[32,8,256]{2,1,0:T(8,128)S(1)}, bf16[32,8,256]{2,1,0:T(8,128)(2,1)S(1)}, s32[1,2]{1,0:T(1,128)S(4)}, s32...) custom-call(f32[32,8,256]{2,1,0:T(8,128)} %bitcast.15, ...), custom_call_target="tpu_custom_call" | custom-call | tf_op jit(solution)/shard_map/load_fields/pallas_call | solution.py:363
  6.3 0.1 collective-permute-start
  6.4 0.0 copy-start
  6.4 0.0 copy-start.1
  6.4 0.0 copy-start.2
  6.4 1.6 %collective-permute-start.1 = (bf16[2,4,8,256]{3,2,1,0:T(8,128)(2,1)S(1)}, bf16[2,4,8,256]{3,2,1,0:T(8,128)(2,1)S(1)}, u32[]{:S(2)}, u32[]{:S(2)}) collective-permute-start(bf16[2,4,8,256]{3,2,1,0:T(8,128)(2,1)S(1)} %get-tuple-element.41), channel_id=1, source_target_pairs={{0,2},{2,0},{1,3},{3,1},{4,6},{6,4},{5,7},{7,5},{8,10},{10,8},{9,1... | collective-permute-start | bytes 98312 | tf_op jit(solution)/shard_map/ppermute | solution.py:414
  8.1 0.0 collective-permute-done.refs_0_._
  8.1 0.2 collective-permute-start.2
  8.2 0.0 copy-done.2
  8.2 0.5 %collective-permute-start.3 = (bf16[32,8,256]{2,1,0:T(8,128)(2,1)S(1)}, bf16[32,8,256]{2,1,0:T(8,128)(2,1)S(1)}, u32[]{:S(2)}, u32[]{:S(2)}) collective-permute-start(bf16[32,8,256]{2,1,0:T(8,128)(2,1)S(1)} %bitcast.21), channel_id=1, source_target_pairs={{0,8},{8,0},{16,24},{24,16},{1,9},{9,1},{17,25},{25,17},{2,10},{10... | collective-permute-start | bytes 393224 | tf_op jit(solution)/shard_map/ppermute | solution.py:350
  9.4 0.0 copy-done
  9.4 0.0 copy-done.1
  9.5 0.8 %inner_cells.1._ = f32[4,32,8,256]{3,2,1,0:T(8,128)S(1)} custom-call(f32[1,1]{1,0:T(1,128)} %bitcast.12.strength_ref, s32[1,2]{1,0:T(1,128)S(4)} %get-tuple-element.32.source_ref, s32[2,128]{1,0:T(2,128)S(1)} %get-tuple-element.33.receiver_ref, f32[1,128]{1,0:T(1,128)S(1)} %get-tuple-element.34.trace_ref, ...), custom_call_target="tpu_custom_call" | custom-call | bytes 60000000 | tf_op jit(solution)/shard_map/inner_cells/pallas_call | solution.py:416
  10.2 0.2 collective-permute-done.1.x_even_ref
  10.4 0.0 collective-permute-done.2.x_odd_ref
  10.5 0.0 collective-permute-done.5.slab_ref
  10.5 0.2 rows_to_send.5
  10.6 2.4 %collective-permute-start.7 = (s16[144,128]{1,0:T(8,128)(2,1)S(1)}, s16[144,128]{1,0:T(8,128)(2,1)S(1)}, u32[]{:S(2)}, u32[]{:S(2)}) collective-permute-start(s16[144,128]{1,0:T(8,128)(2,1)S(1)} %get-tuple-element.55), channel_id=1, source_target_pairs={{0,24},{8,16},{16,8},{24,0},{1,25},{9,17},{17,9},{25,1},{2,26},{10... | collective-permute-start | bytes 110600 | tf_op jit(solution)/shard_map/ppermute | solution.py:350
  13.0 0.0 collective-permute-done.4.slab_ref
  13.0 0.1 rows_to_send.4
  13.1 0.6 %collective-permute-start.6 = (s16[144,128]{1,0:T(8,128)(2,1)S(1)}, s16[144,128]{1,0:T(8,128)(2,1)S(1)}, u32[]{:S(2)}, u32[]{:S(2)}) collective-permute-start(s16[144,128]{1,0:T(8,128)(2,1)S(1)} %get-tuple-element.54), channel_id=1, source_target_pairs={{0,16},{8,24},{16,0},{24,8},{1,17},{9,25},{17,1},{25,9},{2,18},{10... | collective-permute-start | bytes 110600 | tf_op jit(solution)/shard_map/ppermute | solution.py:350
  13.7 0.3 %collective-permute-done.3.slab_ref = bf16[32,8,256]{2,1,0:T(8,128)(2,1)S(1)} collective-permute-done((bf16[32,8,256]{2,1,0:T(8,128)(2,1)S(1)}, bf16[32,8,256]{2,1,0:T(8,128)(2,1)S(1)}, u32[]{:S(2)}, u32[]{:S(2)}) %collective-permute-start.3) | collective-permute-done | bytes 131104 | tf_op jit(solution)/shard_map/ppermute | solution.py:350
  14.0 0.1 rows_to_send.3
  14.1 0.6 %collective-permute-start.8 = (s16[144,128]{1,0:T(8,128)(2,1)S(1)}, s16[144,128]{1,0:T(8,128)(2,1)S(1)}, u32[]{:S(2)}, u32[]{:S(2)}) collective-permute-start(s16[144,128]{1,0:T(8,128)(2,1)S(1)} %get-tuple-element.56), channel_id=1, source_target_pairs={{0,8},{8,0},{16,24},{24,16},{1,9},{9,1},{17,25},{25,17},{2,10},{10... | collective-permute-start | bytes 110600 | tf_op jit(solution)/shard_map/ppermute | solution.py:350
  14.7 0.9 %next_fields.1 = (f32[32,8,256]{2,1,0:T(8,128)}, f32[32,8,256]{2,1,0:T(8,128)}, f32[8,8,256]{2,1,0:T(8,128)S(1)}, s32[8,128]{1,0:T(8,128)S(1)}) custom-call(s32[32]{0:T(128)S(4)} %get-tuple-element.30.rows_ref, s32[32]{0:T(128)S(4)} %get-tuple-element.31.blocks_ref, f32[4,32,8,256]{3,2,1,0:T(8,128)S(1)} %edge_cells.1.state_ref, ...), custom_call_target="tpu_custom_call" | custom-call | bytes 60000000 | tf_op jit(solution)/shard_map/next_fields/pallas_call | solution.py:469
  15.6 0.2 collective-permute-done.7.refs_1_
  15.7 1.4 %collective-permute-done.6.refs_0_ = s16[144,128]{1,0:T(8,128)(2,1)S(1)} collective-permute-done((s16[144,128]{1,0:T(8,128)(2,1)S(1)}, s16[144,128]{1,0:T(8,128)(2,1)S(1)}, u32[]{:S(2)}, u32[]{:S(2)}) %collective-permute-start.6) | collective-permute-done | bytes 36896 | tf_op jit(solution)/shard_map/ppermute | solution.py:350
  17.1 0.3 %image_of_first.1.in_ref = f32[32,8,256]{2,1,0:T(8,128)S(1)} custom-call(f32[8,8,256]{2,1,0:T(8,128)S(1)} %get-tuple-element.52.own_ref, s32[8,128]{1,0:T(8,128)S(1)} %get-tuple-element.53.own_place_ref, s16[144,128]{1,0:T(8,128)(2,1)S(1)} %collective-permute-done.6.refs_0_, s16[144,128]{1,0:T(8,128)(2,1)S(1)} %collective-permute-done.7.refs_1_), custom_call_target="tpu_custom_call" | custom-call | tf_op jit(solution)/shard_map/image_of_first/pallas_call | solution.py:481
  17.4 0.7 %collective-permute-done.8.message_ref = s16[144,128]{1,0:T(8,128)(2,1)S(1)} collective-permute-done((s16[144,128]{1,0:T(8,128)(2,1)S(1)}, s16[144,128]{1,0:T(8,128)(2,1)S(1)}, u32[]{:S(2)}, u32[]{:S(2)}) %collective-permute-start.8) | collective-permute-done | bytes 36896 | tf_op jit(solution)/shard_map/ppermute | solution.py:350
  18.2 0.9 %image_rows.1 = f32[32,8,256]{2,1,0:T(8,128)} custom-call(f32[32,8,256]{2,1,0:T(8,128)S(1)} %image_of_first.1.in_ref, s16[144,128]{1,0:T(8,128)(2,1)S(1)} %collective-permute-done.8.message_ref), custom_call_target="tpu_custom_call" | custom-call | tf_op jit(solution)/shard_map/image_rows/pallas_call | solution.py:490
  (3 shorter events, 0.1 us)
Async XLA Ops:
  0.6 9.8 %collective-permute-start.5 = (bf16[32,8,256]{2,1,0:T(8,128)(2,1)}, bf16[32,8,256]{2,1,0:T(8,128)(2,1)S(1)}, u32[]{:S(2)}, u32[]{:S(2)}) collective-permute-start(bf16[32,8,256]{2,1,0:T(8,128)(2,1)} %bitcast.18), channel_id=1, source_target_pairs={{0,24},{8,16},{16,8},{24,0},{1,25},{9,17},{17,9},{25,1},{2,26},{10... | collective-permute-start | bytes 393224 | tf_op jit(solution)/shard_map/ppermute | solution.py:350
  4.6 8.4 %collective-permute-start.4 = (bf16[32,8,256]{2,1,0:T(8,128)(2,1)}, bf16[32,8,256]{2,1,0:T(8,128)(2,1)S(1)}, u32[]{:S(2)}, u32[]{:S(2)}) collective-permute-start(bf16[32,8,256]{2,1,0:T(8,128)(2,1)} %bitcast.19), channel_id=1, source_target_pairs={{0,16},{8,24},{16,0},{24,8},{1,17},{9,25},{17,1},{25,9},{2,18},{10... | collective-permute-start | bytes 393224 | tf_op jit(solution)/shard_map/ppermute | solution.py:350
  6.3 1.8 %collective-permute-start = (bf16[2,16,8,256]{3,2,1,0:T(8,128)(2,1)S(1)}, bf16[2,16,8,256]{3,2,1,0:T(8,128)(2,1)S(1)}, u32[]{:S(2)}, u32[]{:S(2)}) collective-permute-start(bf16[2,16,8,256]{3,2,1,0:T(8,128)(2,1)S(1)} %get-tuple-element.40), channel_id=1, source_target_pairs={{0,1},{1,0},{2,3},{3,2},{4,5},{5,4},{6,7},{7,6},{8,9},{9,8},{10,11... | collective-permute-start | bytes 393224 | tf_op jit(solution)/shard_map/ppermute | solution.py:393
  6.4 3.1 %copy-start = (f32[1,32,8,256]{3,2,1,0:T(8,128)S(1)}, f32[1,32,8,256]{3,2,1,0:T(8,128)}, u32[]{:S(2)}) copy-start(f32[1,32,8,256]{3,2,1,0:T(8,128)} %param.10) | copy-start | bytes 786436
  6.4 3.1 %copy-start.1 = (f32[1,32,8,256]{3,2,1,0:T(8,128)S(1)}, f32[1,32,8,256]{3,2,1,0:T(8,128)}, u32[]{:S(2)}) copy-start(f32[1,32,8,256]{3,2,1,0:T(8,128)} %param.12) | copy-start | bytes 786436
  6.4 1.8 %copy-start.2 = (bf16[1,32,8,256]{3,2,1,0:T(8,128)(2,1)S(1)}, bf16[1,32,8,256]{3,2,1,0:T(8,128)(2,1)}, u32[]{:S(2)}) copy-start(bf16[1,32,8,256]{3,2,1,0:T(8,128)(2,1)} %param.14) | copy-start | bytes 393220
  6.4 4.0 %collective-permute-start.1 = (bf16[2,4,8,256]{3,2,1,0:T(8,128)(2,1)S(1)}, bf16[2,4,8,256]{3,2,1,0:T(8,128)(2,1)S(1)}, u32[]{:S(2)}, u32[]{:S(2)}) collective-permute-start(bf16[2,4,8,256]{3,2,1,0:T(8,128)(2,1)S(1)} %get-tuple-element.41), channel_id=1, source_target_pairs={{0,2},{2,0},{1,3},{3,1},{4,6},{6,4},{5,7},{7,5},{8,10},{10,8},{9,1... | collective-permute-start | bytes 98312 | tf_op jit(solution)/shard_map/ppermute | solution.py:414
  8.1 2.3 %collective-permute-start.2 = (bf16[2,4,8,256]{3,2,1,0:T(8,128)(2,1)S(1)}, bf16[2,4,8,256]{3,2,1,0:T(8,128)(2,1)S(1)}, u32[]{:S(2)}, u32[]{:S(2)}) collective-permute-start(bf16[2,4,8,256]{3,2,1,0:T(8,128)(2,1)S(1)} %odd_face_after_y.1), channel_id=1, source_target_pairs={{2,4},{4,2},{3,5},{5,3},{0,1},{1,0},{6,7},{7,6},{10,12},{12,10},{1... | collective-permute-start | bytes 98312 | tf_op jit(solution)/shard_map/ppermute | solution.py:413
  8.2 5.7 %collective-permute-start.3 = (bf16[32,8,256]{2,1,0:T(8,128)(2,1)S(1)}, bf16[32,8,256]{2,1,0:T(8,128)(2,1)S(1)}, u32[]{:S(2)}, u32[]{:S(2)}) collective-permute-start(bf16[32,8,256]{2,1,0:T(8,128)(2,1)S(1)} %bitcast.21), channel_id=1, source_target_pairs={{0,8},{8,0},{16,24},{24,16},{1,9},{9,1},{17,25},{25,17},{2,10},{10... | collective-permute-start | bytes 393224 | tf_op jit(solution)/shard_map/ppermute | solution.py:350
  10.6 5.1 %collective-permute-start.7 = (s16[144,128]{1,0:T(8,128)(2,1)S(1)}, s16[144,128]{1,0:T(8,128)(2,1)S(1)}, u32[]{:S(2)}, u32[]{:S(2)}) collective-permute-start(s16[144,128]{1,0:T(8,128)(2,1)S(1)} %get-tuple-element.55), channel_id=1, source_target_pairs={{0,24},{8,16},{16,8},{24,0},{1,25},{9,17},{17,9},{25,1},{2,26},{10... | collective-permute-start | bytes 110600 | tf_op jit(solution)/shard_map/ppermute | solution.py:350
  13.1 4.0 %collective-permute-start.6 = (s16[144,128]{1,0:T(8,128)(2,1)S(1)}, s16[144,128]{1,0:T(8,128)(2,1)S(1)}, u32[]{:S(2)}, u32[]{:S(2)}) collective-permute-start(s16[144,128]{1,0:T(8,128)(2,1)S(1)} %get-tuple-element.54), channel_id=1, source_target_pairs={{0,16},{8,24},{16,0},{24,8},{1,17},{9,25},{17,1},{25,9},{2,18},{10... | collective-permute-start | bytes 110600 | tf_op jit(solution)/shard_map/ppermute | solution.py:350
  14.1 4.0 %collective-permute-start.8 = (s16[144,128]{1,0:T(8,128)(2,1)S(1)}, s16[144,128]{1,0:T(8,128)(2,1)S(1)}, u32[]{:S(2)}, u32[]{:S(2)}) collective-permute-start(s16[144,128]{1,0:T(8,128)(2,1)S(1)} %get-tuple-element.56), channel_id=1, source_target_pairs={{0,8},{8,0},{16,24},{24,16},{1,9},{9,1},{17,25},{25,17},{2,10},{10... | collective-permute-start | bytes 110600 | tf_op jit(solution)/shard_map/ppermute | solution.py:350
